TPU v7x, 512 devices: a whole 4x8x8 slice. The times are simulated.
512 devices in a mesh: dp: 16 (over z, x_hi), seq: 32 (over x_lo, y, core).
Axes of the slice: x: 4 (x_hi: 2, x_lo: 2; x = x_hi * 2 + x_lo), y: 8, z: 8, core: 2. Of those that a mesh axis runs over, the one named last changes fastest.
Arguments:
- queries: bfloat16 [65536, 1792], P(('dp', 'seq')), may hold values from -64 to 64
- keys: bfloat16 [65536, 256], P(('dp', 'seq')), may hold values from -3 to 3
- values: bfloat16 [65536, 256], P(('dp', 'seq')), may hold values from -6 to 6
- bias_query: bfloat16 [1792], replicated, may hold values from -3 to 3
- bias_value: bfloat16 [256], replicated, may hold values from -3 to 3
- doc_lengths: int32 [16, 16], P('dp'), may hold values from 1 to 3072, 4096 in all within a row
- grad_out: bfloat16 [65536, 1792], P(('dp', 'seq')), may hold values from -24 to 24
Outputs:
- attended: bfloat16 [65536, 1792], P(('dp', 'seq'))
- grad_queries: bfloat16 [65536, 1792], P(('dp', 'seq'))
- grad_keys: bfloat16 [65536, 256], P(('dp', 'seq'))
- grad_values: bfloat16 [65536, 256], P(('dp', 'seq'))
- grad_bias_query: float32 [1792], replicated
- grad_bias_value: float32 [256], replicated
Inputs may be any that keep to these rules, and one draw needn't show every extreme that they name: `doc_lengths`: the 16 lengths of each pack add up to 4096, and the longest is 3072.
All inputs are finite; a program needn't handle non-finite values.
Results may differ from a plain program's by a relative error of at most 0.023.
Values may be sent and summed in bfloat16 or wider, within the bound.
No kernel may reach another device: no remote copies, remote signals or barrier semaphores. Data moves between devices by JAX's collectives and lax.ppermute only.
A program may use at most 64 MiB of HBM per device.

v0:
```python
import math

import jax
import jax.numpy as jnp
from jax import lax
from jax.sharding import PartitionSpec as P

HEADS = 14
KV_HEADS = 2
HEAD_DIM = 128


NEGATIVE = -1e30


def doc_starts(doc_lengths, token_index):
    lengths_row = doc_lengths.reshape(-1)
    ends = jnp.cumsum(lengths_row)
    begins = ends - lengths_row
    below = begins[None, :] <= token_index[:, None]
    return jnp.max(jnp.where(below, begins[None, :], 0), axis=1)


def body(queries, keys, values, bias_query, bias_value, doc_lengths, grad_out):
    row_count = queries.shape[0]
    group_q = HEADS // KV_HEADS
    scale = 1.0 / math.sqrt(HEAD_DIM)
    shard_index = lax.axis_index("seq")
    pack_tokens = row_count * lax.axis_size("seq")
    token_index = shard_index * row_count + jnp.arange(row_count, dtype=jnp.int32)
    first_seen = doc_starts(doc_lengths, token_index)
    lowest = first_seen[0]
    highest = token_index[row_count - 1]
    query_rows = (queries.astype(jnp.float32) + bias_query.astype(jnp.float32)[None, :]).astype(
        jnp.bfloat16
    )
    query_rows = query_rows.reshape(row_count, KV_HEADS, group_q, HEAD_DIM)
    value_rows = (values.astype(jnp.float32) + bias_value.astype(jnp.float32)[None, :]).astype(
        jnp.bfloat16
    )
    grad_rows = grad_out.reshape(row_count, KV_HEADS, group_q, HEAD_DIM)

    def allowed_of(start, count):
        key_index = start + jnp.arange(count, dtype=jnp.int32)
        return jnp.logical_and(
            key_index[None, :] <= token_index[:, None], key_index[None, :] >= first_seen[:, None]
        )

    def scores_of(key_piece, start):
        count = key_piece.shape[0]
        key_heads = key_piece.reshape(count, KV_HEADS, HEAD_DIM)
        raw = (
            jnp.einsum("tkgd,skd->kgts", query_rows, key_heads, preferred_element_type=jnp.float32)
            * scale
        )
        return (raw, allowed_of(start, count), key_heads)

    def blocked(step, carry, pieces):
        count = pieces[0].shape[0]
        width = math.gcd(count, 512)

        def turn(index, state):
            offset = index * width
            parts = tuple((lax.dynamic_slice_in_dim(member, offset, width, 0) for member in pieces))
            seen = jnp.logical_and(offset + width > lowest, offset <= highest)
            return lax.cond(
                seen, lambda inner: step(inner, parts, offset), lambda inner: inner, state
            )

        return lax.fori_loop(0, count // width, turn, carry)

    def scan_step(state, parts, first):
        best, totals = state
        raw, allowed, unused_heads = scores_of(parts[0], first)
        masked = jnp.where(allowed[None, None], raw, NEGATIVE)
        newest = jnp.maximum(best, jnp.max(masked, axis=-1))
        weights = jnp.where(allowed[None, None], jnp.exp(masked - newest[..., None]), 0.0)
        return (newest, totals * jnp.exp(best - newest) + jnp.sum(weights, axis=-1))

    def value_step_of(log_total):

        def value_step(state, parts, first):
            raw, allowed, unused_heads = scores_of(parts[0], first)
            count = parts[1].shape[0]
            value_heads = parts[1].reshape(count, KV_HEADS, HEAD_DIM)
            rounded = jnp.where(
                allowed[None, None], jnp.exp(raw - log_total[..., None]), 0.0
            ).astype(jnp.bfloat16)
            return state + jnp.einsum(
                "kgts,skd->tkgd", rounded, value_heads, preferred_element_type=jnp.float32
            )

        return value_step

    def grad_step_of(log_total, delta, base):

        def grad_step(state, parts, first):
            query_acc, key_acc, value_acc = state
            raw, allowed, key_heads = scores_of(parts[0], first)
            count = parts[0].shape[0]
            value_heads = parts[1].reshape(count, KV_HEADS, HEAD_DIM)
            probs = jnp.where(allowed[None, None], jnp.exp(raw - log_total[..., None]), 0.0)
            rounded = probs.astype(jnp.bfloat16)
            dots = jnp.einsum(
                "tkgd,skd->kgts", grad_rows, value_heads, preferred_element_type=jnp.float32
            )
            slopes = (probs * (dots - delta[..., None])).astype(jnp.bfloat16)
            query_acc = query_acc + jnp.einsum(
                "kgts,skd->tkgd", slopes, key_heads, preferred_element_type=jnp.float32
            )
            key_part = jnp.einsum(
                "kgts,tkgd->skd", slopes, query_rows, preferred_element_type=jnp.float32
            ).reshape(count, -1)
            value_part = jnp.einsum(
                "kgts,tkgd->skd", rounded, grad_rows, preferred_element_type=jnp.float32
            ).reshape(count, -1)
            place = first - base
            key_acc = lax.dynamic_update_slice_in_dim(
                key_acc, lax.dynamic_slice_in_dim(key_acc, place, count, 0) + key_part, place, 0
            )
            value_acc = lax.dynamic_update_slice_in_dim(
                value_acc,
                lax.dynamic_slice_in_dim(value_acc, place, count, 0) + value_part,
                place,
                0,
            )
            return (query_acc, key_acc, value_acc)

        return grad_step

    scan_init = (
        jnp.full((KV_HEADS, group_q, row_count), NEGATIVE, jnp.float32),
        jnp.zeros((KV_HEADS, group_q, row_count), jnp.float32),
    )
    value_init = jnp.zeros((row_count, KV_HEADS, group_q, HEAD_DIM), jnp.float32)
    best, totals = blocked(scan_step, scan_init, (lax.all_gather(keys, "seq", axis=0, tiled=True),))
    log_total = best + jnp.log(totals)
    value_step = value_step_of(log_total)
    out_sum = blocked(
        value_step,
        value_init,
        (
            lax.all_gather(keys, "seq", axis=0, tiled=True),
            lax.all_gather(value_rows, "seq", axis=0, tiled=True),
        ),
    )
    attended = out_sum.astype(jnp.bfloat16)
    delta = jnp.sum(
        grad_rows.astype(jnp.float32) * attended.astype(jnp.float32), axis=-1
    ).transpose(1, 2, 0)
    grad_step = grad_step_of(log_total, delta, 0)
    grad_init = (
        jnp.zeros((row_count, KV_HEADS, group_q, HEAD_DIM), jnp.float32),
        jnp.zeros((pack_tokens, KV_HEADS * HEAD_DIM), jnp.float32),
        jnp.zeros((pack_tokens, KV_HEADS * HEAD_DIM), jnp.float32),
    )
    query_acc, key_acc, value_acc = blocked(
        grad_step,
        grad_init,
        (
            lax.all_gather(keys, "seq", axis=0, tiled=True),
            lax.all_gather(value_rows, "seq", axis=0, tiled=True),
        ),
    )
    key_sum, value_sum = (
        lax.psum_scatter(
            (key_acc * scale).astype(jnp.bfloat16), "seq", scatter_dimension=0, tiled=True
        ).astype(jnp.float32),
        lax.psum_scatter(
            value_acc.astype(jnp.bfloat16), "seq", scatter_dimension=0, tiled=True
        ).astype(jnp.float32),
    )
    query_grad = (query_acc * scale).reshape(row_count, HEADS * HEAD_DIM)
    bias_q_grad, bias_v_grad = lax.psum(
        (jnp.sum(query_grad, axis=0), jnp.sum(value_sum, axis=0)), ("dp", "seq")
    )
    return (
        attended.reshape(row_count, HEADS * HEAD_DIM),
        query_grad.astype(jnp.bfloat16),
        key_sum.astype(jnp.bfloat16),
        value_sum.astype(jnp.bfloat16),
        bias_q_grad,
        bias_v_grad,
    )


def solution(mesh):
    in_specs = (
        P(("dp", "seq"), None),
        P(("dp", "seq"), None),
        P(("dp", "seq"), None),
        P(),
        P(),
        P("dp", None),
        P(("dp", "seq"), None),
    )
    out_specs = (
        P(("dp", "seq"), None),
        P(("dp", "seq"), None),
        P(("dp", "seq"), None),
        P(("dp", "seq"), None),
        P(),
        P(),
    )
    return jax.shard_map(body, mesh=mesh, in_specs=in_specs, out_specs=out_specs, check_vma=False)
```

profile of v0, /device:TPU:1, one launch (start us, length us, event | category | flops | bytes accessed | tf_op | source)
XLA Modules:
  0.0 503.9 jit_solution(2658353248780875170)
XLA Ops:
  7.2 0.0 copy-start
  7.2 0.0 all-gather.3.cloned.1.call-start
  7.2 1.6 copy.86
  8.8 0.0 all-gather.3.cloned.1.call-update
  8.8 0.0 all-gather.5.cloned.1.call-start
  8.9 0.7 convert_element_type.88
  9.5 0.9 copy.89
  10.5 0.7 add_convert_fusion.1
  11.2 0.0 all-gather.5.cloned.1.call-update
  11.2 0.0 reduce-scatter.5.cloned.1.call-start
  11.3 0.6 slice.7
  11.9 0.8 reduce-window_clone.1
  12.8 0.7 convert_element_type.85
  13.5 1.1 add_convert_fusion
  14.5 0.3 copy.87
  14.8 0.3 copy.90
  15.1 1.3 copy.92
  16.4 0.0 copy-done
  16.4 0.1 select_reduce_fusion.1
  16.5 68.4 %all-gather.3.cloned.1.call-done = bf16[4096,256]{0,1:T(8,128)(2,1)} async-done(((bf16[128,256]{0,1:T(8,128)(2,1)}), bf16[4096,256]{0,1:T(8,128)(2,1)}) %all-gather.3.cloned.1.call-update) | async-done | bytes 2097168 | tf_op jit(solution)/shard_map/all_gather | solution.py:143
  84.9 8.4 %while.51 = (s32[]{:T(128)}, f32[2,7,128]{2,1,0:T(8,128)S(1)}, f32[2,7,128]{2,1,0:T(8,128)S(1)}, s32[]{:T(128)S(1)}, s32[]{:T(128)}, /*index=5*/s32[128]{0:T(128...) while((s32[]{:T(128)}, f32[2,7,128]{2,1,0:T(8,128)S(1)}, ...), condition=%wide.region_7.8_spmd.clone, body=%wide.region_2.7_spmd.clone.sunk | while | flops 242421888 | bytes 8881973 | solution.py:70
  85.6 2.9 conditional.9
  85.6 0.1 compare_and_fusion
  85.7 1.0 constant_dynamic-slice_fusion
  86.7 0.8 fusion.6
  87.5 0.9 select_reduce_fusion
  93.3 61.3 %all-gather.5.cloned.1.call-done = bf16[4096,256]{0,1:T(8,128)(2,1)} async-done(((bf16[128,256]{0,1:T(8,128)(2,1)}), bf16[4096,256]{0,1:T(8,128)(2,1)}) %all-gather.5.cloned.1.call-update) | async-done | bytes 2097168 | tf_op jit(solution)/shard_map/all_gather | solution.py:144
  154.6 0.1 broadcast.193.clone
  154.7 8.6 %while.52 = (s32[]{:T(128)}, f32[128,2,7,128]{3,0,2,1:T(8,128)S(1)}, s32[]{:T(128)S(1)}, s32[]{:T(128)}, s32[128]{0:T(128)S(1)}, /*index=5*/bf16[4096,256]{0,1:T...) while((s32[]{:T(128)}, ...), condition=%wide.region_11.12_spmd.clone, body=%wide.region_8.11_spmd.clone.sunk | while | flops 473858688 | bytes 4011813 | solution.py:70
  155.3 3.1 conditional.10
  155.4 0.1 compare_and_fusion.1
  155.5 1.1 constant_dynamic-slice_fusion.1
  156.6 1.8 fusion.12
  163.3 0.3 copy.91
  163.6 0.1 multiply_reduce_fusion
  163.7 0.1 broadcast.193
  163.8 2.5 broadcast.194.clone
  166.2 2.4 broadcast.194
  168.7 14.8 %while.53 = (s32[]{:T(128)}, f32[128,2,7,128]{3,0,2,1:T(8,128)S(1)}, f32[4096,256]{0,1:T(8,128)}, f32[4096,256]{0,1:T(8,128)}, s32[]{:T(128)S(1)}, /*index=5*/s3...) while((s32[]{:T(128)}, ...), condition=%wide.region_16.17_spmd.clone, body=%wide.region_13.16_spmd.clone.sunk | while | flops 1184268928 | bytes 26439580 | solution.py:70
  169.3 9.2 %conditional.11 = ((f32[128,2,7,128]{3,0,2,1:T(8,128)S(1)}, f32[4096,256]{0,1:T(8,128)}, f32[4096,256]{0,1:T(8,128)})) conditional(s32[]{:T(128)} %convert_element_type.125, (f32[128,2,7,128]{3,0,2,1:T(8,128)S(1)}, f32[4096,256]{0,1:T(8,128)}, f32[4096,256]{0,1:T(8,128)}) %tuple.163, (s32[]{:T(128)}, s32[]{:T(128)}, s32[128]{0:T(128)S(1)}, ...), branch_computations={%region_14.14_spmd, %region_15.15_spmd} | conditional | flops 1184268928 | bytes 26438742 | solution.py:66
  169.4 0.1 compare_and_fusion.2
  169.5 1.0 constant_dynamic-slice_fusion.4
  170.5 1.0 constant_dynamic-slice_fusion.3
  171.5 0.7 fusion.26
  172.2 0.9 fusion.20
  173.0 1.3 fusion.16
  174.3 0.7 fusion.27
  175.1 1.1 fusion.23
  176.2 2.4 constant_dynamic-update-slice_fusion
  183.4 4.6 copy.95
  188.1 0.0 reduce-scatter.5.cloned.1.call-update
  188.1 0.2 reduce-scatter.3.cloned.1.call-start
  188.3 5.6 %copy.94 = f32[4096,256]{1,0:T(8,128)} copy(f32[4096,256]{0,1:T(8,128)} %get-tuple-element.901) | data formatting | bytes 8388608 | tf_op jit(solution)/shard_map/while | solution.py:70
  194.0 4.0 multiply_convert_fusion
  197.9 0.0 reduce-scatter.3.cloned.1.call-update
  198.0 1.0 copy.96
  198.9 0.3 copy.93
  199.3 0.3 multiply_reduce_fusion.1
  199.6 1.0 copy.97
  200.6 176.3 %reduce-scatter.5.cloned.1.call-done = bf16[128,256]{1,0:T(8,128)(2,1)} async-done(((bf16[4096,256]{1,0:T(8,128)(2,1)}), bf16[128,256]{1,0:T(8,128)(2,1)}) %reduce-scatter.5.cloned.1.call-update) | async-done | bytes 65552 | tf_op jit(solution)/shard_map/reduce_scatter | solution.py:169
  376.9 0.9 convert_reduce_fusion
  377.7 101.0 %all-reduce = (f32[1792]{0:T(1024)}, f32[256]{0:T(256)}) all-reduce(f32[1792]{0:T(1024)S(1)} %reduce_sum.42, f32[256]{0:T(256)S(1)} %convert_reduce_fusion), channel_id=1, replica_groups=mesh['dp'=16,'seq'=32] {'dp','seq'}, use_global_device_ids=true, to_apply=%region_20.21 | all-reduce | flops 2048 | bytes 16384 | tf_op jit(solution)/shard_map/psum | solution.py:174
  478.7 18.7 %reduce-scatter.3.cloned.1.call-done = bf16[128,256]{1,0:T(8,128)(2,1)} async-done(((bf16[4096,256]{1,0:T(8,128)(2,1)}), bf16[128,256]{1,0:T(8,128)(2,1)}) %reduce-scatter.3.cloned.1.call-update) | async-done | bytes 65552 | tf_op jit(solution)/shard_map/reduce_scatter | solution.py:166
  (60 shorter events, 0.4 us)
Async XLA Ops:
  7.2 9.2 %copy-start = (s32[1,16]{1,0:T(1,128)S(1)}, s32[1,16]{1,0:T(1,128)}, u32[]{:S(2)}) copy-start(s32[1,16]{1,0:T(1,128)} %param.24) | copy-start | bytes 196
  7.2 77.7 %all-gather.3.cloned.1.call-start = ((), (), s32[]{:S(2)}) async-start(), calls=%async_computation.2 | async-start | bytes 2162688 | tf_op jit(solution)/shard_map/all_gather | solution.py:143
  8.8 145.8 %all-gather.5.cloned.1.call-start = ((), (), s32[]{:S(2)}) async-start(), calls=%async_computation.3 | async-start | bytes 2162688 | tf_op jit(solution)/shard_map/all_gather | solution.py:144
  11.2 365.6 %reduce-scatter.5.cloned.1.call-start = ((), (), s32[]{:S(2)}) async-start(), calls=%async_computation.5 | async-start | bytes 2162688 | tf_op jit(solution)/shard_map/reduce_scatter | solution.py:169
  188.1 309.3 %reduce-scatter.3.cloned.1.call-start = ((), (), s32[]{:S(2)}) async-start(), calls=%async_computation.4 | async-start | bytes 2162688 | tf_op jit(solution)/shard_map/reduce_scatter | solution.py:166
Sparse Core Ops, SparseCore 0:
  10.6 74.2 all-gather.2
  87.5 67.0 all-gather.4
  188.2 188.5 reduce-scatter.4
  380.3 117.0 reduce-scatter.2
where the time goes:
time: 507 us; the launch traced here: 504 us
  waiting for transfers between devices  325 us (64%)
  blocking collectives  101 us (20%)
  local copies, waits for them, and re-layouts  26.8 us (5%)
  loops' own time  16.7 us (3%)
  between operations  13.9 us (3%)
  other arithmetic  13.2 us (3%)
  matrix products  7.28 us (1%)
    reduce_scatter x1, waiting for transfers between devices, body(): lax.psum_scatter(value_acc.astype(jnp.bfloat16), 'seq', scatter_dimension...  176 us
    psum x1, blocking collectives, body(): lax.psum((jnp.sum(query_grad, axis=0), jnp.sum(value_sum, axis=0)), ('dp'...  101 us
    all_gather x1, waiting for transfers between devices, body(): lax.all_gather(keys, 'seq', axis=0, tiled=True)  68.4 us
    all_gather x1, waiting for transfers between devices, body(): lax.all_gather(value_rows, 'seq', axis=0, tiled=True)  61.3 us
    reduce_scatter x1, waiting for transfers between devices, body(): lax.psum_scatter((key_acc * scale).astype(jnp.bfloat16), 'seq', scatter_d...  18.7 us
    another operation x3, loops' own time, blocked(): return lax.fori_loop(0, count // width, turn, carry)  16.2 us
    while x4, local copies, waits for them, and re-layouts, blocked(): return lax.fori_loop(0, count // width, turn, carry)  10.8 us
  transfers between devices with their start and end apart: 4, of which 4 were waited for; matrix products, arithmetic and copies ran while one was open for 5% of the time, Pallas kernels for 0%

commit v1 on v0

v1 whole, which is shorter than its diff:
```python
import functools
import math

import jax
import jax.numpy as jnp
from jax import lax
from jax.experimental import pallas as pl
from jax.experimental.pallas import tpu as pltpu
from jax.sharding import Mesh, PartitionSpec as P

HEADS = 14
KV_HEADS = 2
HEAD_DIM = 128
GROUP = HEADS // KV_HEADS
TOK = 128
CHUNK = 256
LONGEST = 3072
SLOTS = LONGEST // CHUNK + 1
NDOC = 16
SCALE = 1.0 / math.sqrt(HEAD_DIM)
LOG2E = math.log2(math.e)
NEGATIVE = -1e30
F32 = jnp.float32
BF16 = jnp.bfloat16


def dot(a, b):
    return jnp.dot(a, b, preferred_element_type=F32)


def fold_rows(values, how):
    return how(values.reshape(values.shape[0] // 8, 8, values.shape[1]), axis=0)


def attention_kernel(
    place, lengths, q_own, g_own, q_other, g_other, bias, kv,
    att_own, att_send, gq_own, gq_send, dkv, bias_out,
    q_s, qt_s, g_s, gt_s, s_s, mx_s, l_s, ot_s, dqt_s, rl_s, delta_s, mask_s, bv_s,
):
    core = place[0]
    chunk_id = place[1]
    first_token = chunk_id * CHUNK

    token = first_token + lax.broadcasted_iota(jnp.int32, (1, CHUNK), 1)
    first_seen = jnp.zeros((1, CHUNK), jnp.int32)
    begin = jnp.int32(0)
    lowest = jnp.int32(0)
    for i in range(NDOC):
        first_seen = jnp.where(token >= begin, begin, first_seen)
        lowest = jnp.where(first_token >= begin, begin, lowest)
        begin = begin + lengths[0, i]
    low = lax.div(lowest, jnp.int32(CHUNK))

    own_at = pl.multiple_of(core * TOK, TOK)
    other_at = pl.multiple_of((1 - core) * TOK, TOK)
    for h in range(GROUP):
        cols = pl.ds(h * HEAD_DIM, HEAD_DIM)
        own_cols = pl.ds(pl.multiple_of((core * GROUP + h) * HEAD_DIM, HEAD_DIM), HEAD_DIM)
        bias_row = bias[:, own_cols].astype(F32)
        q_s[h, pl.ds(own_at, TOK), :] = (q_own[:, own_cols].astype(F32) + bias_row).astype(BF16)
        q_s[h, pl.ds(other_at, TOK), :] = (q_other[:, cols].astype(F32) + bias_row).astype(BF16)
        g_s[h, pl.ds(own_at, TOK), :] = g_own[:, own_cols]
        g_s[h, pl.ds(other_at, TOK), :] = g_other[:, cols]
    for h in range(GROUP):
        qt_s[h] = q_s[h].T
        gt_s[h] = g_s[h].T
    mx_s[...] = jnp.full(mx_s.shape, NEGATIVE, F32)
    l_s[...] = jnp.zeros(l_s.shape, F32)
    ot_s[...] = jnp.zeros(ot_s.shape, F32)
    dqt_s[...] = jnp.zeros(dqt_s.shape, F32)
    bv_s[...] = jnp.zeros(bv_s.shape, F32)
    dkv[...] = jnp.zeros(dkv.shape, BF16)

    def where_of(c):
        return lax.rem(c, 8), lax.div(c, 8)

    def scores(c, carry):
        y, x = where_of(c)
        keys = kv[y, x, :, :HEAD_DIM]
        key_index = c * CHUNK + lax.broadcasted_iota(jnp.int32, (CHUNK, CHUNK), 0)
        allowed = jnp.logical_and(key_index <= token, key_index >= first_seen)
        mask_s[...] = jnp.where(allowed, 0.0, NEGATIVE)
        for h in range(GROUP):
            raw = dot(keys, qt_s[h]) * (SCALE * LOG2E) + mask_s[...]
            s_s[c - low, h] = raw
            mx_s[h] = jnp.maximum(mx_s[h], fold_rows(raw, jnp.max))
        return carry

    lax.fori_loop(low, chunk_id + 1, scores, 0)
    for h in range(GROUP):
        mx_s[h] = jnp.broadcast_to(jnp.max(mx_s[h], axis=0, keepdims=True), (8, CHUNK))

    def weigh(c, carry):
        y, x = where_of(c)
        values_t = kv[y, x, :, HEAD_DIM:].T
        for h in range(GROUP):
            probs = jnp.exp2(s_s[c - low, h] - mx_s[h, 0:1, :])
            s_s[c - low, h] = probs
            l_s[h] = l_s[h] + fold_rows(probs, jnp.sum)
            ot_s[h] = ot_s[h] + dot(values_t, probs.astype(BF16))
        return carry

    lax.fori_loop(low, chunk_id + 1, weigh, 0)

    for h in range(GROUP):
        cols = pl.ds(h * HEAD_DIM, HEAD_DIM)
        inverse = 1.0 / jnp.sum(l_s[h], axis=0, keepdims=True)
        rl_s[h] = jnp.broadcast_to(inverse, (8, CHUNK))
        out_t = (ot_s[h] * inverse).astype(BF16).astype(F32)
        delta = jnp.sum(out_t * gt_s[h].astype(F32), axis=0, keepdims=True)
        delta_s[h] = jnp.broadcast_to(delta, (8, CHUNK))
        ot_s[h] = out_t
        mx_s[h, :, :] = jnp.zeros((8, CHUNK), F32)
        out = out_t.T.astype(BF16)
        g_s_rows = out.reshape(2, TOK, HEAD_DIM)
        att_own[:, cols] = jnp.where(core == 0, g_s_rows[0], g_s_rows[1])
        att_send[:, cols] = jnp.where(core == 0, g_s_rows[1], g_s_rows[0])

    def slopes_of(c, carry):
        y, x = where_of(c)
        keys_t = kv[y, x, :, :HEAD_DIM].T
        values = kv[y, x, :, HEAD_DIM:]
        dk = jnp.zeros((CHUNK, HEAD_DIM), F32)
        dv = jnp.zeros((CHUNK, HEAD_DIM), F32)
        for h in range(GROUP):
            dots = dot(values, gt_s[h])
            probs = s_s[c - low, h] * rl_s[h, 0:1, :]
            slopes = (probs * (dots - delta_s[h, 0:1, :])).astype(BF16)
            dk = dk + dot(slopes, q_s[h])
            dv = dv + dot(probs.astype(BF16), g_s[h])
            dqt_s[h] = dqt_s[h] + dot(keys_t, slopes)
        dkv[y, x, :, :HEAD_DIM] = (dk * SCALE).astype(BF16)
        dkv[y, x, :, HEAD_DIM:] = dv.astype(BF16)
        bv_s[...] = bv_s[...] + fold_rows(dv, jnp.sum)
        return carry

    lax.fori_loop(low, chunk_id + 1, slopes_of, 0)

    for h in range(GROUP):
        cols = pl.ds(h * HEAD_DIM, HEAD_DIM)
        grad = (dqt_s[h] * SCALE).T
        bias_out[h : h + 1, :] = jnp.sum(grad, axis=0, keepdims=True)
        rows = grad.astype(BF16).reshape(2, TOK, HEAD_DIM)
        gq_own[:, cols] = jnp.where(core == 0, rows[0], rows[1])
        gq_send[:, cols] = jnp.where(core == 0, rows[1], rows[0])
    bias_out[GROUP : GROUP + 1, :] = jnp.sum(bv_s[...], axis=0, keepdims=True)


def attention(place, lengths, q_own, g_own, q_other, g_other, bias, kv):
    half = jax.ShapeDtypeStruct((TOK, GROUP * HEAD_DIM), BF16)
    vmem = pl.BlockSpec(memory_space=pltpu.VMEM)
    smem = pl.BlockSpec(memory_space=pltpu.SMEM)
    head = (GROUP, CHUNK, HEAD_DIM)
    head_t = (GROUP, HEAD_DIM, CHUNK)
    stat = (GROUP, 8, CHUNK)
    pairs = CHUNK * SLOTS * CHUNK * GROUP
    return pl.pallas_call(
        attention_kernel,
        out_shape=[half] * 4
        + [
            jax.ShapeDtypeStruct(kv.shape, BF16),
            jax.ShapeDtypeStruct((8, HEAD_DIM), F32),
        ],
        in_specs=[smem] * 2 + [vmem] * 6,
        out_specs=[vmem] * 6,
        scratch_shapes=[
            pltpu.VMEM(head, BF16),
            pltpu.VMEM(head_t, BF16),
            pltpu.VMEM(head, BF16),
            pltpu.VMEM(head_t, BF16),
            pltpu.VMEM((SLOTS, GROUP, CHUNK, CHUNK), F32),
            pltpu.VMEM(stat, F32),
            pltpu.VMEM(stat, F32),
            pltpu.VMEM(head_t, F32),
            pltpu.VMEM(head_t, F32),
            pltpu.VMEM(stat, F32),
            pltpu.VMEM(stat, F32),
            pltpu.VMEM((CHUNK, CHUNK), F32),
            pltpu.VMEM((8, HEAD_DIM), F32),
        ],
        compiler_params=pltpu.CompilerParams(vmem_limit_bytes=58 * 1024 * 1024),
        cost_estimate=pl.CostEstimate(
            flops=12 * pairs * HEAD_DIM, bytes_accessed=8 << 20, transcendentals=pairs
        ),
    )(place, lengths, q_own, g_own, q_other, g_other, bias, kv)


SEQ = ("xlo", "y", "core")
SWAP = [(0, 1), (1, 0)]


def everyone(part, axes, count):
    spread = jnp.broadcast_to(part[None], (count,) + part.shape)
    return lax.all_to_all(spread, axes, split_axis=0, concat_axis=0, tiled=True)


def body(queries, keys, values, bias_query, bias_value, doc_lengths, grad_out):
    x = lax.axis_index("xlo")
    y = lax.axis_index("y")
    core = lax.axis_index("core")
    width = GROUP * HEAD_DIM

    def by_core(mine, other):
        return jnp.concatenate(
            [jnp.where(core == 0, mine, other), jnp.where(core == 0, other, mine)], axis=0
        )

    def columns(array, which, size):
        return jnp.where(which == 0, array[:, :size], array[:, size:])

    value_rows = (values.astype(F32) + bias_value.astype(F32)[None, :]).astype(BF16)

    def kv_head(which):
        return jnp.concatenate(
            [columns(keys, which, HEAD_DIM), columns(value_rows, which, HEAD_DIM)], axis=1
        )

    kv_other = lax.ppermute(kv_head(1 - core), "core", SWAP)
    chip_kv = by_core(kv_head(core), kv_other)
    from_low = lax.ppermute(chip_kv, "xlo", [(0, 1)])
    two = jnp.stack([jnp.where(x == 0, chip_kv, from_low), chip_kv])
    gathered = lax.all_gather(two, "y", axis=0, tiled=False)

    q_other = lax.ppermute(columns(queries, 1 - core, width), "core", SWAP)
    g_other = lax.ppermute(columns(grad_out, 1 - core, width), "core", SWAP)
    place = jnp.stack([core, x * 8 + y]).astype(jnp.int32)
    att_own, att_send, gq_own, gq_send, dkv, bias_part = attention(
        place, doc_lengths, queries, grad_out, q_other, g_other, bias_query[None, :], gathered
    )

    reduced = lax.psum_scatter(dkv, "y", scatter_dimension=0, tiled=False)

    att_other = lax.ppermute(att_send, "core", SWAP)
    gq_other = lax.ppermute(gq_send, "core", SWAP)

    def side_by_side(mine, other):
        return jnp.concatenate(
            [jnp.where(core == 0, mine, other), jnp.where(core == 0, other, mine)], axis=1
        )

    attended = side_by_side(att_own, att_other)
    grad_queries = side_by_side(gq_own, gq_other)

    over_packs = jnp.sum(everyone(bias_part, ("z", "xhi", "xlo"), 32), axis=0)
    over_all = jnp.sum(everyone(over_packs, ("y", "core"), 16).reshape(8, 2, 8, HEAD_DIM), axis=0)
    grad_bias_query = over_all[:, :GROUP].reshape(HEADS * HEAD_DIM)
    grad_bias_value = over_all[:, GROUP].reshape(KV_HEADS * HEAD_DIM)

    from_high = lax.ppermute(reduced[0], "xlo", [(1, 0)])
    total = jnp.where(
        x == 0, (reduced[0].astype(F32) + from_high.astype(F32)).astype(BF16), reduced[1]
    )
    mine = jnp.where(core == 0, total[:TOK], total[TOK:])
    theirs = jnp.where(core == 0, total[TOK:], total[:TOK])
    other = lax.ppermute(theirs, "core", SWAP)
    grad_keys = side_by_side(mine[:, :HEAD_DIM], other[:, :HEAD_DIM])
    grad_values = side_by_side(mine[:, HEAD_DIM:], other[:, HEAD_DIM:])
    return attended, grad_queries, grad_keys, grad_values, grad_bias_query, grad_bias_value


def solution(mesh):
    parts = Mesh(mesh.devices.reshape(8, 2, 2, 8, 2), ("z", "xhi", "xlo", "y", "core"))
    rows = P(("z", "xhi") + SEQ, None)
    in_specs = (rows, rows, rows, P(), P(), P(("z", "xhi"), None), rows)
    out_specs = (rows, rows, rows, rows, P(), P())
    return jax.shard_map(body, mesh=parts, in_specs=in_specs, out_specs=out_specs, check_vma=False)
```

time: 507 us -> 179 us (0.35)
  waiting for transfers between devices: 325 us -> 77.3 us
  blocking collectives: 101 us -> 0 us
  starting transfers between devices: 0.34 us -> 65.4 us
  local copies, waits for them, and re-layouts: 26.8 us -> 4.89 us
  loops' own time: 16.7 us -> 0 us
  Pallas kernels: 0 us -> 7.48 us
  matrix products: 7.28 us -> 0 us
  other arithmetic: 13.2 us -> 7.91 us
    reduce_scatter x2 -> x1, waiting for transfers between devices: 195 us -> 32.5 us  [body(): reduced = lax.psum_scatter(dkv, 'y', scatter_dimension=0, tiled=False)]
    psum x1 -> x0, blocking collectives: 101 us -> none  [body(): lax.psum((jnp.sum(query_grad, axis=0), jnp.sum(value_sum, axis=0)), ('dp'...]
    all_gather x2 -> x1, waiting for transfers between devices: 130 us -> 35.8 us  [body(): gathered = lax.all_gather(two, 'y', axis=0, tiled=False)]
    all_to_all x0 -> x2, starting transfers between devices: none -> 38.9 us  [everyone(): return lax.all_to_all(spread, axes, split_axis=0, concat_axis=0, tiled=True)]
    ppermute x0 -> x8, starting transfers between devices: none -> 26.5 us  [the longest x1 8.79 us: body(): kv_other = lax.ppermute(kv_head(1 - core), 'core', SWAP)]
    another operation x27 -> x0, loops' own time: 16.7 us -> none  [the longest x3 16.2 us: blocked(): return lax.fori_loop(0, count // width, turn, carry)]
    while x4 -> x0, local copies, waits for them, and re-layouts: 10.8 us -> none  [blocked(): return lax.fori_loop(0, count // width, turn, carry)]
    pallas_call x0 -> x1, Pallas kernels: none -> 7.48 us  [attention(): pl.pallas_call(attention_kernel, out_shape=[half] * 4 + [jax.ShapeDtypeSt...]
  transfers between devices with their start and end apart: 4 -> 12, of which waited for: 4 -> 7; matrix products, arithmetic and copies ran while one was open for 5% -> 4% of each run, Pallas kernels for 0% -> 0%
where the time goes in v1:
time: 179 us; the launch traced here: 177 us
  waiting for transfers between devices  77.3 us (43%)
  starting transfers between devices  65.4 us (37%)
  between operations  14.3 us (8%)
  other arithmetic  7.91 us (4%)
  Pallas kernels  7.48 us (4%)
  local copies, waits for them, and re-layouts  4.89 us (3%)
    all_to_all x2, starting transfers between devices, everyone(): return lax.all_to_all(spread, axes, split_axis=0, concat_axis=0, tiled=True)  38.9 us
    all_gather x1, waiting for transfers between devices, body(): gathered = lax.all_gather(two, 'y', axis=0, tiled=False)  35.8 us
    reduce_scatter x1, waiting for transfers between devices, body(): reduced = lax.psum_scatter(dkv, 'y', scatter_dimension=0, tiled=False)  32.5 us
    ppermute x1, starting transfers between devices, body(): kv_other = lax.ppermute(kv_head(1 - core), 'core', SWAP)  8.79 us
    pallas_call x1, Pallas kernels, attention(): pl.pallas_call(attention_kernel, out_shape=[half] * 4 + [jax.ShapeDtypeSt...  7.48 us
    ppermute x1, starting transfers between devices, body(): att_other = lax.ppermute(att_send, 'core', SWAP)  6.2 us
    all_to_all x2, waiting for transfers between devices, everyone(): return lax.all_to_all(spread, axes, split_axis=0, concat_axis=0, tiled=True)  3.93 us
  transfers between devices with their start and end apart: 12, of which 7 were waited for; matrix products, arithmetic and copies ran while one was open for 4% of the time, Pallas kernels for 0%

profile of v1, /device:TPU:1, one launch (start us, length us, event | category | flops | bytes accessed | tf_op | source)
XLA Modules:
  0.0 177.3 jit_solution(11939893489359962542)
XLA Ops:
  7.2 0.0 copy-start.1
  7.2 0.0 copy-start
  7.2 0.0 copy-start.5
  7.2 0.0 all-gather.3.cloned.1.call-start
  7.3 0.7 convert_element_type.19
  8.0 0.9 add_convert_fusion.1
  8.8 0.8 broadcast_select_fusion.14
  9.6 8.8 %collective-permute-start.2 = (bf16[128,256]{1,0:T(8,128)(2,1)S(1)}, bf16[128,256]{1,0:T(8,128)(2,1)S(1)}, u32[]{:S(2)}, u32[]{:S(2)}) collective-permute-start(bf16[128,256]{1,0:T(8,128)(2,1)S(1)} %pad_maximum_fusion.5), channel_id=1, source_target_pairs={{0,1},{1,0},{2,3},{3,2},{4,5},{5,4},{6,7},{7,6},{8,9},{9,8},{10,11... | collective-permute-start | bytes 196616 | tf_op jit(solution)/shard_map/ppermute | solution.py:218
  18.4 0.9 collective-permute-done.2
  19.4 1.3 collective-permute-start.3
  20.7 2.8 %collective-permute-done.3 = bf16[256,256]{1,0:T(8,128)(2,1)S(1)} collective-permute-done((bf16[256,256]{1,0:T(8,128)(2,1)S(1)}, bf16[256,256]{1,0:T(8,128)(2,1)S(1)}, u32[]{:S(2)}, u32[]{:S(2)}) %collective-permute-start.3) | collective-permute-done | bytes 131104 | tf_op jit(solution)/shard_map/ppermute | solution.py:220
  23.5 0.7 pad_maximum_fusion.2
  24.3 0.0 all-gather.3.cloned.1.call-update
  24.3 0.0 reduce-scatter.2.cloned.1.call-start
  24.3 0.0 copy-done.1
  24.4 2.8 %collective-permute-start.1 = (bf16[128,896]{1,0:T(8,128)(2,1)S(1)}, bf16[128,896]{1,0:T(8,128)(2,1)S(1)}, u32[]{:S(2)}, u32[]{:S(2)}) collective-permute-start(bf16[128,896]{1,0:T(8,128)(2,1)S(1)} %slice_select_fusion), channel_id=1, source_target_pairs={{0,1},{1,0},{2,3},{3,2},{4,5},{5,4},{6,7},{7,6},{8,9},{9,8},{10,11... | collective-permute-start | bytes 688136 | tf_op jit(solution)/shard_map/ppermute | solution.py:225
  27.2 0.0 copy-done
  27.2 1.9 %collective-permute-start = (bf16[128,896]{1,0:T(8,128)(2,1)S(1)}, bf16[128,896]{1,0:T(8,128)(2,1)S(1)}, u32[]{:S(2)}, u32[]{:S(2)}) collective-permute-start(bf16[128,896]{1,0:T(8,128)(2,1)S(1)} %slice_select_fusion.1), channel_id=1, source_target_pairs={{0,1},{1,0},{2,3},{3,2},{4,5},{5,4},{6,7},{7,6},{8,9},{9,8},{10,11... | collective-permute-start | bytes 688136 | tf_op jit(solution)/shard_map/ppermute | solution.py:224
  29.1 0.0 copy-done.5
  29.2 0.6 broadcast_in_dim.6.bias
  29.8 0.6 pad_add_fusion.place
  30.3 0.0 collective-permute-done.1.g_other
  30.3 0.0 copy-start.6
  30.3 0.2 collective-permute-done.q_other
  30.6 35.8 %all-gather.3.cloned.1.call-done = bf16[16,256,256]{2,1,0:T(8,128)(2,1)} async-done(((bf16[2,256,256]{2,1,0:T(8,128)(2,1)}), bf16[16,256,256]{2,1,0:T(8,128)(2,1)}) %all-gather.3.cloned.1.call-update) | async-done | bytes 2097168 | tf_op jit(solution)/shard_map/all_gather | solution.py:222
  66.4 0.0 copy-done.6
  66.4 0.0 copy-done.8
  66.4 7.5 %shard_map.118 = (bf16[128,896]{1,0:T(8,128)(2,1)}, bf16[128,896]{1,0:T(8,128)(2,1)}, bf16[128,896]{1,0:T(8,128)(2,1)}, bf16[128,896]{1,0:T(8,128)(2,1)}, bf16[8...) custom-call(s32[2]{0:T(128)} %pad_add_fusion.place, s32[1,16]{1,0:T(1,128)} %lengths.1, bf16[128,1792]{1,0:T(8,128)(2,1)} %q_own.1, ...), custom_call_target="tpu_custom_call" | custom-call | flops 9160359936 | bytes 8388608 | tf_op jit(solution)/shard_map/pallas_call | solution.py:157
  73.9 0.0 copy-start.9
  73.9 0.0 copy-start.4
  73.9 0.0 copy-start.7
  73.9 0.0 copy-start.3
  73.9 0.0 copy-start.2
  73.9 0.0 reduce-scatter.2.cloned.1.call-update
  73.9 0.9 copy-done.9
  74.8 6.2 %collective-permute-start.4 = (bf16[128,896]{1,0:T(8,128)(2,1)S(1)}, bf16[128,896]{1,0:T(8,128)(2,1)S(1)}, u32[]{:S(2)}, u32[]{:S(2)}) collective-permute-start(bf16[128,896]{1,0:T(8,128)(2,1)S(1)} %copy-done.9), channel_id=1, source_target_pairs={{0,1},{1,0},{2,3},{3,2},{4,5},{5,4},{6,7},{7,6},{8,9},{9,8},{10,11... | collective-permute-start | bytes 688136 | tf_op jit(solution)/shard_map/ppermute | solution.py:233
  81.0 0.0 copy-done.4
  81.0 0.7 broadcast_in_dim.7
  81.7 29.3 %all-to-all-start = ((f32[32,8,128]{2,1,0:T(8,128)}), f32[32,8,128]{2,1,0:T(8,128)S(1)}, u32[]{:S(2)}, u32[]{:S(2)}) async-start(f32[32,8,128]{2,1,0:T(8,128)} %broadcast_in_dim.7), calls=%async_computation.1 | async-start | bytes 262144 | tf_op jit(solution)/shard_map/all_to_all | solution.py:194
  111.0 0.0 copy-done.7
  111.0 2.2 %collective-permute-start.5 = (bf16[128,896]{1,0:T(8,128)(2,1)S(1)}, bf16[128,896]{1,0:T(8,128)(2,1)S(1)}, u32[]{:S(2)}, u32[]{:S(2)}) collective-permute-start(bf16[128,896]{1,0:T(8,128)(2,1)S(1)} %copy-done.7), channel_id=1, source_target_pairs={{0,1},{1,0},{2,3},{3,2},{4,5},{5,4},{6,7},{7,6},{8,9},{9,8},{10,11... | collective-permute-start | bytes 688136 | tf_op jit(solution)/shard_map/ppermute | solution.py:234
  113.2 0.0 collective-permute-done.4
  113.2 0.0 copy-done.3
  113.2 0.1 broadcast_select_fusion.3
  113.3 1.1 collective-permute-done.5
  114.4 0.0 copy-done.2
  114.4 0.1 broadcast_select_fusion.1
  114.4 32.5 %reduce-scatter.2.cloned.1.call-done = bf16[1,2,256,256]{3,2,1,0:T(8,128)(2,1)} async-done(((bf16[8,2,256,256]{3,2,1,0:T(8,128)(2,1)}), bf16[1,2,256,256]{3,2,1,0:T(8,128)(2,1)}) %reduce-scatter.2.cloned.1.call-update) | async-done | bytes 262160 | tf_op jit(solution)/shard_map/reduce_scatter | solution.py:231
  146.9 0.9 slice_bitcast_fusion.1
  147.8 1.3 collective-permute-start.6
  149.1 0.8 pad_maximum_fusion
  149.9 0.0 all-to-all-done
  150.0 0.6 broadcast_in_dim.8
  150.6 9.6 %all-to-all-start.1 = ((f32[16,8,128]{2,1,0:T(8,128)}), f32[16,8,128]{2,1,0:T(8,128)S(1)}, u32[]{:S(2)}, u32[]{:S(2)}) async-start(f32[16,8,128]{2,1,0:T(8,128)} %broadcast_in_dim.8), calls=%async_computation.2 | async-start | bytes 131072 | tf_op jit(solution)/shard_map/all_to_all | solution.py:194
  160.2 0.0 collective-permute-done.6
  160.2 1.0 fusion
  161.3 2.0 %collective-permute-start.7 = (bf16[128,256]{1,0:T(8,128)(2,1)S(1)}, bf16[128,256]{1,0:T(8,128)(2,1)S(1)}, u32[]{:S(2)}, u32[]{:S(2)}) collective-permute-start(bf16[128,256]{1,0:T(8,128)(2,1)S(1)} %get-tuple-element.27), channel_id=1, source_target_pairs={{0,1},{1,0},{2,3},{3,2},{4,5},{5,4},{6,7},{7,6},{8,9},{9,8},{10,11... | collective-permute-start | bytes 196616 | tf_op jit(solution)/shard_map/ppermute | solution.py:255
  163.3 0.8 pad_maximum_fusion.1
  164.1 3.9 %all-to-all-done.1 = f32[16,8,128]{2,1,0:T(8,128)S(1)} async-done(((f32[16,8,128]{2,1,0:T(8,128)}), f32[16,8,128]{2,1,0:T(8,128)S(1)}, u32[]{:S(2)}, u32[]{:S(2)}) %all-to-all-start.1) | async-done | bytes 65568 | tf_op jit(solution)/shard_map/all_to_all | solution.py:194
  168.0 0.6 slice.92
  168.6 0.6 reshape.26
  169.2 0.0 collective-permute-done.7
  169.2 0.6 pad_maximum_fusion.7
  169.9 0.6 pad_maximum_fusion.6
  (11 shorter events, 0.2 us)
Async XLA Ops:
  7.2 17.2 %copy-start.1 = (bf16[128,1792]{1,0:T(8,128)(2,1)S(1)}, bf16[128,1792]{1,0:T(8,128)(2,1)}, u32[]{:S(2)}) copy-start(bf16[128,1792]{1,0:T(8,128)(2,1)} %g_own.1) | copy-start | bytes 1376260
  7.2 20.0 %copy-start = (bf16[128,1792]{1,0:T(8,128)(2,1)S(1)}, bf16[128,1792]{1,0:T(8,128)(2,1)}, u32[]{:S(2)}) copy-start(bf16[128,1792]{1,0:T(8,128)(2,1)} %q_own.1) | copy-start | bytes 1376260
  7.2 22.0 %copy-start.5 = (bf16[1792]{0:T(1024)(128)(2,1)S(1)}, bf16[1792]{0:T(1024)(128)(2,1)}, u32[]{:S(2)}) copy-start(bf16[1792]{0:T(1024)(128)(2,1)} %param.10) | copy-start | bytes 10756
  7.2 59.2 %all-gather.3.cloned.1.call-start = ((), (), s32[]{:S(2)}) async-start(), calls=%async_computation.4 | async-start | bytes 2359296 | tf_op jit(solution)/shard_map/all_gather | solution.py:222
  9.6 9.7 %collective-permute-start.2 = (bf16[128,256]{1,0:T(8,128)(2,1)S(1)}, bf16[128,256]{1,0:T(8,128)(2,1)S(1)}, u32[]{:S(2)}, u32[]{:S(2)}) collective-permute-start(bf16[128,256]{1,0:T(8,128)(2,1)S(1)} %pad_maximum_fusion.5), channel_id=1, source_target_pairs={{0,1},{1,0},{2,3},{3,2},{4,5},{5,4},{6,7},{7,6},{8,9},{9,8},{10,11... | collective-permute-start | bytes 196616 | tf_op jit(solution)/shard_map/ppermute | solution.py:218
  19.4 4.1 %collective-permute-start.3 = (bf16[256,256]{1,0:T(8,128)(2,1)S(1)}, bf16[256,256]{1,0:T(8,128)(2,1)S(1)}, u32[]{:S(2)}, u32[]{:S(2)}) collective-permute-start(bf16[256,256]{1,0:T(8,128)(2,1)S(1)} %pad_maximum_fusion.3), channel_id=1, source_target_pairs={{0,16},{1,17},{2,18},{3,19},{4,20},{5,21},{6,22},{7,23},{8,24},{9,... | collective-permute-start | bytes 393224 | tf_op jit(solution)/shard_map/ppermute | solution.py:220
  24.3 122.6 %reduce-scatter.2.cloned.1.call-start = ((), (), s32[]{:S(2)}) async-start(), calls=%async_computation.3 | async-start | bytes 2359296 | tf_op jit(solution)/shard_map/reduce_scatter | solution.py:231
  24.4 6.0 %collective-permute-start.1 = (bf16[128,896]{1,0:T(8,128)(2,1)S(1)}, bf16[128,896]{1,0:T(8,128)(2,1)S(1)}, u32[]{:S(2)}, u32[]{:S(2)}) collective-permute-start(bf16[128,896]{1,0:T(8,128)(2,1)S(1)} %slice_select_fusion), channel_id=1, source_target_pairs={{0,1},{1,0},{2,3},{3,2},{4,5},{5,4},{6,7},{7,6},{8,9},{9,8},{10,11... | collective-permute-start | bytes 688136 | tf_op jit(solution)/shard_map/ppermute | solution.py:225
  27.2 3.4 %collective-permute-start = (bf16[128,896]{1,0:T(8,128)(2,1)S(1)}, bf16[128,896]{1,0:T(8,128)(2,1)S(1)}, u32[]{:S(2)}, u32[]{:S(2)}) collective-permute-start(bf16[128,896]{1,0:T(8,128)(2,1)S(1)} %slice_select_fusion.1), channel_id=1, source_target_pairs={{0,1},{1,0},{2,3},{3,2},{4,5},{5,4},{6,7},{7,6},{8,9},{9,8},{10,11... | collective-permute-start | bytes 688136 | tf_op jit(solution)/shard_map/ppermute | solution.py:224
  30.3 36.0 %copy-start.6 = (bf16[128,896]{1,0:T(8,128)(2,1)}, bf16[128,896]{1,0:T(8,128)(2,1)S(1)}, u32[]{:S(2)}) copy-start(bf16[128,896]{1,0:T(8,128)(2,1)S(1)} %collective-permute-done.1.g_other) | copy-start | bytes 688132
  30.6 35.8 %copy-start.8 = (bf16[128,896]{1,0:T(8,128)(2,1)}, bf16[128,896]{1,0:T(8,128)(2,1)S(1)}, u32[]{:S(2)}) copy-start(bf16[128,896]{1,0:T(8,128)(2,1)S(1)} %collective-permute-done.q_other) | copy-start | bytes 688132
  73.9 0.9 copy-start.9
  73.9 7.1 %copy-start.4 = (f32[8,128]{1,0:T(8,128)S(1)}, f32[8,128]{1,0:T(8,128)}, u32[]{:S(2)}) copy-start(f32[8,128]{1,0:T(8,128)} %get-tuple-element.17) | copy-start | bytes 12292
  73.9 37.1 %copy-start.7 = (bf16[128,896]{1,0:T(8,128)(2,1)S(1)}, bf16[128,896]{1,0:T(8,128)(2,1)}, u32[]{:S(2)}) copy-start(bf16[128,896]{1,0:T(8,128)(2,1)} %get-tuple-element.15) | copy-start | bytes 688132
  73.9 39.3 %copy-start.3 = (bf16[128,896]{1,0:T(8,128)(2,1)S(1)}, bf16[128,896]{1,0:T(8,128)(2,1)}, u32[]{:S(2)}) copy-start(bf16[128,896]{1,0:T(8,128)(2,1)} %get-tuple-element.12) | copy-start | bytes 688132
  73.9 40.5 %copy-start.2 = (bf16[128,896]{1,0:T(8,128)(2,1)S(1)}, bf16[128,896]{1,0:T(8,128)(2,1)}, u32[]{:S(2)}) copy-start(bf16[128,896]{1,0:T(8,128)(2,1)} %get-tuple-element.14) | copy-start | bytes 688132
  74.8 38.4 %collective-permute-start.4 = (bf16[128,896]{1,0:T(8,128)(2,1)S(1)}, bf16[128,896]{1,0:T(8,128)(2,1)S(1)}, u32[]{:S(2)}, u32[]{:S(2)}) collective-permute-start(bf16[128,896]{1,0:T(8,128)(2,1)S(1)} %copy-done.9), channel_id=1, source_target_pairs={{0,1},{1,0},{2,3},{3,2},{4,5},{5,4},{6,7},{7,6},{8,9},{9,8},{10,11... | collective-permute-start | bytes 688136 | tf_op jit(solution)/shard_map/ppermute | solution.py:233
  81.7 68.3 %all-to-all-start = ((f32[32,8,128]{2,1,0:T(8,128)}), f32[32,8,128]{2,1,0:T(8,128)S(1)}, u32[]{:S(2)}, u32[]{:S(2)}) async-start(f32[32,8,128]{2,1,0:T(8,128)} %broadcast_in_dim.7), calls=%async_computation.1 | async-start | bytes 262144 | tf_op jit(solution)/shard_map/all_to_all | solution.py:194
  111.0 3.4 %collective-permute-start.5 = (bf16[128,896]{1,0:T(8,128)(2,1)S(1)}, bf16[128,896]{1,0:T(8,128)(2,1)S(1)}, u32[]{:S(2)}, u32[]{:S(2)}) collective-permute-start(bf16[128,896]{1,0:T(8,128)(2,1)S(1)} %copy-done.7), channel_id=1, source_target_pairs={{0,1},{1,0},{2,3},{3,2},{4,5},{5,4},{6,7},{7,6},{8,9},{9,8},{10,11... | collective-permute-start | bytes 688136 | tf_op jit(solution)/shard_map/ppermute | solution.py:234
  147.8 12.4 %collective-permute-start.6 = (bf16[256,256]{1,0:T(8,128)(2,1)S(1)}, bf16[256,256]{1,0:T(8,128)(2,1)S(1)}, u32[]{:S(2)}, u32[]{:S(2)}) collective-permute-start(bf16[256,256]{1,0:T(8,128)(2,1)S(1)} %slice_bitcast_fusion.1), channel_id=1, source_target_pairs={{16,0},{17,1},{18,2},{19,3},{20,4},{21,5},{22,6},{23,7},{24,8},{25... | collective-permute-start | bytes 393224 | tf_op jit(solution)/shard_map/ppermute | solution.py:249
  150.6 17.4 %all-to-all-start.1 = ((f32[16,8,128]{2,1,0:T(8,128)}), f32[16,8,128]{2,1,0:T(8,128)S(1)}, u32[]{:S(2)}, u32[]{:S(2)}) async-start(f32[16,8,128]{2,1,0:T(8,128)} %broadcast_in_dim.8), calls=%async_computation.2 | async-start | bytes 131072 | tf_op jit(solution)/shard_map/all_to_all | solution.py:194
  161.3 7.9 %collective-permute-start.7 = (bf16[128,256]{1,0:T(8,128)(2,1)S(1)}, bf16[128,256]{1,0:T(8,128)(2,1)S(1)}, u32[]{:S(2)}, u32[]{:S(2)}) collective-permute-start(bf16[128,256]{1,0:T(8,128)(2,1)S(1)} %get-tuple-element.27), channel_id=1, source_target_pairs={{0,1},{1,0},{2,3},{3,2},{4,5},{5,4},{6,7},{7,6},{8,9},{9,8},{10,11... | collective-permute-start | bytes 196616 | tf_op jit(solution)/shard_map/ppermute | solution.py:255
Sparse Core Ops, SparseCore 0:
  24.4 41.9 all-gather.2
  74.1 72.8 reduce-scatter.1

commit v2 on v1

v2 whole, which is shorter than its diff:
```python
import functools
import math

import jax
import jax.numpy as jnp
from jax import lax
from jax.experimental import pallas as pl
from jax.experimental.pallas import tpu as pltpu
from jax.sharding import Mesh, PartitionSpec as P

HEADS = 14
KV_HEADS = 2
HEAD_DIM = 128
GROUP = HEADS // KV_HEADS
TOK = 128
CHUNK = 256
LONGEST = 3072
SLOTS = LONGEST // CHUNK + 1
NDOC = 16
SCALE = 1.0 / math.sqrt(HEAD_DIM)
LOG2E = math.log2(math.e)
NEGATIVE = -1e30
F32 = jnp.float32
BF16 = jnp.bfloat16


def dot(a, b):
    return jnp.dot(a, b, preferred_element_type=F32)


def fold_rows(values, how):
    return how(values.reshape(values.shape[0] // 8, 8, values.shape[1]), axis=0)


def attention_kernel(
    place, lengths, q_own, g_own, q_other, g_other, bias_q, bias_v, kv,
    att_own, att_send, gq_own, gq_send, dkv, bias_out,
    q_s, qt_s, g_s, gt_s, v_s, s_s, p_s, d_s, mx_s, l_s, ot_s, dqt_s, rl_s, delta_s, mask_s, bv_s,
):
    core = place[0]
    chunk_id = place[1]
    first_token = chunk_id * CHUNK

    token = first_token + lax.broadcasted_iota(jnp.int32, (1, CHUNK), 1)
    first_seen = jnp.zeros((1, CHUNK), jnp.int32)
    begin = jnp.int32(0)
    lowest = jnp.int32(0)
    for i in range(NDOC):
        first_seen = jnp.where(token >= begin, begin, first_seen)
        lowest = jnp.where(first_token >= begin, begin, lowest)
        begin = begin + lengths[0, i]
    low = lax.div(lowest, jnp.int32(CHUNK))

    own_at = pl.multiple_of(core * TOK, TOK)
    other_at = pl.multiple_of((1 - core) * TOK, TOK)
    for h in range(GROUP):
        cols = pl.ds(h * HEAD_DIM, HEAD_DIM)
        own_cols = pl.ds(pl.multiple_of((core * GROUP + h) * HEAD_DIM, HEAD_DIM), HEAD_DIM)
        bias_row = bias_q[:, own_cols].astype(F32)
        own_rows = pl.ds(h * CHUNK + own_at, TOK)
        other_rows = pl.ds(h * CHUNK + other_at, TOK)
        q_s[own_rows, :] = (q_own[:, own_cols].astype(F32) + bias_row).astype(BF16)
        q_s[other_rows, :] = (q_other[:, cols].astype(F32) + bias_row).astype(BF16)
        g_s[own_rows, :] = g_own[:, own_cols]
        g_s[other_rows, :] = g_other[:, cols]
    for h in range(GROUP):
        at = pl.ds(h * CHUNK, CHUNK)
        qt_s[:, at] = q_s[at, :].T
        gt_s[:, at] = g_s[at, :].T
    mx_s[...] = jnp.full(mx_s.shape, NEGATIVE, F32)
    l_s[...] = jnp.zeros(l_s.shape, F32)
    ot_s[...] = jnp.zeros(ot_s.shape, F32)
    dqt_s[...] = jnp.zeros(dqt_s.shape, F32)
    bv_s[...] = jnp.zeros(bv_s.shape, F32)
    dkv[...] = jnp.zeros(dkv.shape, BF16)
    bias_v_row = bias_v[:, pl.ds(pl.multiple_of(core * HEAD_DIM, HEAD_DIM), HEAD_DIM)].astype(F32)

    def where_of(c):
        return lax.rem(c, 8), lax.div(c, 8)

    def scores(c, carry):
        y, x = where_of(c)
        keys = kv[y, x, :, :HEAD_DIM]
        v_s[c - low] = (kv[y, x, :, HEAD_DIM:].astype(F32) + bias_v_row).astype(BF16)
        key_index = c * CHUNK + lax.broadcasted_iota(jnp.int32, (CHUNK, CHUNK), 0)
        allowed = jnp.logical_and(key_index <= token, key_index >= first_seen)
        mask_s[...] = jnp.where(allowed, 0.0, NEGATIVE)
        for h in range(GROUP):
            at = pl.ds(h * CHUNK, CHUNK)
            raw = dot(keys, qt_s[:, at]) * (SCALE * LOG2E) + mask_s[...]
            s_s[c - low, :, at] = raw
            mx_s[:, at] = jnp.maximum(mx_s[:, at], fold_rows(raw, jnp.max))
        return carry

    lax.fori_loop(low, chunk_id + 1, scores, 0)
    mx_s[...] = jnp.broadcast_to(jnp.max(mx_s[...], axis=0, keepdims=True), mx_s.shape)

    def weigh(c, carry):
        values_t = v_s[c - low].T
        for h in range(GROUP):
            at = pl.ds(h * CHUNK, CHUNK)
            probs = jnp.exp2(s_s[c - low, :, at] - mx_s[0:1, at])
            s_s[c - low, :, at] = probs
            l_s[:, at] = l_s[:, at] + fold_rows(probs, jnp.sum)
            ot_s[:, at] = ot_s[:, at] + dot(values_t, probs.astype(BF16))
        return carry

    lax.fori_loop(low, chunk_id + 1, weigh, 0)

    for h in range(GROUP):
        at = pl.ds(h * CHUNK, CHUNK)
        cols = pl.ds(h * HEAD_DIM, HEAD_DIM)
        inverse = 1.0 / jnp.sum(l_s[:, at], axis=0, keepdims=True)
        rl_s[:, at] = jnp.broadcast_to(inverse, (8, CHUNK))
        out_t = (ot_s[:, at] * inverse).astype(BF16)
        delta = jnp.sum(out_t.astype(F32) * gt_s[:, at].astype(F32), axis=0, keepdims=True)
        delta_s[:, at] = jnp.broadcast_to(delta, (8, CHUNK))
        rows = out_t.T.reshape(2, TOK, HEAD_DIM)
        att_own[:, cols] = jnp.where(core == 0, rows[0], rows[1])
        att_send[:, cols] = jnp.where(core == 0, rows[1], rows[0])

    def slopes_of(c, carry):
        y, x = where_of(c)
        values = v_s[c - low]
        for h in range(GROUP):
            at = pl.ds(h * CHUNK, CHUNK)
            dots = dot(values, gt_s[:, at])
            probs = s_s[c - low, :, at] * rl_s[0:1, at]
            p_s[:, at] = probs.astype(BF16)
            d_s[:, at] = (probs * (dots - delta_s[0:1, at])).astype(BF16)
        dk = dot(d_s[...], q_s[...])
        dv = dot(p_s[...], g_s[...])
        keys_t = kv[y, x, :, :HEAD_DIM].T
        dqt_s[...] = dqt_s[...] + dot(keys_t, d_s[...])
        dkv[y, x, :, :HEAD_DIM] = (dk * SCALE).astype(BF16)
        dkv[y, x, :, HEAD_DIM:] = dv.astype(BF16)
        bv_s[...] = bv_s[...] + fold_rows(dv, jnp.sum)
        return carry

    lax.fori_loop(low, chunk_id + 1, slopes_of, 0)

    for h in range(GROUP):
        cols = pl.ds(h * HEAD_DIM, HEAD_DIM)
        grad = (dqt_s[:, pl.ds(h * CHUNK, CHUNK)] * SCALE).T
        bias_out[h : h + 1, :] = jnp.sum(grad, axis=0, keepdims=True)
        rows = grad.astype(BF16).reshape(2, TOK, HEAD_DIM)
        gq_own[:, cols] = jnp.where(core == 0, rows[0], rows[1])
        gq_send[:, cols] = jnp.where(core == 0, rows[1], rows[0])
    bias_out[GROUP : GROUP + 1, :] = jnp.sum(bv_s[...], axis=0, keepdims=True)


def attention(place, lengths, q_own, g_own, q_other, g_other, bias_q, bias_v, kv):
    half = jax.ShapeDtypeStruct((TOK, GROUP * HEAD_DIM), BF16)
    vmem = pl.BlockSpec(memory_space=pltpu.VMEM)
    smem = pl.BlockSpec(memory_space=pltpu.SMEM)
    queries = GROUP * CHUNK
    stat = pltpu.VMEM((8, queries), F32)
    pairs = CHUNK * SLOTS * queries
    return pl.pallas_call(
        attention_kernel,
        out_shape=[half] * 4
        + [
            jax.ShapeDtypeStruct(kv.shape, BF16),
            jax.ShapeDtypeStruct((8, HEAD_DIM), F32),
        ],
        in_specs=[smem] * 2 + [vmem] * 7,
        out_specs=[vmem] * 6,
        scratch_shapes=[
            pltpu.VMEM((queries, HEAD_DIM), BF16),
            pltpu.VMEM((HEAD_DIM, queries), BF16),
            pltpu.VMEM((queries, HEAD_DIM), BF16),
            pltpu.VMEM((HEAD_DIM, queries), BF16),
            pltpu.VMEM((SLOTS, CHUNK, HEAD_DIM), BF16),
            pltpu.VMEM((SLOTS, CHUNK, queries), F32),
            pltpu.VMEM((CHUNK, queries), BF16),
            pltpu.VMEM((CHUNK, queries), BF16),
            stat,
            stat,
            pltpu.VMEM((HEAD_DIM, queries), F32),
            pltpu.VMEM((HEAD_DIM, queries), F32),
            stat,
            stat,
            pltpu.VMEM((CHUNK, CHUNK), F32),
            pltpu.VMEM((8, HEAD_DIM), F32),
        ],
        compiler_params=pltpu.CompilerParams(vmem_limit_bytes=58 * 1024 * 1024),
        cost_estimate=pl.CostEstimate(
            flops=12 * pairs * HEAD_DIM, bytes_accessed=8 << 20, transcendentals=pairs
        ),
    )(place, lengths, q_own, g_own, q_other, g_other, bias_q, bias_v, kv)


SEQ = ("xlo", "y", "core")
SWAP = [(0, 1), (1, 0)]


def everyone(part, axes, count):
    spread = jnp.broadcast_to(part[None], (count,) + part.shape)
    return lax.all_to_all(spread, axes, split_axis=0, concat_axis=0, tiled=True)


def body(queries, keys, values, bias_query, bias_value, doc_lengths, grad_out):
    x = lax.axis_index("xlo")
    y = lax.axis_index("y")
    core = lax.axis_index("core")
    width = GROUP * HEAD_DIM
    low_core = core == 0

    def columns(array, which, size):
        return jnp.where(which == 0, array[:, :size], array[:, size:])

    def joined(mine, other, axis):
        return jnp.where(
            low_core,
            jnp.concatenate([mine, other], axis=axis),
            jnp.concatenate([other, mine], axis=axis),
        )

    def kv_head(which):
        return jnp.concatenate(
            [columns(keys, which, HEAD_DIM), columns(values, which, HEAD_DIM)], axis=1
        )

    kv_mine, kv_send = kv_head(core), kv_head(1 - core)
    kv_other = lax.ppermute(kv_send, "core", SWAP)
    low_mine = lax.ppermute(kv_mine, "xlo", [(0, 1)])
    low_other = lax.ppermute(kv_send, ("xlo", "core"), [(0, 3), (1, 2)])
    own = joined(kv_mine, kv_other, 0)
    two = jnp.stack([jnp.where(x == 0, own, joined(low_mine, low_other, 0)), own])
    gathered = lax.all_gather(two, "y", axis=0, tiled=False)

    q_other = lax.ppermute(columns(queries, 1 - core, width), "core", SWAP)
    g_other = lax.ppermute(columns(grad_out, 1 - core, width), "core", SWAP)
    place = jnp.stack([core, x * 8 + y]).astype(jnp.int32)
    att_own, att_send, gq_own, gq_send, dkv, bias_part = attention(
        place,
        doc_lengths,
        queries,
        grad_out,
        q_other,
        g_other,
        bias_query[None, :],
        bias_value[None, :],
        gathered,
    )

    reduced = lax.psum_scatter(dkv, "y", scatter_dimension=0, tiled=False)

    att_other = lax.ppermute(att_send, "core", SWAP)
    gq_other = lax.ppermute(gq_send, "core", SWAP)
    attended = joined(att_own, att_other, 1)
    grad_queries = joined(gq_own, gq_other, 1)
    over_packs = jnp.sum(everyone(bias_part, ("z", "xhi", "xlo"), 32), axis=0)
    over_all = jnp.sum(everyone(over_packs, ("y", "core"), 16).reshape(8, 2, 8, HEAD_DIM), axis=0)
    grad_bias_query = over_all[:, :GROUP].reshape(HEADS * HEAD_DIM)
    grad_bias_value = over_all[:, GROUP].reshape(KV_HEADS * HEAD_DIM)
    reduced, attended, grad_queries, grad_bias_query, grad_bias_value = lax.optimization_barrier(
        (reduced, attended, grad_queries, grad_bias_query, grad_bias_value)
    )

    low_sum = reduced[0]
    half_sum = jnp.where(x == 0, low_sum, reduced[1])

    def tokens(array, which):
        return jnp.where(which == 0, array[:TOK], array[TOK:])

    from_core = lax.ppermute(tokens(half_sum, 1 - core), "core", SWAP)
    high_mine = lax.ppermute(tokens(low_sum, core), "xlo", [(1, 0)])
    high_other = lax.ppermute(tokens(low_sum, 1 - core), ("xlo", "core"), [(2, 1), (3, 0)])

    def added(first, second):
        return (first.astype(F32) + jnp.where(x == 0, second.astype(F32), 0.0)).astype(BF16)

    mine = added(tokens(half_sum, core), high_mine)
    other = added(from_core, high_other)
    grad_keys = joined(mine[:, :HEAD_DIM], other[:, :HEAD_DIM], 1)
    grad_values = joined(mine[:, HEAD_DIM:], other[:, HEAD_DIM:], 1)
    return attended, grad_queries, grad_keys, grad_values, grad_bias_query, grad_bias_value


def solution(mesh):
    parts = Mesh(mesh.devices.reshape(8, 2, 2, 8, 2), ("z", "xhi", "xlo", "y", "core"))
    rows = P(("z", "xhi") + SEQ, None)
    in_specs = (rows, rows, rows, P(), P(), P(("z", "xhi"), None), rows)
    out_specs = (rows, rows, rows, rows, P(), P())
    return jax.shard_map(body, mesh=parts, in_specs=in_specs, out_specs=out_specs, check_vma=False)
```

time: 179 us -> 159 us (0.89)
  waiting for transfers between devices: 77.3 us -> 54.6 us
  starting transfers between devices: 65.4 us -> 70.6 us
    reduce_scatter x1, waiting for transfers between devices: 32.5 us -> 0.18 us  [body(): reduced = lax.psum_scatter(dkv, 'y', scatter_dimension=0, tiled=False)]
    all_to_all x2, waiting for transfers between devices: 3.93 us -> 14.4 us  [everyone(): return lax.all_to_all(spread, axes, split_axis=0, concat_axis=0, tiled=True)]
    ppermute x4 -> x6, starting transfers between devices: 13.4 us -> 20.6 us  [the longest x1 6.66 us: body(): from_core = lax.ppermute(tokens(half_sum, 1 - core), 'core', SWAP)]
    select_n x6 -> x8, other arithmetic: 1.19 us -> 5.04 us  [the longest x4 3.04 us: joined(): jnp.where(low_core, jnp.concatenate([mine, other], axis=axis), jnp.concat...]
    concatenate x6 -> x2, other arithmetic: 2.9 us -> 0.02 us  [kv_head(): jnp.concatenate([columns(keys, which, HEAD_DIM), columns(values, which, H...]
    ppermute x4 -> x6, waiting for transfers between devices: 3.7 us -> 5.48 us  [the longest x1 4.62 us: body(): lax.ppermute(tokens(low_sum, 1 - core), ('xlo', 'core'), [(2, 1), (3, 0)])]
  transfers between devices with their start and end apart: 12 -> 14, of which waited for: 7 -> 6; matrix products, arithmetic and copies ran while one was open for 4% -> 4% of each run, Pallas kernels for 0% -> 0%
where the time goes in v2:
time: 159 us; the launch traced here: 158 us
  starting transfers between devices  70.6 us (44%)
  waiting for transfers between devices  54.6 us (34%)
  between operations  14.4 us (9%)
  other arithmetic  7.48 us (5%)
  Pallas kernels  6.75 us (4%)
  local copies, waits for them, and re-layouts  4.55 us (3%)
    all_to_all x2, starting transfers between devices, everyone(): return lax.all_to_all(spread, axes, split_axis=0, concat_axis=0, tiled=True)  37.2 us
    all_gather x1, waiting for transfers between devices, body(): gathered = lax.all_gather(two, 'y', axis=0, tiled=False)  34.5 us
    all_to_all x2, waiting for transfers between devices, everyone(): return lax.all_to_all(spread, axes, split_axis=0, concat_axis=0, tiled=True)  14.4 us
    pallas_call x1, Pallas kernels, attention(): pl.pallas_call(attention_kernel, out_shape=[half] * 4 + [jax.ShapeDtypeSt...  6.75 us
    ppermute x1, starting transfers between devices, body(): from_core = lax.ppermute(tokens(half_sum, 1 - core), 'core', SWAP)  6.66 us
    ppermute x1, starting transfers between devices, body(): att_other = lax.ppermute(att_send, 'core', SWAP)  6.2 us
    ppermute x1, starting transfers between devices, body(): kv_other = lax.ppermute(kv_send, 'core', SWAP)  5.57 us
    ppermute x1, waiting for transfers between devices, body(): lax.ppermute(tokens(low_sum, 1 - core), ('xlo', 'core'), [(2, 1), (3, 0)])  4.62 us
  transfers between devices with their start and end apart: 14, of which 6 were waited for; matrix products, arithmetic and copies ran while one was open for 4% of the time, Pallas kernels for 0%

profile of v2, /device:TPU:1, one launch (start us, length us, event | category | flops | bytes accessed | tf_op | source)
XLA Modules:
  0.0 158.5 jit_solution(502866819211448758)
XLA Ops:
  7.2 0.0 copy-start.1
  7.2 0.0 copy-start
  7.2 0.0 copy-start.10
  7.2 0.0 copy-start.5
  7.2 0.0 all-gather.3.cloned.1.call-start
  7.3 0.9 broadcast_select_fusion.2
  8.2 3.9 %collective-permute-start.3 = (bf16[128,256]{1,0:T(8,128)(2,1)S(1)}, bf16[128,256]{1,0:T(8,128)(2,1)S(1)}, u32[]{:S(2)}, u32[]{:S(2)}) collective-permute-start(bf16[128,256]{1,0:T(8,128)(2,1)S(1)} %get-tuple-element.36), channel_id=1, source_target_pairs={{0,16},{1,17},{2,18},{3,19},{4,20},{5,21},{6,22},{7,23},{8,24},{9,... | collective-permute-start | bytes 196616 | tf_op jit(solution)/shard_map/ppermute | solution.py:226
  12.1 1.9 %collective-permute-start.4 = (bf16[128,256]{1,0:T(8,128)(2,1)S(1)}, bf16[128,256]{1,0:T(8,128)(2,1)S(1)}, u32[]{:S(2)}, u32[]{:S(2)}) collective-permute-start(bf16[128,256]{1,0:T(8,128)(2,1)S(1)} %pad_maximum_fusion.2), channel_id=1, source_target_pairs={{0,17},{1,16},{2,19},{3,18},{4,21},{5,20},{6,23},{7,22},{8,25},{9,... | collective-permute-start | bytes 196616 | tf_op jit(solution)/shard_map/ppermute | solution.py:227
  14.0 5.6 %collective-permute-start.2 = (bf16[128,256]{1,0:T(8,128)(2,1)S(1)}, bf16[128,256]{1,0:T(8,128)(2,1)S(1)}, u32[]{:S(2)}, u32[]{:S(2)}) collective-permute-start(bf16[128,256]{1,0:T(8,128)(2,1)S(1)} %pad_maximum_fusion.2), channel_id=1, source_target_pairs={{0,1},{1,0},{2,3},{3,2},{4,5},{5,4},{6,7},{7,6},{8,9},{9,8},{10,11... | collective-permute-start | bytes 196616 | tf_op jit(solution)/shard_map/ppermute | solution.py:225
  19.6 0.0 collective-permute-done.3
  19.6 0.0 collective-permute-done.4
  19.6 0.9 collective-permute-done.2
  20.5 0.1 fusion
  20.6 0.7 pad_maximum_fusion
  21.3 0.0 all-gather.3.cloned.1.call-update
  21.3 0.0 reduce-scatter.2.cloned.1.call-start
  21.4 0.0 copy-done.1
  21.4 2.3 %collective-permute-start.1 = (bf16[128,896]{1,0:T(8,128)(2,1)S(1)}, bf16[128,896]{1,0:T(8,128)(2,1)S(1)}, u32[]{:S(2)}, u32[]{:S(2)}) collective-permute-start(bf16[128,896]{1,0:T(8,128)(2,1)S(1)} %slice_select_fusion), channel_id=1, source_target_pairs={{0,1},{1,0},{2,3},{3,2},{4,5},{5,4},{6,7},{7,6},{8,9},{9,8},{10,11... | collective-permute-start | bytes 688136 | tf_op jit(solution)/shard_map/ppermute | solution.py:233
  23.7 0.0 copy-done
  23.8 2.1 %collective-permute-start = (bf16[128,896]{1,0:T(8,128)(2,1)S(1)}, bf16[128,896]{1,0:T(8,128)(2,1)S(1)}, u32[]{:S(2)}, u32[]{:S(2)}) collective-permute-start(bf16[128,896]{1,0:T(8,128)(2,1)S(1)} %slice_select_fusion.1), channel_id=1, source_target_pairs={{0,1},{1,0},{2,3},{3,2},{4,5},{5,4},{6,7},{7,6},{8,9},{9,8},{10,11... | collective-permute-start | bytes 688136 | tf_op jit(solution)/shard_map/ppermute | solution.py:232
  25.8 0.0 copy-done.10
  25.8 0.6 broadcast_in_dim.24.bias_v
  26.4 0.0 copy-done.5
  26.4 0.6 broadcast_in_dim.23.bias_q
  27.0 0.6 pad_add_fusion.place
  27.7 0.0 collective-permute-done.1.g_other
  27.7 0.0 collective-permute-done.q_other
  27.7 0.0 copy-start.8
  27.7 34.5 %all-gather.3.cloned.1.call-done = bf16[16,256,256]{2,1,0:T(8,128)(2,1)} async-done(((bf16[2,256,256]{2,1,0:T(8,128)(2,1)}), bf16[16,256,256]{2,1,0:T(8,128)(2,1)}) %all-gather.3.cloned.1.call-update) | async-done | bytes 2097168 | tf_op jit(solution)/shard_map/all_gather | solution.py:230
  62.2 0.0 copy-done.7
  62.2 0.0 copy-done.8
  62.2 6.7 %shard_map.118 = (bf16[128,896]{1,0:T(8,128)(2,1)}, bf16[128,896]{1,0:T(8,128)(2,1)}, bf16[128,896]{1,0:T(8,128)(2,1)}, bf16[128,896]{1,0:T(8,128)(2,1)}, bf16[8...) custom-call(s32[2]{0:T(128)} %pad_add_fusion.place, s32[1,16]{1,0:T(1,128)} %lengths.1, bf16[128,1792]{1,0:T(8,128)(2,1)} %q_own.1, ...), custom_call_target="tpu_custom_call" | custom-call | flops 9160359936 | bytes 8388608 | tf_op jit(solution)/shard_map/pallas_call | solution.py:159
  68.9 0.0 copy-start.6
  68.9 0.0 copy-start.3
  69.0 0.0 copy-start.2
  69.0 0.0 reduce-scatter.2.cloned.1.call-update
  69.0 0.9 copy-done.9
  69.9 6.2 %collective-permute-start.5 = (bf16[128,896]{1,0:T(8,128)(2,1)S(1)}, bf16[128,896]{1,0:T(8,128)(2,1)S(1)}, u32[]{:S(2)}, u32[]{:S(2)}) collective-permute-start(bf16[128,896]{1,0:T(8,128)(2,1)S(1)} %copy-done.9), channel_id=1, source_target_pairs={{0,1},{1,0},{2,3},{3,2},{4,5},{5,4},{6,7},{7,6},{8,9},{9,8},{10,11... | collective-permute-start | bytes 688136 | tf_op jit(solution)/shard_map/ppermute | solution.py:249
  76.1 0.0 copy-done.4
  76.1 0.6 broadcast_in_dim.25
  76.7 24.8 %all-to-all-start = ((f32[32,8,128]{2,1,0:T(8,128)}), f32[32,8,128]{2,1,0:T(8,128)S(1)}, u32[]{:S(2)}, u32[]{:S(2)}) async-start(f32[32,8,128]{2,1,0:T(8,128)} %broadcast_in_dim.25), calls=%async_computation.1 | async-start | bytes 262144 | tf_op jit(solution)/shard_map/all_to_all | solution.py:199
  101.6 0.0 copy-done.6
  101.6 2.2 %collective-permute-start.6 = (bf16[128,896]{1,0:T(8,128)(2,1)S(1)}, bf16[128,896]{1,0:T(8,128)(2,1)S(1)}, u32[]{:S(2)}, u32[]{:S(2)}) collective-permute-start(bf16[128,896]{1,0:T(8,128)(2,1)S(1)} %copy-done.6), channel_id=1, source_target_pairs={{0,1},{1,0},{2,3},{3,2},{4,5},{5,4},{6,7},{7,6},{8,9},{9,8},{10,11... | collective-permute-start | bytes 688136 | tf_op jit(solution)/shard_map/ppermute | solution.py:250
  103.8 0.0 collective-permute-done.5
  103.8 0.9 maximum_select_fusion
  104.7 6.8 %all-to-all-done = f32[32,8,128]{2,1,0:T(8,128)S(1)} async-done(((f32[32,8,128]{2,1,0:T(8,128)}), f32[32,8,128]{2,1,0:T(8,128)S(1)}, u32[]{:S(2)}, u32[]{:S(2)}) %all-to-all-start) | async-done | bytes 131104 | tf_op jit(solution)/shard_map/all_to_all | solution.py:199
  111.6 0.6 broadcast_in_dim.26
  112.2 12.4 %all-to-all-start.1 = ((f32[16,8,128]{2,1,0:T(8,128)}), f32[16,8,128]{2,1,0:T(8,128)S(1)}, u32[]{:S(2)}, u32[]{:S(2)}) async-start(f32[16,8,128]{2,1,0:T(8,128)} %broadcast_in_dim.26), calls=%async_computation.2 | async-start | bytes 131072 | tf_op jit(solution)/shard_map/all_to_all | solution.py:199
  124.6 0.0 collective-permute-done.6
  124.6 0.9 maximum_select_fusion.1
  125.5 7.6 %all-to-all-done.1 = f32[16,8,128]{2,1,0:T(8,128)S(1)} async-done(((f32[16,8,128]{2,1,0:T(8,128)}), f32[16,8,128]{2,1,0:T(8,128)S(1)}, u32[]{:S(2)}, u32[]{:S(2)}) %all-to-all-start.1) | async-done | bytes 65568 | tf_op jit(solution)/shard_map/all_to_all | solution.py:199
  133.1 0.6 slice.95
  133.7 0.6 reshape.166
  134.3 0.2 reduce-scatter.2.cloned.1.call-done
  134.4 1.0 slice_select_fusion.2
  135.4 0.9 select_bitcast_fusion.2
  136.3 1.3 collective-permute-start.7
  137.6 6.7 %collective-permute-start.8 = (bf16[128,256]{1,0:T(8,128)(2,1)S(1)}, bf16[128,256]{1,0:T(8,128)(2,1)S(1)}, u32[]{:S(2)}, u32[]{:S(2)}) collective-permute-start(bf16[128,256]{1,0:T(8,128)(2,1)S(1)} %select_bitcast_fusion.1), channel_id=1, source_target_pairs={{0,1},{1,0},{2,3},{3,2},{4,5},{5,4},{6,7},{7,6},{8,9},{9,8},{10,11... | collective-permute-start | bytes 196616 | tf_op jit(solution)/shard_map/ppermute | solution.py:267
  144.3 1.3 collective-permute-start.9
  145.6 0.0 collective-permute-done.7
  145.7 0.0 collective-permute-done.8
  145.7 4.6 %collective-permute-done.9 = bf16[128,256]{1,0:T(8,128)(2,1)S(1)} collective-permute-done((bf16[128,256]{1,0:T(8,128)(2,1)S(1)}, bf16[128,256]{1,0:T(8,128)(2,1)S(1)}, u32[]{:S(2)}, u32[]{:S(2)}) %collective-permute-start.9) | collective-permute-done | bytes 65568 | tf_op jit(solution)/shard_map/ppermute | solution.py:269
  150.3 0.6 maximum_select_fusion.5
  151.0 0.6 maximum_select_fusion.4
  (16 shorter events, 0.2 us)
Async XLA Ops:
  7.2 14.2 %copy-start.1 = (bf16[128,1792]{1,0:T(8,128)(2,1)S(1)}, bf16[128,1792]{1,0:T(8,128)(2,1)}, u32[]{:S(2)}) copy-start(bf16[128,1792]{1,0:T(8,128)(2,1)} %g_own.1) | copy-start | bytes 1376260
  7.2 16.5 %copy-start = (bf16[128,1792]{1,0:T(8,128)(2,1)S(1)}, bf16[128,1792]{1,0:T(8,128)(2,1)}, u32[]{:S(2)}) copy-start(bf16[128,1792]{1,0:T(8,128)(2,1)} %q_own.1) | copy-start | bytes 1376260
  7.2 18.6 %copy-start.10 = (bf16[256]{0:T(256)(128)(2,1)S(1)}, bf16[256]{0:T(256)(128)(2,1)}, u32[]{:S(2)}) copy-start(bf16[256]{0:T(256)(128)(2,1)} %param.11) | copy-start | bytes 1540
  7.2 19.2 %copy-start.5 = (bf16[1792]{0:T(1024)(128)(2,1)S(1)}, bf16[1792]{0:T(1024)(128)(2,1)}, u32[]{:S(2)}) copy-start(bf16[1792]{0:T(1024)(128)(2,1)} %param.10) | copy-start | bytes 10756
  7.2 55.0 %all-gather.3.cloned.1.call-start = ((), (), s32[]{:S(2)}) async-start(), calls=%async_computation.4 | async-start | bytes 2359296 | tf_op jit(solution)/shard_map/all_gather | solution.py:230
  8.2 11.4 %collective-permute-start.3 = (bf16[128,256]{1,0:T(8,128)(2,1)S(1)}, bf16[128,256]{1,0:T(8,128)(2,1)S(1)}, u32[]{:S(2)}, u32[]{:S(2)}) collective-permute-start(bf16[128,256]{1,0:T(8,128)(2,1)S(1)} %get-tuple-element.36), channel_id=1, source_target_pairs={{0,16},{1,17},{2,18},{3,19},{4,20},{5,21},{6,22},{7,23},{8,24},{9,... | collective-permute-start | bytes 196616 | tf_op jit(solution)/shard_map/ppermute | solution.py:226
  12.1 7.5 %collective-permute-start.4 = (bf16[128,256]{1,0:T(8,128)(2,1)S(1)}, bf16[128,256]{1,0:T(8,128)(2,1)S(1)}, u32[]{:S(2)}, u32[]{:S(2)}) collective-permute-start(bf16[128,256]{1,0:T(8,128)(2,1)S(1)} %pad_maximum_fusion.2), channel_id=1, source_target_pairs={{0,17},{1,16},{2,19},{3,18},{4,21},{5,20},{6,23},{7,22},{8,25},{9,... | collective-permute-start | bytes 196616 | tf_op jit(solution)/shard_map/ppermute | solution.py:227
  14.0 6.5 %collective-permute-start.2 = (bf16[128,256]{1,0:T(8,128)(2,1)S(1)}, bf16[128,256]{1,0:T(8,128)(2,1)S(1)}, u32[]{:S(2)}, u32[]{:S(2)}) collective-permute-start(bf16[128,256]{1,0:T(8,128)(2,1)S(1)} %pad_maximum_fusion.2), channel_id=1, source_target_pairs={{0,1},{1,0},{2,3},{3,2},{4,5},{5,4},{6,7},{7,6},{8,9},{9,8},{10,11... | collective-permute-start | bytes 196616 | tf_op jit(solution)/shard_map/ppermute | solution.py:225
  21.3 113.1 %reduce-scatter.2.cloned.1.call-start = ((), (), s32[]{:S(2)}) async-start(), calls=%async_computation.3 | async-start | bytes 2359296 | tf_op jit(solution)/shard_map/reduce_scatter | solution.py:247
  21.4 6.2 %collective-permute-start.1 = (bf16[128,896]{1,0:T(8,128)(2,1)S(1)}, bf16[128,896]{1,0:T(8,128)(2,1)S(1)}, u32[]{:S(2)}, u32[]{:S(2)}) collective-permute-start(bf16[128,896]{1,0:T(8,128)(2,1)S(1)} %slice_select_fusion), channel_id=1, source_target_pairs={{0,1},{1,0},{2,3},{3,2},{4,5},{5,4},{6,7},{7,6},{8,9},{9,8},{10,11... | collective-permute-start | bytes 688136 | tf_op jit(solution)/shard_map/ppermute | solution.py:233
  23.8 3.9 %collective-permute-start = (bf16[128,896]{1,0:T(8,128)(2,1)S(1)}, bf16[128,896]{1,0:T(8,128)(2,1)S(1)}, u32[]{:S(2)}, u32[]{:S(2)}) collective-permute-start(bf16[128,896]{1,0:T(8,128)(2,1)S(1)} %slice_select_fusion.1), channel_id=1, source_target_pairs={{0,1},{1,0},{2,3},{3,2},{4,5},{5,4},{6,7},{7,6},{8,9},{9,8},{10,11... | collective-permute-start | bytes 688136 | tf_op jit(solution)/shard_map/ppermute | solution.py:232
  27.7 34.5 %copy-start.7 = (bf16[128,896]{1,0:T(8,128)(2,1)}, bf16[128,896]{1,0:T(8,128)(2,1)S(1)}, u32[]{:S(2)}) copy-start(bf16[128,896]{1,0:T(8,128)(2,1)S(1)} %collective-permute-done.1.g_other) | copy-start | bytes 688132
  27.7 34.5 %copy-start.8 = (bf16[128,896]{1,0:T(8,128)(2,1)}, bf16[128,896]{1,0:T(8,128)(2,1)S(1)}, u32[]{:S(2)}) copy-start(bf16[128,896]{1,0:T(8,128)(2,1)S(1)} %collective-permute-done.q_other) | copy-start | bytes 688132
  68.9 0.9 copy-start.9
  68.9 7.1 %copy-start.4 = (f32[8,128]{1,0:T(8,128)S(1)}, f32[8,128]{1,0:T(8,128)}, u32[]{:S(2)}) copy-start(f32[8,128]{1,0:T(8,128)} %get-tuple-element.22) | copy-start | bytes 12292
  68.9 32.6 %copy-start.6 = (bf16[128,896]{1,0:T(8,128)(2,1)S(1)}, bf16[128,896]{1,0:T(8,128)(2,1)}, u32[]{:S(2)}) copy-start(bf16[128,896]{1,0:T(8,128)(2,1)} %get-tuple-element.21) | copy-start | bytes 688132
  68.9 34.9 %copy-start.3 = (bf16[128,896]{1,0:T(8,128)(2,1)S(1)}, bf16[128,896]{1,0:T(8,128)(2,1)}, u32[]{:S(2)}) copy-start(bf16[128,896]{1,0:T(8,128)(2,1)} %get-tuple-element.18) | copy-start | bytes 688132
  69.0 55.6 %copy-start.2 = (bf16[128,896]{1,0:T(8,128)(2,1)S(1)}, bf16[128,896]{1,0:T(8,128)(2,1)}, u32[]{:S(2)}) copy-start(bf16[128,896]{1,0:T(8,128)(2,1)} %get-tuple-element.20) | copy-start | bytes 688132
  69.9 33.9 %collective-permute-start.5 = (bf16[128,896]{1,0:T(8,128)(2,1)S(1)}, bf16[128,896]{1,0:T(8,128)(2,1)S(1)}, u32[]{:S(2)}, u32[]{:S(2)}) collective-permute-start(bf16[128,896]{1,0:T(8,128)(2,1)S(1)} %copy-done.9), channel_id=1, source_target_pairs={{0,1},{1,0},{2,3},{3,2},{4,5},{5,4},{6,7},{7,6},{8,9},{9,8},{10,11... | collective-permute-start | bytes 688136 | tf_op jit(solution)/shard_map/ppermute | solution.py:249
  76.7 34.8 %all-to-all-start = ((f32[32,8,128]{2,1,0:T(8,128)}), f32[32,8,128]{2,1,0:T(8,128)S(1)}, u32[]{:S(2)}, u32[]{:S(2)}) async-start(f32[32,8,128]{2,1,0:T(8,128)} %broadcast_in_dim.25), calls=%async_computation.1 | async-start | bytes 262144 | tf_op jit(solution)/shard_map/all_to_all | solution.py:199
  101.6 23.0 %collective-permute-start.6 = (bf16[128,896]{1,0:T(8,128)(2,1)S(1)}, bf16[128,896]{1,0:T(8,128)(2,1)S(1)}, u32[]{:S(2)}, u32[]{:S(2)}) collective-permute-start(bf16[128,896]{1,0:T(8,128)(2,1)S(1)} %copy-done.6), channel_id=1, source_target_pairs={{0,1},{1,0},{2,3},{3,2},{4,5},{5,4},{6,7},{7,6},{8,9},{9,8},{10,11... | collective-permute-start | bytes 688136 | tf_op jit(solution)/shard_map/ppermute | solution.py:250
  112.2 20.9 %all-to-all-start.1 = ((f32[16,8,128]{2,1,0:T(8,128)}), f32[16,8,128]{2,1,0:T(8,128)S(1)}, u32[]{:S(2)}, u32[]{:S(2)}) async-start(f32[16,8,128]{2,1,0:T(8,128)} %broadcast_in_dim.26), calls=%async_computation.2 | async-start | bytes 131072 | tf_op jit(solution)/shard_map/all_to_all | solution.py:199
  136.3 9.3 %collective-permute-start.7 = (bf16[128,256]{1,0:T(8,128)(2,1)S(1)}, bf16[128,256]{1,0:T(8,128)(2,1)S(1)}, u32[]{:S(2)}, u32[]{:S(2)}) collective-permute-start(bf16[128,256]{1,0:T(8,128)(2,1)S(1)} %get-tuple-element.28), channel_id=1, source_target_pairs={{16,0},{17,1},{18,2},{19,3},{20,4},{21,5},{22,6},{23,7},{24,8},{25... | collective-permute-start | bytes 196616 | tf_op jit(solution)/shard_map/ppermute | solution.py:268
  137.6 8.0 %collective-permute-start.8 = (bf16[128,256]{1,0:T(8,128)(2,1)S(1)}, bf16[128,256]{1,0:T(8,128)(2,1)S(1)}, u32[]{:S(2)}, u32[]{:S(2)}) collective-permute-start(bf16[128,256]{1,0:T(8,128)(2,1)S(1)} %select_bitcast_fusion.1), channel_id=1, source_target_pairs={{0,1},{1,0},{2,3},{3,2},{4,5},{5,4},{6,7},{7,6},{8,9},{9,8},{10,11... | collective-permute-start | bytes 196616 | tf_op jit(solution)/shard_map/ppermute | solution.py:267
  144.3 6.0 %collective-permute-start.9 = (bf16[128,256]{1,0:T(8,128)(2,1)S(1)}, bf16[128,256]{1,0:T(8,128)(2,1)S(1)}, u32[]{:S(2)}, u32[]{:S(2)}) collective-permute-start(bf16[128,256]{1,0:T(8,128)(2,1)S(1)} %get-tuple-element.29), channel_id=1, source_target_pairs={{16,1},{17,0},{18,3},{19,2},{20,5},{21,4},{22,7},{23,6},{24,9},{25... | collective-permute-start | bytes 196616 | tf_op jit(solution)/shard_map/ppermute | solution.py:269
Sparse Core Ops, SparseCore 0:
  21.5 40.6 all-gather.2
  69.1 65.2 reduce-scatter.1

commit v3 on v2

v3 whole, which is shorter than its diff:
```python
import functools
import math

import jax
import jax.numpy as jnp
from jax import lax
from jax.experimental import pallas as pl
from jax.experimental.pallas import tpu as pltpu
from jax.sharding import Mesh, PartitionSpec as P

HEADS = 14
KV_HEADS = 2
HEAD_DIM = 128
GROUP = HEADS // KV_HEADS
TOK = 128
CHUNK = 256
LONGEST = 3072
SLOTS = LONGEST // CHUNK + 1
NDOC = 16
SCALE = 1.0 / math.sqrt(HEAD_DIM)
LOG2E = math.log2(math.e)
NEGATIVE = -1e30
F32 = jnp.float32
BF16 = jnp.bfloat16


def dot(a, b):
    return jnp.dot(a, b, preferred_element_type=F32)


def fold_rows(values, how):
    return how(values.reshape(values.shape[0] // 8, 8, values.shape[1]), axis=0)


def arrange_kernel(place, q_own, g_own, q_other, g_other, bias_q, q_s, qt_s, g_s, gt_s):
    core = place[0]
    for h in range(GROUP):
        cols = pl.ds(h * HEAD_DIM, HEAD_DIM)
        own_cols = pl.ds(pl.multiple_of((core * GROUP + h) * HEAD_DIM, HEAD_DIM), HEAD_DIM)
        bias_row = bias_q[:, own_cols].astype(F32)
        own_rows = pl.ds(h * CHUNK, TOK)
        other_rows = pl.ds(h * CHUNK + TOK, TOK)
        q_s[own_rows, :] = (q_own[:, own_cols].astype(F32) + bias_row).astype(BF16)
        q_s[other_rows, :] = (q_other[:, cols].astype(F32) + bias_row).astype(BF16)
        g_s[own_rows, :] = g_own[:, own_cols]
        g_s[other_rows, :] = g_other[:, cols]
    for h in range(GROUP):
        at = pl.ds(h * CHUNK, CHUNK)
        qt_s[:, at] = q_s[at, :].T
        gt_s[:, at] = g_s[at, :].T


def arrange(place, q_own, g_own, q_other, g_other, bias_q):
    vmem = pl.BlockSpec(memory_space=pltpu.VMEM)
    smem = pl.BlockSpec(memory_space=pltpu.SMEM)
    rows = jax.ShapeDtypeStruct((GROUP * CHUNK, HEAD_DIM), BF16)
    columns = jax.ShapeDtypeStruct((HEAD_DIM, GROUP * CHUNK), BF16)
    return pl.pallas_call(
        arrange_kernel,
        out_shape=[rows, columns, rows, columns],
        in_specs=[smem] + [vmem] * 5,
        out_specs=[vmem] * 4,
        compiler_params=pltpu.CompilerParams(vmem_limit_bytes=24 * 1024 * 1024),
        cost_estimate=pl.CostEstimate(flops=1 << 22, bytes_accessed=4 << 20, transcendentals=0),
    )(place, q_own, g_own, q_other, g_other, bias_q)


def attention_kernel(
    place, lengths, q_s, qt_s, g_s, gt_s, bias_v, kv,
    att_own, att_send, gq_own, gq_send, dkv, bias_out,
    v_s, s_s, p_s, d_s, mx_s, l_s, ot_s, dqt_s, rl_s, delta_s, mask_s, bv_s,
):
    core = place[0]
    chunk_id = place[1]
    first_token = chunk_id * CHUNK
    half_start = chunk_id - lax.rem(chunk_id, 8)

    def position(shape, dim):
        return lax.rem(lax.broadcasted_iota(jnp.int32, shape, dim) + core * TOK, CHUNK)

    token = first_token + position((1, CHUNK), 1)
    first_seen = jnp.zeros((1, CHUNK), jnp.int32)
    begin = jnp.int32(0)
    lowest = jnp.int32(0)
    for i in range(NDOC):
        first_seen = jnp.where(token >= begin, begin, first_seen)
        lowest = jnp.where(first_token >= begin, begin, lowest)
        begin = begin + lengths[0, i]
    low = lax.div(lowest, jnp.int32(CHUNK))

    mx_s[...] = jnp.full(mx_s.shape, NEGATIVE, F32)
    l_s[...] = jnp.zeros(l_s.shape, F32)
    ot_s[...] = jnp.zeros(ot_s.shape, F32)
    dqt_s[...] = jnp.zeros(dqt_s.shape, F32)
    bv_s[...] = jnp.zeros(bv_s.shape, F32)
    dkv[...] = jnp.zeros(dkv.shape, BF16)
    bias_v_row = bias_v[:, pl.ds(pl.multiple_of(core * HEAD_DIM, HEAD_DIM), HEAD_DIM)].astype(F32)

    def rows_of(c):
        return lax.rem(c, 8), pl.ds(jnp.where(c >= half_start, 0, 2), 2)

    def part_of(c, at):
        y, blocks = rows_of(c)
        return kv[y, blocks, :, pl.ds(at, HEAD_DIM)].reshape(CHUNK, HEAD_DIM)

    count = chunk_id + 1 - low
    odd = lax.rem(count, 2)

    def scores(c, part):
        keys = part_of(c, 0)
        v_s[c - low] = (part_of(c, HEAD_DIM).astype(F32) + bias_v_row).astype(BF16)
        key_index = c * CHUNK + position((CHUNK, CHUNK), 0)
        allowed = jnp.logical_and(key_index <= token, key_index >= first_seen)
        mask_s[part] = jnp.where(allowed, 0.0, NEGATIVE)
        for h in range(GROUP):
            at = pl.ds(h * CHUNK, CHUNK)
            raw = dot(keys, qt_s[:, at]) * (SCALE * LOG2E) + mask_s[part]
            s_s[c - low, :, at] = raw
            mx_s[:, at] = jnp.maximum(mx_s[:, at], fold_rows(raw, jnp.max))

    def weigh(c, part):
        values_t = v_s[c - low].T
        for h in range(GROUP):
            at = pl.ds(h * CHUNK, CHUNK)
            probs = jnp.exp2(s_s[c - low, :, at] - mx_s[0:1, at])
            s_s[c - low, :, at] = probs
            l_s[:, at] = l_s[:, at] + fold_rows(probs, jnp.sum)
            ot_s[:, at] = ot_s[:, at] + dot(values_t, probs.astype(BF16))

    def in_pairs(step):
        @pl.when(odd == 1)
        def _():
            step(low, 0)

        def pair(i, carry):
            step(low + odd + 2 * i, 0)
            step(low + odd + 2 * i + 1, 1)
            return carry

        lax.fori_loop(0, lax.div(count, 2), pair, 0)

    in_pairs(scores)
    mx_s[...] = jnp.broadcast_to(jnp.max(mx_s[...], axis=0, keepdims=True), mx_s.shape)
    in_pairs(weigh)

    for h in range(GROUP):
        at = pl.ds(h * CHUNK, CHUNK)
        cols = pl.ds(h * HEAD_DIM, HEAD_DIM)
        inverse = 1.0 / jnp.sum(l_s[:, at], axis=0, keepdims=True)
        rl_s[:, at] = jnp.broadcast_to(inverse, (8, CHUNK))
        out_t = (ot_s[:, at] * inverse).astype(BF16)
        delta = jnp.sum(out_t.astype(F32) * gt_s[:, at].astype(F32), axis=0, keepdims=True)
        delta_s[:, at] = jnp.broadcast_to(delta, (8, CHUNK))
        rows = out_t.T
        att_own[:, cols] = rows[:TOK]
        att_send[:, cols] = rows[TOK:]

    def slopes_of(c, part):
        values = v_s[c - low]
        for h in range(GROUP):
            at = pl.ds(h * CHUNK, CHUNK)
            dots = dot(values, gt_s[:, at])
            probs = s_s[c - low, :, at] * rl_s[0:1, at]
            p_s[part, :, at] = probs.astype(BF16)
            d_s[part, :, at] = (probs * (dots - delta_s[0:1, at])).astype(BF16)

    def gradients(c, part):
        dk = dot(d_s[part], q_s[...])
        dv = dot(p_s[part], g_s[...])
        keys_t = part_of(c, 0).T
        dqt_s[...] = dqt_s[...] + dot(keys_t, d_s[part])
        y, blocks = rows_of(c)
        dkv[y, blocks, :, :HEAD_DIM] = (dk * SCALE).astype(BF16).reshape(2, TOK, HEAD_DIM)
        dkv[y, blocks, :, HEAD_DIM:] = dv.astype(BF16).reshape(2, TOK, HEAD_DIM)
        bv_s[...] = bv_s[...] + fold_rows(dv, jnp.sum)

    @pl.when(odd == 0)
    def _():
        slopes_of(low, 0)
        gradients(low, 0)

    first = low + 1 - odd
    slopes_of(first, 0)

    def staggered(i, carry):
        c = first + 2 * i
        slopes_of(c + 1, 1)
        gradients(c, 0)
        slopes_of(c + 2, 0)
        gradients(c + 1, 1)
        return carry

    lax.fori_loop(0, lax.div(chunk_id - first, 2), staggered, 0)
    gradients(chunk_id, 0)

    for h in range(GROUP):
        cols = pl.ds(h * HEAD_DIM, HEAD_DIM)
        grad = (dqt_s[:, pl.ds(h * CHUNK, CHUNK)] * SCALE).T
        bias_out[h : h + 1, :] = jnp.sum(grad, axis=0, keepdims=True)
        rows = grad.astype(BF16)
        gq_own[:, cols] = rows[:TOK]
        gq_send[:, cols] = rows[TOK:]
    bias_out[GROUP : GROUP + 1, :] = jnp.sum(bv_s[...], axis=0, keepdims=True)


def attention(place, lengths, q_rows, q_cols, g_rows, g_cols, bias_v, kv):
    half = jax.ShapeDtypeStruct((TOK, GROUP * HEAD_DIM), BF16)
    vmem = pl.BlockSpec(memory_space=pltpu.VMEM)
    smem = pl.BlockSpec(memory_space=pltpu.SMEM)
    queries = GROUP * CHUNK
    stat = pltpu.VMEM((8, queries), F32)
    pairs = CHUNK * SLOTS * queries
    return pl.pallas_call(
        attention_kernel,
        out_shape=[half] * 4
        + [
            jax.ShapeDtypeStruct(kv.shape, BF16),
            jax.ShapeDtypeStruct((8, HEAD_DIM), F32),
        ],
        in_specs=[smem] * 2 + [vmem] * 6,
        out_specs=[vmem] * 6,
        scratch_shapes=[
            pltpu.VMEM((SLOTS, CHUNK, HEAD_DIM), BF16),
            pltpu.VMEM((SLOTS, CHUNK, queries), F32),
            pltpu.VMEM((2, CHUNK, queries), BF16),
            pltpu.VMEM((2, CHUNK, queries), BF16),
            stat,
            stat,
            pltpu.VMEM((HEAD_DIM, queries), F32),
            pltpu.VMEM((HEAD_DIM, queries), F32),
            stat,
            stat,
            pltpu.VMEM((2, CHUNK, CHUNK), F32),
            pltpu.VMEM((8, HEAD_DIM), F32),
        ],
        compiler_params=pltpu.CompilerParams(vmem_limit_bytes=58 * 1024 * 1024),
        cost_estimate=pl.CostEstimate(
            flops=12 * pairs * HEAD_DIM, bytes_accessed=8 << 20, transcendentals=pairs
        ),
    )(place, lengths, q_rows, q_cols, g_rows, g_cols, bias_v, kv)


SEQ = ("xlo", "y", "core")
SWAP = [(0, 1), (1, 0)]


def everyone(part, axes, count):
    spread = jnp.broadcast_to(part[None], (count,) + part.shape)
    return lax.all_to_all(spread, axes, split_axis=0, concat_axis=0, tiled=True)


def body(queries, keys, values, bias_query, bias_value, doc_lengths, grad_out):
    x = lax.axis_index("xlo")
    y = lax.axis_index("y")
    core = lax.axis_index("core")
    width = GROUP * HEAD_DIM
    low_core = core == 0

    def columns(array, which, size):
        return jnp.where(which == 0, array[:, :size], array[:, size:])

    def joined(mine, other, axis):
        return jnp.where(
            low_core,
            jnp.concatenate([mine, other], axis=axis),
            jnp.concatenate([other, mine], axis=axis),
        )

    def kv_head(which):
        return jnp.concatenate(
            [columns(keys, which, HEAD_DIM), columns(values, which, HEAD_DIM)], axis=1
        )

    kv_mine, kv_send = kv_head(core), kv_head(1 - core)
    low_mine = lax.ppermute(kv_mine, "xlo", [(0, 1)])
    low_other = lax.ppermute(kv_send, ("xlo", "core"), [(0, 3), (1, 2)])
    kv_other = lax.ppermute(kv_send, "core", SWAP)
    gathered = lax.all_gather(
        jnp.stack([kv_mine, kv_other, low_mine, low_other]), "y", axis=0, tiled=False
    )

    place = jnp.stack([core, x * 8 + y]).astype(jnp.int32)
    q_other = lax.ppermute(columns(queries, 1 - core, width), "core", SWAP)
    g_other = lax.ppermute(columns(grad_out, 1 - core, width), "core", SWAP)
    arranged = arrange(place, queries, grad_out, q_other, g_other, bias_query[None, :])
    att_own, att_send, gq_own, gq_send, dkv, bias_part = attention(
        place, doc_lengths, *arranged, bias_value[None, :], gathered
    )

    reduced = lax.psum_scatter(dkv, "y", scatter_dimension=0, tiled=False)

    att_other = lax.ppermute(att_send, "core", SWAP)
    gq_other = lax.ppermute(gq_send, "core", SWAP)
    attended = joined(att_own, att_other, 1)
    grad_queries = joined(gq_own, gq_other, 1)
    over_packs = jnp.sum(everyone(bias_part, ("z", "xhi", "xlo"), 32), axis=0)
    over_all = jnp.sum(everyone(over_packs, ("y", "core"), 16).reshape(8, 2, 8, HEAD_DIM), axis=0)
    grad_bias_query = over_all[:, :GROUP].reshape(HEADS * HEAD_DIM)
    grad_bias_value = over_all[:, GROUP].reshape(KV_HEADS * HEAD_DIM)
    reduced, attended, grad_queries, grad_bias_query, grad_bias_value = lax.optimization_barrier(
        (reduced, attended, grad_queries, grad_bias_query, grad_bias_value)
    )

    high_mine = lax.ppermute(reduced[2], "xlo", [(1, 0)])
    high_other = lax.ppermute(reduced[3], ("xlo", "core"), [(2, 1), (3, 0)])
    from_core = lax.ppermute(reduced[1], "core", SWAP)
    mine = (reduced[0].astype(F32) + high_mine.astype(F32)).astype(BF16)
    other = (from_core.astype(F32) + high_other.astype(F32)).astype(BF16)
    grad_keys = joined(mine[:, :HEAD_DIM], other[:, :HEAD_DIM], 1)
    grad_values = joined(mine[:, HEAD_DIM:], other[:, HEAD_DIM:], 1)
    return attended, grad_queries, grad_keys, grad_values, grad_bias_query, grad_bias_value


def solution(mesh):
    parts = Mesh(mesh.devices.reshape(8, 2, 2, 8, 2), ("z", "xhi", "xlo", "y", "core"))
    rows = P(("z", "xhi") + SEQ, None)
    in_specs = (rows, rows, rows, P(), P(), P(("z", "xhi"), None), rows)
    out_specs = (rows, rows, rows, rows, P(), P())
    return jax.shard_map(body, mesh=parts, in_specs=in_specs, out_specs=out_specs, check_vma=False)
```

time: 159 us -> 154 us (0.969)
  waiting for transfers between devices: 54.6 us -> 47.5 us
  local copies, waits for them, and re-layouts: 4.55 us -> 7.99 us
    all_gather x1, waiting for transfers between devices: 34.5 us -> 30 us  [body(): lax.all_gather(jnp.stack([kv_mine, kv_other, low_mine, low_other]), 'y',...]
    ppermute x3, waiting for transfers between devices: 4.62 us -> 1.49 us  [the longest x1 1.49 us: body(): high_other = lax.ppermute(reduced[3], ('xlo', 'core'), [(2, 1), (3, 0)])]
    unnamed x22 -> x28, local copies, waits for them, and re-layouts: 0.92 us -> 4.02 us
    select_n x4 -> x0, other arithmetic: 1.99 us -> none  [the longest x1 0.98 us: body(): half_sum = jnp.where(x == 0, low_sum, reduced[1])]
  transfers between devices with their start and end apart: 14 -> 14, of which waited for: 6 -> 6; matrix products, arithmetic and copies ran while one was open for 4% -> 4% of each run, Pallas kernels for 0% -> 1%
where the time goes in v3:
time: 154 us
  starting transfers between devices  69.8 us (45%)
  waiting for transfers between devices  47.5 us (31%)
  between operations  14.4 us (9%)
  local copies, waits for them, and re-layouts  7.99 us (5%)
  Pallas kernels  7.26 us (5%)
  other arithmetic  6.82 us (4%)
    all_to_all x2, starting transfers between devices, everyone(): return lax.all_to_all(spread, axes, split_axis=0, concat_axis=0, tiled=True)  35.8 us
    all_gather x1, waiting for transfers between devices, body(): lax.all_gather(jnp.stack([kv_mine, kv_other, low_mine, low_other]), 'y',...  30 us
    all_to_all x2, waiting for transfers between devices, everyone(): return lax.all_to_all(spread, axes, split_axis=0, concat_axis=0, tiled=True)  14.5 us
    ppermute x1, starting transfers between devices, body(): from_core = lax.ppermute(reduced[1], 'core', SWAP)  7.23 us
    pallas_call x1, Pallas kernels, attention(): pl.pallas_call(attention_kernel, out_shape=[half] * 4 + [jax.ShapeDtypeSt...  6.4 us
    ppermute x1, starting transfers between devices, body(): att_other = lax.ppermute(att_send, 'core', SWAP)  6.21 us
    ppermute x1, starting transfers between devices, body(): kv_other = lax.ppermute(kv_send, 'core', SWAP)  5.57 us
    unnamed x28, local copies, waits for them, and re-layouts  4.02 us
  transfers between devices with their start and end apart: 14, of which 6 were waited for; matrix products, arithmetic and copies ran while one was open for 4% of the time, Pallas kernels for 1%

profile of v3, /device:TPU:1, one launch (start us, length us, event | category | flops | bytes accessed | tf_op | source)
XLA Modules:
  0.0 153.7 jit_solution(1641104256689815892)
XLA Ops:
  7.2 0.0 copy-start.1
  7.2 0.0 copy-start
  7.2 0.0 copy-start.13
  7.2 0.0 copy-start.10
  7.2 0.0 all-gather.3.cloned.1.call-start
  7.3 0.9 broadcast_select_fusion.2
  8.2 3.9 %collective-permute-start.3 = (bf16[128,256]{1,0:T(8,128)(2,1)S(1)}, bf16[128,256]{1,0:T(8,128)(2,1)S(1)}, u32[]{:S(2)}, u32[]{:S(2)}) collective-permute-start(bf16[128,256]{1,0:T(8,128)(2,1)S(1)} %get-tuple-element.44), channel_id=1, source_target_pairs={{0,16},{1,17},{2,18},{3,19},{4,20},{5,21},{6,22},{7,23},{8,24},{9,... | collective-permute-start | bytes 196616 | tf_op jit(solution)/shard_map/ppermute | solution.py:275
  12.1 1.9 %collective-permute-start.4 = (bf16[128,256]{1,0:T(8,128)(2,1)S(1)}, bf16[128,256]{1,0:T(8,128)(2,1)S(1)}, u32[]{:S(2)}, u32[]{:S(2)}) collective-permute-start(bf16[128,256]{1,0:T(8,128)(2,1)S(1)} %pad_maximum_fusion.2), channel_id=1, source_target_pairs={{0,17},{1,16},{2,19},{3,18},{4,21},{5,20},{6,23},{7,22},{8,25},{9,... | collective-permute-start | bytes 196616 | tf_op jit(solution)/shard_map/ppermute | solution.py:276
  14.0 5.6 %collective-permute-start.2 = (bf16[128,256]{1,0:T(8,128)(2,1)S(1)}, bf16[128,256]{1,0:T(8,128)(2,1)S(1)}, u32[]{:S(2)}, u32[]{:S(2)}) collective-permute-start(bf16[128,256]{1,0:T(8,128)(2,1)S(1)} %pad_maximum_fusion.2), channel_id=1, source_target_pairs={{0,1},{1,0},{2,3},{3,2},{4,5},{5,4},{6,7},{7,6},{8,9},{9,8},{10,11... | collective-permute-start | bytes 196616 | tf_op jit(solution)/shard_map/ppermute | solution.py:277
  19.6 0.0 collective-permute-done.3
  19.6 0.0 collective-permute-done.4
  19.6 0.9 collective-permute-done.2
  20.5 0.7 pad_maximum_fusion
  21.2 0.0 all-gather.3.cloned.1.call-update
  21.2 0.0 reduce-scatter.2.cloned.1.call-start
  21.3 1.1 slice_select_fusion
  22.4 2.3 %collective-permute-start.1 = (bf16[128,896]{1,0:T(8,128)(2,1)S(1)}, bf16[128,896]{1,0:T(8,128)(2,1)S(1)}, u32[]{:S(2)}, u32[]{:S(2)}) collective-permute-start(bf16[128,896]{1,0:T(8,128)(2,1)S(1)} %slice_select_fusion), channel_id=1, source_target_pairs={{0,1},{1,0},{2,3},{3,2},{4,5},{5,4},{6,7},{7,6},{8,9},{9,8},{10,11... | collective-permute-start | bytes 688136 | tf_op jit(solution)/shard_map/ppermute | solution.py:284
  24.6 0.0 copy-done
  24.7 2.1 %collective-permute-start = (bf16[128,896]{1,0:T(8,128)(2,1)S(1)}, bf16[128,896]{1,0:T(8,128)(2,1)S(1)}, u32[]{:S(2)}, u32[]{:S(2)}) collective-permute-start(bf16[128,896]{1,0:T(8,128)(2,1)S(1)} %slice_select_fusion.1), channel_id=1, source_target_pairs={{0,1},{1,0},{2,3},{3,2},{4,5},{5,4},{6,7},{7,6},{8,9},{9,8},{10,11... | collective-permute-start | bytes 688136 | tf_op jit(solution)/shard_map/ppermute | solution.py:283
  26.8 0.0 copy-done.13
  26.8 0.6 broadcast_in_dim.9.bias_v
  27.4 0.0 copy-done.10
  27.4 0.1 pad_add_fusion.place
  27.4 0.0 collective-permute-done.1.g_other
  27.5 0.6 collective-permute-done.q_other
  28.1 0.0 copy-done.1
  28.1 0.9 shard_map.118
  28.9 0.0 copy-start.3
  29.0 0.8 copy-done.3
  29.7 0.8 copy-done.4
  30.5 0.8 copy-done.5
  31.3 0.8 copy-done.6
  32.1 30.0 %all-gather.3.cloned.1.call-done = bf16[32,128,256]{2,1,0:T(8,128)(2,1)} async-done(((bf16[4,128,256]{2,1,0:T(8,128)(2,1)}), bf16[32,128,256]{2,1,0:T(8,128)(2,1)}) %all-gather.3.cloned.1.call-update) | async-done | bytes 2097168 | tf_op jit(solution)/shard_map/all_gather | solution.py:278
  62.1 0.0 copy-done.2
  62.1 6.4 %shard_map.119 = (bf16[128,896]{1,0:T(8,128)(2,1)}, bf16[128,896]{1,0:T(8,128)(2,1)}, bf16[128,896]{1,0:T(8,128)(2,1)}, bf16[128,896]{1,0:T(8,128)(2,1)}, bf16[8...) custom-call(s32[2]{0:T(128)} %copy-done.2, s32[1,16]{1,0:T(1,128)} %lengths.1, bf16[1792,128]{1,0:T(8,128)(2,1)} %copy-done.3, ...), custom_call_target="tpu_custom_call" | custom-call | flops 9160359936 | bytes 8388608 | tf_op jit(solution)/shard_map/pallas_call | solution.py:213
  68.5 0.0 copy-start.11
  68.5 0.0 copy-start.8
  68.5 0.0 reduce-scatter.2.cloned.1.call-update
  68.5 0.9 copy-done.12
  69.4 6.2 %collective-permute-start.5 = (bf16[128,896]{1,0:T(8,128)(2,1)S(1)}, bf16[128,896]{1,0:T(8,128)(2,1)S(1)}, u32[]{:S(2)}, u32[]{:S(2)}) collective-permute-start(bf16[128,896]{1,0:T(8,128)(2,1)S(1)} %copy-done.12), channel_id=1, source_target_pairs={{0,1},{1,0},{2,3},{3,2},{4,5},{5,4},{6,7},{7,6},{8,9},{9,8},{10,11... | collective-permute-start | bytes 688136 | tf_op jit(solution)/shard_map/ppermute | solution.py:292
  75.6 0.7 broadcast_in_dim.20
  76.3 22.0 %all-to-all-start = ((f32[32,8,128]{2,1,0:T(8,128)}), f32[32,8,128]{2,1,0:T(8,128)S(1)}, u32[]{:S(2)}, u32[]{:S(2)}) async-start(f32[32,8,128]{2,1,0:T(8,128)} %broadcast_in_dim.20), calls=%async_computation.1 | async-start | bytes 262144 | tf_op jit(solution)/shard_map/all_to_all | solution.py:249
  98.3 2.2 %collective-permute-start.6 = (bf16[128,896]{1,0:T(8,128)(2,1)S(1)}, bf16[128,896]{1,0:T(8,128)(2,1)S(1)}, u32[]{:S(2)}, u32[]{:S(2)}) collective-permute-start(bf16[128,896]{1,0:T(8,128)(2,1)S(1)} %copy-done.11), channel_id=1, source_target_pairs={{0,1},{1,0},{2,3},{3,2},{4,5},{5,4},{6,7},{7,6},{8,9},{9,8},{10,11... | collective-permute-start | bytes 688136 | tf_op jit(solution)/shard_map/ppermute | solution.py:293
  100.5 0.0 collective-permute-done.5
  100.5 0.9 maximum_select_fusion
  101.4 6.8 %all-to-all-done = f32[32,8,128]{2,1,0:T(8,128)S(1)} async-done(((f32[32,8,128]{2,1,0:T(8,128)}), f32[32,8,128]{2,1,0:T(8,128)S(1)}, u32[]{:S(2)}, u32[]{:S(2)}) %all-to-all-start) | async-done | bytes 131104 | tf_op jit(solution)/shard_map/all_to_all | solution.py:249
  108.3 0.6 broadcast_in_dim.21
  108.9 13.8 %all-to-all-start.1 = ((f32[16,8,128]{2,1,0:T(8,128)}), f32[16,8,128]{2,1,0:T(8,128)S(1)}, u32[]{:S(2)}, u32[]{:S(2)}) async-start(f32[16,8,128]{2,1,0:T(8,128)} %broadcast_in_dim.21), calls=%async_computation.2 | async-start | bytes 131072 | tf_op jit(solution)/shard_map/all_to_all | solution.py:249
  122.7 0.0 collective-permute-done.6
  122.7 0.9 maximum_select_fusion.1
  123.6 7.6 %all-to-all-done.1 = f32[16,8,128]{2,1,0:T(8,128)S(1)} async-done(((f32[16,8,128]{2,1,0:T(8,128)}), f32[16,8,128]{2,1,0:T(8,128)S(1)}, u32[]{:S(2)}, u32[]{:S(2)}) %all-to-all-start.1) | async-done | bytes 65568 | tf_op jit(solution)/shard_map/all_to_all | solution.py:249
  131.2 0.6 slice.77
  131.8 0.6 reshape.23
  132.4 0.0 reduce-scatter.2.cloned.1.call-done
  132.4 0.9 slice_bitcast_fusion.2
  133.3 1.3 collective-permute-start.7
  134.6 1.3 collective-permute-start.9
  135.9 7.2 %collective-permute-start.8 = (bf16[128,256]{1,0:T(8,128)(2,1)S(1)}, bf16[128,256]{1,0:T(8,128)(2,1)S(1)}, u32[]{:S(2)}, u32[]{:S(2)}) collective-permute-start(bf16[128,256]{1,0:T(8,128)(2,1)S(1)} %get-tuple-element.38), channel_id=1, source_target_pairs={{0,1},{1,0},{2,3},{3,2},{4,5},{5,4},{6,7},{7,6},{8,9},{9,8},{10,11... | collective-permute-start | bytes 196616 | tf_op jit(solution)/shard_map/ppermute | solution.py:306
  143.2 0.0 collective-permute-done.7
  143.2 0.9 fusion
  144.1 1.5 collective-permute-done.9
  145.6 0.0 collective-permute-done.8
  145.6 0.6 maximum_select_fusion.3
  146.2 0.6 maximum_select_fusion.2
  (20 shorter events, 0.2 us)
Async XLA Ops:
  7.2 20.9 %copy-start.1 = (bf16[128,1792]{1,0:T(8,128)(2,1)S(1)}, bf16[128,1792]{1,0:T(8,128)(2,1)}, u32[]{:S(2)}) copy-start(bf16[128,1792]{1,0:T(8,128)(2,1)} %g_own.1) | copy-start | bytes 1376260
  7.2 17.5 %copy-start = (bf16[128,1792]{1,0:T(8,128)(2,1)S(1)}, bf16[128,1792]{1,0:T(8,128)(2,1)}, u32[]{:S(2)}) copy-start(bf16[128,1792]{1,0:T(8,128)(2,1)} %q_own.1) | copy-start | bytes 1376260
  7.2 19.6 %copy-start.13 = (bf16[256]{0:T(256)(128)(2,1)S(1)}, bf16[256]{0:T(256)(128)(2,1)}, u32[]{:S(2)}) copy-start(bf16[256]{0:T(256)(128)(2,1)} %param.11) | copy-start | bytes 1540
  7.2 20.2 %copy-start.10 = (bf16[1792]{0:T(1024)(128)(2,1)S(1)}, bf16[1792]{0:T(1024)(128)(2,1)}, u32[]{:S(2)}) copy-start(bf16[1792]{0:T(1024)(128)(2,1)} %param.10) | copy-start | bytes 10756
  7.2 54.9 %all-gather.3.cloned.1.call-start = ((), (), s32[]{:S(2)}) async-start(), calls=%async_computation.4 | async-start | bytes 2359296 | tf_op jit(solution)/shard_map/all_gather | solution.py:278
  8.2 11.4 %collective-permute-start.3 = (bf16[128,256]{1,0:T(8,128)(2,1)S(1)}, bf16[128,256]{1,0:T(8,128)(2,1)S(1)}, u32[]{:S(2)}, u32[]{:S(2)}) collective-permute-start(bf16[128,256]{1,0:T(8,128)(2,1)S(1)} %get-tuple-element.44), channel_id=1, source_target_pairs={{0,16},{1,17},{2,18},{3,19},{4,20},{5,21},{6,22},{7,23},{8,24},{9,... | collective-permute-start | bytes 196616 | tf_op jit(solution)/shard_map/ppermute | solution.py:275
  12.1 7.5 %collective-permute-start.4 = (bf16[128,256]{1,0:T(8,128)(2,1)S(1)}, bf16[128,256]{1,0:T(8,128)(2,1)S(1)}, u32[]{:S(2)}, u32[]{:S(2)}) collective-permute-start(bf16[128,256]{1,0:T(8,128)(2,1)S(1)} %pad_maximum_fusion.2), channel_id=1, source_target_pairs={{0,17},{1,16},{2,19},{3,18},{4,21},{5,20},{6,23},{7,22},{8,25},{9,... | collective-permute-start | bytes 196616 | tf_op jit(solution)/shard_map/ppermute | solution.py:276
  14.0 6.5 %collective-permute-start.2 = (bf16[128,256]{1,0:T(8,128)(2,1)S(1)}, bf16[128,256]{1,0:T(8,128)(2,1)S(1)}, u32[]{:S(2)}, u32[]{:S(2)}) collective-permute-start(bf16[128,256]{1,0:T(8,128)(2,1)S(1)} %pad_maximum_fusion.2), channel_id=1, source_target_pairs={{0,1},{1,0},{2,3},{3,2},{4,5},{5,4},{6,7},{7,6},{8,9},{9,8},{10,11... | collective-permute-start | bytes 196616 | tf_op jit(solution)/shard_map/ppermute | solution.py:277
  21.2 111.2 %reduce-scatter.2.cloned.1.call-start = ((), (), s32[]{:S(2)}) async-start(), calls=%async_computation.3 | async-start | bytes 2359296 | tf_op jit(solution)/shard_map/reduce_scatter | solution.py:290
  22.4 5.1 %collective-permute-start.1 = (bf16[128,896]{1,0:T(8,128)(2,1)S(1)}, bf16[128,896]{1,0:T(8,128)(2,1)S(1)}, u32[]{:S(2)}, u32[]{:S(2)}) collective-permute-start(bf16[128,896]{1,0:T(8,128)(2,1)S(1)} %slice_select_fusion), channel_id=1, source_target_pairs={{0,1},{1,0},{2,3},{3,2},{4,5},{5,4},{6,7},{7,6},{8,9},{9,8},{10,11... | collective-permute-start | bytes 688136 | tf_op jit(solution)/shard_map/ppermute | solution.py:284
  24.7 3.4 %collective-permute-start = (bf16[128,896]{1,0:T(8,128)(2,1)S(1)}, bf16[128,896]{1,0:T(8,128)(2,1)S(1)}, u32[]{:S(2)}, u32[]{:S(2)}) collective-permute-start(bf16[128,896]{1,0:T(8,128)(2,1)S(1)} %slice_select_fusion.1), channel_id=1, source_target_pairs={{0,1},{1,0},{2,3},{3,2},{4,5},{5,4},{6,7},{7,6},{8,9},{9,8},{10,11... | collective-permute-start | bytes 688136 | tf_op jit(solution)/shard_map/ppermute | solution.py:283
  27.4 34.6 %copy-start.2 = (s32[2]{0:T(128)}, s32[2]{0:T(128)S(1)}, u32[]{:S(2)}) copy-start(s32[2]{0:T(128)S(1)} %pad_add_fusion.place) | copy-start | bytes 28
  28.9 0.8 copy-start.3
  29.7 0.8 copy-start.4
  30.5 0.8 copy-start.5
  31.3 0.8 copy-start.6
  68.5 0.9 copy-start.12
  68.5 7.2 %copy-start.9 = (f32[8,128]{1,0:T(8,128)S(1)}, f32[8,128]{1,0:T(8,128)}, u32[]{:S(2)}) copy-start(f32[8,128]{1,0:T(8,128)} %get-tuple-element.30) | copy-start | bytes 12292
  68.5 29.8 %copy-start.11 = (bf16[128,896]{1,0:T(8,128)(2,1)S(1)}, bf16[128,896]{1,0:T(8,128)(2,1)}, u32[]{:S(2)}) copy-start(bf16[128,896]{1,0:T(8,128)(2,1)} %get-tuple-element.29) | copy-start | bytes 688132
  68.5 32.0 %copy-start.8 = (bf16[128,896]{1,0:T(8,128)(2,1)S(1)}, bf16[128,896]{1,0:T(8,128)(2,1)}, u32[]{:S(2)}) copy-start(bf16[128,896]{1,0:T(8,128)(2,1)} %get-tuple-element.26) | copy-start | bytes 688132
  68.5 54.2 %copy-start.7 = (bf16[128,896]{1,0:T(8,128)(2,1)S(1)}, bf16[128,896]{1,0:T(8,128)(2,1)}, u32[]{:S(2)}) copy-start(bf16[128,896]{1,0:T(8,128)(2,1)} %get-tuple-element.28) | copy-start | bytes 688132
  69.4 31.1 %collective-permute-start.5 = (bf16[128,896]{1,0:T(8,128)(2,1)S(1)}, bf16[128,896]{1,0:T(8,128)(2,1)S(1)}, u32[]{:S(2)}, u32[]{:S(2)}) collective-permute-start(bf16[128,896]{1,0:T(8,128)(2,1)S(1)} %copy-done.12), channel_id=1, source_target_pairs={{0,1},{1,0},{2,3},{3,2},{4,5},{5,4},{6,7},{7,6},{8,9},{9,8},{10,11... | collective-permute-start | bytes 688136 | tf_op jit(solution)/shard_map/ppermute | solution.py:292
  76.3 31.9 %all-to-all-start = ((f32[32,8,128]{2,1,0:T(8,128)}), f32[32,8,128]{2,1,0:T(8,128)S(1)}, u32[]{:S(2)}, u32[]{:S(2)}) async-start(f32[32,8,128]{2,1,0:T(8,128)} %broadcast_in_dim.20), calls=%async_computation.1 | async-start | bytes 262144 | tf_op jit(solution)/shard_map/all_to_all | solution.py:249
  98.3 24.4 %collective-permute-start.6 = (bf16[128,896]{1,0:T(8,128)(2,1)S(1)}, bf16[128,896]{1,0:T(8,128)(2,1)S(1)}, u32[]{:S(2)}, u32[]{:S(2)}) collective-permute-start(bf16[128,896]{1,0:T(8,128)(2,1)S(1)} %copy-done.11), channel_id=1, source_target_pairs={{0,1},{1,0},{2,3},{3,2},{4,5},{5,4},{6,7},{7,6},{8,9},{9,8},{10,11... | collective-permute-start | bytes 688136 | tf_op jit(solution)/shard_map/ppermute | solution.py:293
  108.9 22.3 %all-to-all-start.1 = ((f32[16,8,128]{2,1,0:T(8,128)}), f32[16,8,128]{2,1,0:T(8,128)S(1)}, u32[]{:S(2)}, u32[]{:S(2)}) async-start(f32[16,8,128]{2,1,0:T(8,128)} %broadcast_in_dim.21), calls=%async_computation.2 | async-start | bytes 131072 | tf_op jit(solution)/shard_map/all_to_all | solution.py:249
  133.3 9.8 %collective-permute-start.7 = (bf16[128,256]{1,0:T(8,128)(2,1)S(1)}, bf16[128,256]{1,0:T(8,128)(2,1)S(1)}, u32[]{:S(2)}, u32[]{:S(2)}) collective-permute-start(bf16[128,256]{1,0:T(8,128)(2,1)S(1)} %get-tuple-element.36), channel_id=1, source_target_pairs={{16,0},{17,1},{18,2},{19,3},{20,4},{21,5},{22,6},{23,7},{24,8},{25... | collective-permute-start | bytes 196616 | tf_op jit(solution)/shard_map/ppermute | solution.py:304
  134.6 10.9 %collective-permute-start.9 = (bf16[128,256]{1,0:T(8,128)(2,1)S(1)}, bf16[128,256]{1,0:T(8,128)(2,1)S(1)}, u32[]{:S(2)}, u32[]{:S(2)}) collective-permute-start(bf16[128,256]{1,0:T(8,128)(2,1)S(1)} %get-tuple-element.37), channel_id=1, source_target_pairs={{16,1},{17,0},{18,3},{19,2},{20,5},{21,4},{22,7},{23,6},{24,9},{25... | collective-permute-start | bytes 196616 | tf_op jit(solution)/shard_map/ppermute | solution.py:305
  135.9 9.6 %collective-permute-start.8 = (bf16[128,256]{1,0:T(8,128)(2,1)S(1)}, bf16[128,256]{1,0:T(8,128)(2,1)S(1)}, u32[]{:S(2)}, u32[]{:S(2)}) collective-permute-start(bf16[128,256]{1,0:T(8,128)(2,1)S(1)} %get-tuple-element.38), channel_id=1, source_target_pairs={{0,1},{1,0},{2,3},{3,2},{4,5},{5,4},{6,7},{7,6},{8,9},{9,8},{10,11... | collective-permute-start | bytes 196616 | tf_op jit(solution)/shard_map/ppermute | solution.py:306
Sparse Core Ops, SparseCore 0:
  21.4 40.6 all-gather.2
  68.7 63.7 reduce-scatter.1

commit v4 on v3

v4 whole, which is shorter than its diff:
```python
import functools
import math

import jax
import jax.numpy as jnp
from jax import lax
from jax.experimental import pallas as pl
from jax.experimental.pallas import tpu as pltpu
from jax.sharding import Mesh, PartitionSpec as P

HEADS = 14
KV_HEADS = 2
HEAD_DIM = 128
GROUP = HEADS // KV_HEADS
TOK = 128
CHUNK = 256
LONGEST = 3072
SLOTS = LONGEST // CHUNK + 1
NDOC = 16
SCALE = 1.0 / math.sqrt(HEAD_DIM)
LOG2E = math.log2(math.e)
NEGATIVE = -1e30
F32 = jnp.float32
BF16 = jnp.bfloat16


def dot(a, b):
    return jnp.dot(a, b, preferred_element_type=F32)


def fold_rows(values, how):
    return how(values.reshape(values.shape[0] // 8, 8, values.shape[1]), axis=0)


def arrange_kernel(place, first, second, bias_q, q_s, qt_s, g_s, gt_s):
    head = place[0]
    width = GROUP * HEAD_DIM
    for h in range(GROUP):
        at = h * HEAD_DIM
        bias_row = bias_q[:, pl.ds(pl.multiple_of(head * width + at, HEAD_DIM), HEAD_DIM)].astype(F32)
        for part, rows in enumerate((first, second)):
            to = pl.ds(h * CHUNK + part * TOK, TOK)
            q_s[to, :] = (rows[:, pl.ds(at, HEAD_DIM)].astype(F32) + bias_row).astype(BF16)
            g_s[to, :] = rows[:, pl.ds(width + at, HEAD_DIM)]
    for h in range(GROUP):
        at = pl.ds(h * CHUNK, CHUNK)
        qt_s[:, at] = q_s[at, :].T
        gt_s[:, at] = g_s[at, :].T


def arrange(place, first, second, bias_q):
    vmem = pl.BlockSpec(memory_space=pltpu.VMEM)
    smem = pl.BlockSpec(memory_space=pltpu.SMEM)
    rows = jax.ShapeDtypeStruct((GROUP * CHUNK, HEAD_DIM), BF16)
    columns = jax.ShapeDtypeStruct((HEAD_DIM, GROUP * CHUNK), BF16)
    return pl.pallas_call(
        arrange_kernel,
        out_shape=[rows, columns, rows, columns],
        in_specs=[smem] + [vmem] * 3,
        out_specs=[vmem] * 4,
        compiler_params=pltpu.CompilerParams(vmem_limit_bytes=24 * 1024 * 1024),
        cost_estimate=pl.CostEstimate(flops=1 << 22, bytes_accessed=4 << 20, transcendentals=0),
    )(place, first, second, bias_q)


def attention_kernel(
    place, lengths, q_s, qt_s, g_s, gt_s, bias_v, kv_half, kv_low,
    first, second, dkv_half, dkv_low, bias_out,
    v_s, s_s, p_s, d_s, mx_s, l_s, ot_s, dqt_s, rl_s, delta_s, mask_s, bv_s,
):
    head = place[0]
    chunk_id = place[1]
    first_token = chunk_id * CHUNK
    half_start = chunk_id - lax.rem(chunk_id, 8)

    def position(shape, dim):
        return lax.rem(lax.broadcasted_iota(jnp.int32, shape, dim) + head * TOK, CHUNK)

    token = first_token + position((1, CHUNK), 1)
    first_seen = jnp.zeros((1, CHUNK), jnp.int32)
    begin = jnp.int32(0)
    lowest = jnp.int32(0)
    for i in range(NDOC):
        first_seen = jnp.where(token >= begin, begin, first_seen)
        lowest = jnp.where(first_token >= begin, begin, lowest)
        begin = begin + lengths[0, i]
    low = lax.div(lowest, jnp.int32(CHUNK))

    mx_s[...] = jnp.full(mx_s.shape, NEGATIVE, F32)
    l_s[...] = jnp.zeros(l_s.shape, F32)
    ot_s[...] = jnp.zeros(ot_s.shape, F32)
    dqt_s[...] = jnp.zeros(dqt_s.shape, F32)
    bv_s[...] = jnp.zeros(bv_s.shape, F32)
    dkv_half[...] = jnp.zeros(dkv_half.shape, BF16)
    dkv_low[...] = jnp.zeros(dkv_low.shape, BF16)
    bias_v_row = bias_v[:, pl.ds(pl.multiple_of(head * HEAD_DIM, HEAD_DIM), HEAD_DIM)].astype(F32)

    def part_of(c, at):
        y, cols = lax.rem(c, 8), pl.ds(at, HEAD_DIM)
        rows = jnp.where(c >= half_start, kv_half[y, :, :, cols], kv_low[y, :, :, cols])
        return rows.reshape(CHUNK, HEAD_DIM)

    count = chunk_id + 1 - low
    odd = lax.rem(count, 2)

    def scores(c, part):
        keys = part_of(c, 0)
        v_s[c - low] = (part_of(c, HEAD_DIM).astype(F32) + bias_v_row).astype(BF16)
        key_index = c * CHUNK + position((CHUNK, CHUNK), 0)
        allowed = jnp.logical_and(key_index <= token, key_index >= first_seen)
        mask_s[part] = jnp.where(allowed, 0.0, NEGATIVE)
        for h in range(GROUP):
            at = pl.ds(h * CHUNK, CHUNK)
            raw = dot(keys, qt_s[:, at]) * (SCALE * LOG2E) + mask_s[part]
            s_s[c - low, :, at] = raw
            mx_s[:, at] = jnp.maximum(mx_s[:, at], fold_rows(raw, jnp.max))

    def weigh(c, part):
        values_t = v_s[c - low].T
        for h in range(GROUP):
            at = pl.ds(h * CHUNK, CHUNK)
            probs = jnp.exp2(s_s[c - low, :, at] - mx_s[0:1, at])
            s_s[c - low, :, at] = probs
            l_s[:, at] = l_s[:, at] + fold_rows(probs, jnp.sum)
            ot_s[:, at] = ot_s[:, at] + dot(values_t, probs.astype(BF16))

    def in_pairs(step):
        @pl.when(odd == 1)
        def _():
            step(low, 0)

        def pair(i, carry):
            step(low + odd + 2 * i, 0)
            step(low + odd + 2 * i + 1, 1)
            return carry

        lax.fori_loop(0, lax.div(count, 2), pair, 0)

    in_pairs(scores)
    mx_s[...] = jnp.broadcast_to(jnp.max(mx_s[...], axis=0, keepdims=True), mx_s.shape)
    in_pairs(weigh)

    for h in range(GROUP):
        at = pl.ds(h * CHUNK, CHUNK)
        inverse = 1.0 / jnp.sum(l_s[:, at], axis=0, keepdims=True)
        rl_s[:, at] = jnp.broadcast_to(inverse, (8, CHUNK))
        out = (ot_s[:, at] * inverse).astype(BF16)
        cols = pl.ds(h * HEAD_DIM, HEAD_DIM)
        rows = out.T
        first[:, cols] = rows[:TOK]
        second[:, cols] = rows[TOK:]
        delta = jnp.sum(out.astype(F32) * gt_s[:, at].astype(F32), axis=0, keepdims=True)
        delta_s[:, at] = jnp.broadcast_to(delta, (8, CHUNK))

    def slopes_of(c, part):
        values = v_s[c - low]
        for h in range(GROUP):
            at = pl.ds(h * CHUNK, CHUNK)
            dots = dot(values, gt_s[:, at])
            probs = s_s[c - low, :, at] * rl_s[0:1, at]
            p_s[part, :, at] = probs.astype(BF16)
            d_s[part, :, at] = (probs * (dots - delta_s[0:1, at])).astype(BF16)

    def gradients(c, part):
        dk = dot(d_s[part], q_s[...])
        dv = dot(p_s[part], g_s[...])
        keys_t = part_of(c, 0).T
        dqt_s[...] = dqt_s[...] + dot(keys_t, d_s[part])
        bv_s[...] = bv_s[...] + fold_rows(dv, jnp.sum)
        y = lax.rem(c, 8)
        dk = (dk * SCALE).astype(BF16).reshape(2, TOK, HEAD_DIM)
        dv = dv.astype(BF16).reshape(2, TOK, HEAD_DIM)

        @pl.when(c >= half_start)
        def _():
            dkv_half[y, :, :, :HEAD_DIM] = dk
            dkv_half[y, :, :, HEAD_DIM:] = dv

        @pl.when(c < half_start)
        def _():
            dkv_low[y, :, :, :HEAD_DIM] = dk
            dkv_low[y, :, :, HEAD_DIM:] = dv

    @pl.when(odd == 0)
    def _():
        slopes_of(low, 0)
        gradients(low, 0)

    start = low + 1 - odd
    slopes_of(start, 0)

    def staggered(i, carry):
        c = start + 2 * i
        slopes_of(c + 1, 1)
        gradients(c, 0)
        slopes_of(c + 2, 0)
        gradients(c + 1, 1)
        return carry

    lax.fori_loop(0, lax.div(chunk_id - start, 2), staggered, 0)
    gradients(chunk_id, 0)

    for h in range(GROUP):
        grad = (dqt_s[:, pl.ds(h * CHUNK, CHUNK)] * SCALE).T
        bias_out[h : h + 1, :] = jnp.sum(grad, axis=0, keepdims=True)
        rows = grad.astype(BF16)
        cols = pl.ds((GROUP + h) * HEAD_DIM, HEAD_DIM)
        first[:, cols] = rows[:TOK]
        second[:, cols] = rows[TOK:]
    bias_out[GROUP : GROUP + 1, :] = jnp.sum(bv_s[...], axis=0, keepdims=True)


def attention(place, lengths, q_rows, q_cols, g_rows, g_cols, bias_v, kv_half, kv_low):
    vmem = pl.BlockSpec(memory_space=pltpu.VMEM)
    smem = pl.BlockSpec(memory_space=pltpu.SMEM)
    queries = GROUP * CHUNK
    stat = pltpu.VMEM((8, queries), F32)
    pairs = CHUNK * SLOTS * queries
    return pl.pallas_call(
        attention_kernel,
        out_shape=[
            jax.ShapeDtypeStruct((TOK, 2 * GROUP * HEAD_DIM), BF16),
            jax.ShapeDtypeStruct((TOK, 2 * GROUP * HEAD_DIM), BF16),
            jax.ShapeDtypeStruct(kv_half.shape, BF16),
            jax.ShapeDtypeStruct(kv_low.shape, BF16),
            jax.ShapeDtypeStruct((8, HEAD_DIM), F32),
        ],
        in_specs=[smem] * 2 + [vmem] * 7,
        out_specs=[vmem] * 5,
        scratch_shapes=[
            pltpu.VMEM((SLOTS, CHUNK, HEAD_DIM), BF16),
            pltpu.VMEM((SLOTS, CHUNK, queries), F32),
            pltpu.VMEM((2, CHUNK, queries), BF16),
            pltpu.VMEM((2, CHUNK, queries), BF16),
            stat,
            stat,
            pltpu.VMEM((HEAD_DIM, queries), F32),
            pltpu.VMEM((HEAD_DIM, queries), F32),
            stat,
            stat,
            pltpu.VMEM((2, CHUNK, CHUNK), F32),
            pltpu.VMEM((8, HEAD_DIM), F32),
        ],
        compiler_params=pltpu.CompilerParams(vmem_limit_bytes=39 * 1024 * 1024),
        cost_estimate=pl.CostEstimate(
            flops=12 * pairs * HEAD_DIM, bytes_accessed=8 << 20, transcendentals=pairs
        ),
    )(place, lengths, q_rows, q_cols, g_rows, g_cols, bias_v, kv_half, kv_low)


def merge_kernel(half, upper, bias_own, bias_other, out):
    sums = bias_own[...] + bias_other[...]
    high = sums.astype(BF16)
    rows = jnp.concatenate([high, (sums - high.astype(F32)).astype(BF16)], axis=1)
    rows = jnp.concatenate([rows, jnp.zeros_like(rows)], axis=0)
    for y in range(8):
        for part in range(2):
            total = half[y, part].astype(F32) + upper[y, part].astype(F32)
            out[y, part * TOK : (part + 1) * TOK, :] = total.astype(BF16)
        out[y, CHUNK:, :] = rows


def merge(half, upper, bias_own, bias_other):
    vmem = pl.BlockSpec(memory_space=pltpu.VMEM)
    return pl.pallas_call(
        merge_kernel,
        out_shape=jax.ShapeDtypeStruct((8, CHUNK + 16, 2 * HEAD_DIM), BF16),
        in_specs=[vmem] * 4,
        out_specs=vmem,
        compiler_params=pltpu.CompilerParams(vmem_limit_bytes=12 * 1024 * 1024),
        cost_estimate=pl.CostEstimate(flops=1 << 20, bytes_accessed=3 << 20, transcendentals=0),
    )(half, upper, bias_own, bias_other)


def reduce_kernel(got, first, second, bias_sum):
    for part, out in enumerate((first, second)):
        rows = pl.ds(part * TOK, TOK)
        total = got[0, rows, :].astype(F32)
        for y in range(1, 8):
            total = total + got[y, rows, :].astype(F32)
        out[...] = total.astype(BF16)
    total = got[0, CHUNK:, :].astype(F32)
    for y in range(1, 8):
        total = total + got[y, CHUNK:, :].astype(F32)
    bias_sum[...] = total[:8, :HEAD_DIM] + total[:8, HEAD_DIM:]


def reduce(got):
    vmem = pl.BlockSpec(memory_space=pltpu.VMEM)
    rows = jax.ShapeDtypeStruct((TOK, 2 * HEAD_DIM), BF16)
    return pl.pallas_call(
        reduce_kernel,
        out_shape=[rows] * 2 + [jax.ShapeDtypeStruct((8, HEAD_DIM), F32)],
        in_specs=[vmem],
        out_specs=[vmem] * 3,
        compiler_params=pltpu.CompilerParams(vmem_limit_bytes=12 * 1024 * 1024),
        cost_estimate=pl.CostEstimate(flops=1 << 20, bytes_accessed=1 << 20, transcendentals=0),
    )(got)


def combine_kernel(place, mine, other, gk, gv):
    core = place[2]
    own_cols = pl.ds(pl.multiple_of(core * HEAD_DIM, HEAD_DIM), HEAD_DIM)
    other_cols = pl.ds(pl.multiple_of((1 - core) * HEAD_DIM, HEAD_DIM), HEAD_DIM)
    gk[:, own_cols] = mine[:, :HEAD_DIM]
    gk[:, other_cols] = other[:, :HEAD_DIM]
    gv[:, own_cols] = mine[:, HEAD_DIM:]
    gv[:, other_cols] = other[:, HEAD_DIM:]


def combine(place, mine, other):
    rows = jax.ShapeDtypeStruct((TOK, KV_HEADS * HEAD_DIM), BF16)
    vmem = pl.BlockSpec(memory_space=pltpu.VMEM)
    smem = pl.BlockSpec(memory_space=pltpu.SMEM)
    return pl.pallas_call(
        combine_kernel,
        out_shape=[rows] * 2,
        in_specs=[smem] + [vmem] * 2,
        out_specs=[vmem] * 2,
        compiler_params=pltpu.CompilerParams(vmem_limit_bytes=8 * 1024 * 1024),
        cost_estimate=pl.CostEstimate(flops=1 << 17, bytes_accessed=1 << 19, transcendentals=0),
    )(place, mine, other)


SEQ = ("xlo", "y", "core")

QUAD = ("xlo", "core")
FIRST = [(0, 0), (1, 2), (2, 1), (3, 3)]
SECOND = [(0, 2), (1, 0), (2, 3), (3, 1)]
SECOND_BACK = [(b, a) for a, b in SECOND]


def everyone(part, axes, count):
    spread = jnp.broadcast_to(part[None], (count,) + part.shape)
    return lax.all_to_all(spread, axes, split_axis=0, concat_axis=0, tiled=True)


def body(queries, keys, values, bias_query, bias_value, doc_lengths, grad_out):
    x = lax.axis_index("xlo")
    y = lax.axis_index("y")
    core = lax.axis_index("core")
    width = GROUP * HEAD_DIM

    def columns(array, which, size):
        return jnp.where(which == 0, array[:, :size], array[:, size:])

    def joined(mine, other):
        return jnp.where(
            core == 0,
            jnp.concatenate([mine, other], axis=1),
            jnp.concatenate([other, mine], axis=1),
        )

    def head_of(first, second, which, size):
        return jnp.concatenate([columns(first, which, size), columns(second, which, size)], axis=1)

    kv_first = lax.ppermute(head_of(keys, values, core, HEAD_DIM), QUAD, FIRST)
    kv_second = lax.ppermute(head_of(keys, values, 1 - core, HEAD_DIM), QUAD, SECOND)
    kv_half = everyone(jnp.stack([kv_first, kv_second]), "y", 8)
    place = jnp.stack([x, core * 8 + y, core]).astype(jnp.int32)
    rows_first = lax.ppermute(head_of(queries, grad_out, core, width), QUAD, FIRST)
    rows_second = lax.ppermute(head_of(queries, grad_out, 1 - core, width), QUAD, SECOND)
    arranged = arrange(place, rows_first, rows_second, bias_query[None, :])
    kv_half, *arranged = lax.optimization_barrier((kv_half, *arranged))
    kv_low = lax.ppermute(kv_half, "core", [(0, 1)])
    back_first, back_second, dkv_half, dkv_low, bias_part = attention(
        place, doc_lengths, *arranged, bias_value[None, :], kv_half, kv_low
    )

    from_upper = lax.ppermute(dkv_low, "core", [(1, 0)])
    bias_other = lax.ppermute(bias_part, "core", [(0, 1), (1, 0)])
    terms = merge(dkv_half, from_upper, bias_part, bias_other)
    got = lax.all_to_all(terms, "y", split_axis=0, concat_axis=0, tiled=True)

    back_first = lax.ppermute(back_first, QUAD, FIRST)
    back_second = lax.ppermute(back_second, QUAD, SECOND_BACK)
    attended = joined(back_first[:, :width], back_second[:, :width])
    grad_queries = joined(back_first[:, width:], back_second[:, width:])
    got, attended, grad_queries = lax.optimization_barrier((got, attended, grad_queries))

    sum_first, sum_second, bias_sum = reduce(got)
    sum_first = lax.ppermute(sum_first, QUAD, FIRST)
    sum_second = lax.ppermute(sum_second, QUAD, SECOND_BACK)
    bias_all = everyone(bias_sum, ("z", "xhi", "xlo"), 32)
    bias_both = jnp.sum(bias_all.reshape(16, 2, 8, HEAD_DIM), axis=0)
    grad_bias_query = bias_both[:, :GROUP].reshape(HEADS * HEAD_DIM)
    grad_bias_value = bias_both[:, GROUP].reshape(KV_HEADS * HEAD_DIM)
    grad_keys, grad_values = combine(place, sum_first, sum_second)
    return attended, grad_queries, grad_keys, grad_values, grad_bias_query, grad_bias_value


def solution(mesh):
    parts = Mesh(mesh.devices.reshape(8, 2, 2, 8, 2), ("z", "xhi", "xlo", "y", "core"))
    rows = P(("z", "xhi") + SEQ, None)
    in_specs = (rows, rows, rows, P(), P(), P(("z", "xhi"), None), rows)
    out_specs = (rows, rows, rows, rows, P(), P())
    return jax.shard_map(body, mesh=parts, in_specs=in_specs, out_specs=out_specs, check_vma=False)
```

time: 154 us -> 142 us (0.922)
  starting transfers between devices: 69.8 us -> 53.9 us
  Pallas kernels: 7.26 us -> 21.9 us
  between operations: 14.4 us -> 0.92 us
  waiting for transfers between devices: 47.5 us -> 54.8 us
  other arithmetic: 6.82 us -> 3.01 us
    all_gather x1 -> x0, waiting for transfers between devices: 30 us -> none  [body(): lax.all_gather(jnp.stack([kv_mine, kv_other, low_mine, low_other]), 'y',...]
    ppermute x10 -> x11, waiting for transfers between devices: 2.99 us -> 28.7 us  [the longest x1 9.54 us: body(): lax.ppermute(head_of(queries, grad_out, core, width), QUAD, FIRST)]
    all_to_all x2, starting transfers between devices: 35.8 us -> 16 us  [everyone(): return lax.all_to_all(spread, axes, split_axis=0, concat_axis=0, tiled=True)]
    all_to_all x0 -> x1, waiting for transfers between devices: none -> 17.3 us  [body(): got = lax.all_to_all(terms, 'y', split_axis=0, concat_axis=0, tiled=True)]
    pallas_call x1 -> x4, Pallas kernels: 6.4 us -> 21 us  [the longest x1 18.4 us: attention(): pl.pallas_call(attention_kernel, out_shape=[jax.ShapeDtypeStruct((TOK, 2...]
    all_to_all x0 -> x1, starting transfers between devices: none -> 8.96 us  [body(): got = lax.all_to_all(terms, 'y', split_axis=0, concat_axis=0, tiled=True)]
    all_to_all x2, waiting for transfers between devices: 14.5 us -> 8.86 us  [everyone(): return lax.all_to_all(spread, axes, split_axis=0, concat_axis=0, tiled=True)]
    ppermute x10 -> x11, starting transfers between devices: 33.9 us -> 28.9 us  [the longest x1 8.79 us: body(): lax.ppermute(head_of(keys, values, 1 - core, HEAD_DIM), QUAD, SECOND)]
  transfers between devices with their start and end apart: 14 -> 14, of which waited for: 6 -> 12; matrix products, arithmetic and copies ran while one was open for 4% -> 1% of each run, Pallas kernels for 1% -> 1%
where the time goes in v4:
time: 142 us; the launch traced here: 141 us
  waiting for transfers between devices  54.8 us (39%)
  starting transfers between devices  53.9 us (38%)
  Pallas kernels  21.9 us (15%)
  local copies, waits for them, and re-layouts  6.59 us (5%)
  other arithmetic  3.01 us (2%)
    pallas_call x1, Pallas kernels, attention(): pl.pallas_call(attention_kernel, out_shape=[jax.ShapeDtypeStruct((TOK, 2...  18.4 us
    all_to_all x1, waiting for transfers between devices, body(): got = lax.all_to_all(terms, 'y', split_axis=0, concat_axis=0, tiled=True)  17.3 us
    all_to_all x2, starting transfers between devices, everyone(): return lax.all_to_all(spread, axes, split_axis=0, concat_axis=0, tiled=True)  16 us
    ppermute x1, waiting for transfers between devices, body(): lax.ppermute(head_of(queries, grad_out, core, width), QUAD, FIRST)  9.54 us
    all_to_all x1, starting transfers between devices, body(): got = lax.all_to_all(terms, 'y', split_axis=0, concat_axis=0, tiled=True)  8.96 us
    all_to_all x2, waiting for transfers between devices, everyone(): return lax.all_to_all(spread, axes, split_axis=0, concat_axis=0, tiled=True)  8.86 us
    ppermute x1, starting transfers between devices, body(): lax.ppermute(head_of(keys, values, 1 - core, HEAD_DIM), QUAD, SECOND)  8.79 us
    ppermute x1, waiting for transfers between devices, body(): back_first = lax.ppermute(back_first, QUAD, FIRST)  6.24 us
  transfers between devices with their start and end apart: 14, of which 12 were waited for; matrix products, arithmetic and copies ran while one was open for 1% of the time, Pallas kernels for 1%

profile of v4, /device:TPU:1, one launch (start us, length us, event | category | flops | bytes accessed | tf_op | source)
XLA Modules:
  0.0 141.1 jit_solution(8713455921562925533)
XLA Ops:
  0.6 0.8 broadcast_select_fusion.7
  1.4 0.8 broadcast_select_fusion.6
  2.2 8.8 %collective-permute-start.1 = (bf16[128,256]{1,0:T(8,128)(2,1)S(1)}, bf16[128,256]{1,0:T(8,128)(2,1)S(1)}, u32[]{:S(2)}, u32[]{:S(2)}) collective-permute-start(bf16[128,256]{1,0:T(8,128)(2,1)S(1)} %pad_maximum_fusion.4), channel_id=1, source_target_pairs={{0,16},{1,0},{16,17},{17,1},{2,18},{3,2},{18,19},{19,3},{4,20},{5,... | collective-permute-start | bytes 196616 | tf_op jit(solution)/shard_map/ppermute | solution.py:358
  11.0 1.9 %collective-permute-start = (bf16[128,256]{1,0:T(8,128)(2,1)S(1)}, bf16[128,256]{1,0:T(8,128)(2,1)S(1)}, u32[]{:S(2)}, u32[]{:S(2)}) collective-permute-start(bf16[128,256]{1,0:T(8,128)(2,1)S(1)} %pad_maximum_fusion.3), channel_id=1, source_target_pairs={{0,0},{1,16},{16,1},{17,17},{2,2},{3,18},{18,3},{19,19},{4,4},{5,2... | collective-permute-start | bytes 196616 | tf_op jit(solution)/shard_map/ppermute | solution.py:357
  13.0 0.0 collective-permute-done.1
  13.0 3.6 %collective-permute-done = bf16[128,256]{1,0:T(8,128)(2,1)S(1)} collective-permute-done((bf16[128,256]{1,0:T(8,128)(2,1)S(1)}, bf16[128,256]{1,0:T(8,128)(2,1)S(1)}, u32[]{:S(2)}, u32[]{:S(2)}) %collective-permute-start) | collective-permute-done | bytes 65568 | tf_op jit(solution)/shard_map/ppermute | solution.py:357
  16.6 1.1 broadcast_in_dim.8
  17.7 0.0 copy-start.5
  17.7 0.0 copy-start.6
  17.7 3.7 %all-to-all-start = ((bf16[8,2,128,256]{3,2,1,0:T(8,128)(2,1)}), bf16[8,2,128,256]{3,2,1,0:T(8,128)(2,1)S(1)}, u32[]{:S(2)}, u32[]{:S(2)}) async-start(bf16[8,2,128,256]{3,2,1,0:T(8,128)(2,1)} %broadcast_in_dim.8), calls=%async_computation | async-start | bytes 2097152 | tf_op jit(solution)/shard_map/all_to_all | solution.py:335
  21.4 0.0 copy-done.5
  21.4 0.1 broadcast_select_fusion.1
  21.5 0.0 copy-done.6
  21.5 0.1 broadcast_select_fusion
  21.6 0.0 copy-start.7
  21.6 0.0 copy-start.8
  21.6 0.0 copy-start.4
  21.6 1.9 %collective-permute-start.2 = (bf16[128,1792]{1,0:T(8,128)(2,1)S(1)}, bf16[128,1792]{1,0:T(8,128)(2,1)S(1)}, u32[]{:S(2)}, u32[]{:S(2)}) collective-permute-start(bf16[128,1792]{1,0:T(8,128)(2,1)S(1)} %pad_maximum_fusion), channel_id=1, source_target_pairs={{0,0},{1,16},{16,1},{17,17},{2,2},{3,18},{18,3},{19,19},{4,4},{5,2... | collective-permute-start | bytes 1376264 | tf_op jit(solution)/shard_map/ppermute | solution.py:361
  23.6 1.9 %collective-permute-start.3 = (bf16[128,1792]{1,0:T(8,128)(2,1)S(1)}, bf16[128,1792]{1,0:T(8,128)(2,1)S(1)}, u32[]{:S(2)}, u32[]{:S(2)}) collective-permute-start(bf16[128,1792]{1,0:T(8,128)(2,1)S(1)} %pad_maximum_fusion.1), channel_id=1, source_target_pairs={{0,16},{1,0},{16,17},{17,1},{2,18},{3,2},{18,19},{19,3},{4,20},{5,... | collective-permute-start | bytes 1376264 | tf_op jit(solution)/shard_map/ppermute | solution.py:362
  25.6 0.0 copy-done.7
  25.6 0.1 pad_add_fusion.place
  25.7 9.5 %collective-permute-done.2.first = bf16[128,1792]{1,0:T(8,128)(2,1)S(1)} collective-permute-done((bf16[128,1792]{1,0:T(8,128)(2,1)S(1)}, bf16[128,1792]{1,0:T(8,128)(2,1)S(1)}, u32[]{:S(2)}, u32[]{:S(2)}) %collective-permute-start.2) | collective-permute-done | bytes 458784 | tf_op jit(solution)/shard_map/ppermute | solution.py:361
  35.2 1.5 %collective-permute-done.3.second = bf16[128,1792]{1,0:T(8,128)(2,1)S(1)} collective-permute-done((bf16[128,1792]{1,0:T(8,128)(2,1)S(1)}, bf16[128,1792]{1,0:T(8,128)(2,1)S(1)}, u32[]{:S(2)}, u32[]{:S(2)}) %collective-permute-start.3) | collective-permute-done | bytes 458784 | tf_op jit(solution)/shard_map/ppermute | solution.py:362
  36.7 0.9 shard_map.118
  37.5 0.0 copy-start
  37.5 0.8 copy-done
  38.3 0.0 copy-start.2
  38.3 0.8 copy-done.2
  39.1 8.0 %all-to-all-done.kv_half = bf16[8,2,128,256]{3,2,1,0:T(8,128)(2,1)S(1)} async-done(((bf16[8,2,128,256]{3,2,1,0:T(8,128)(2,1)}), bf16[8,2,128,256]{3,2,1,0:T(8,128)(2,1)S(1)}, u32[]{:S(2)}, u32[]{:S(2)}) %all-to-all-start) | async-done | bytes 1048608 | tf_op jit(solution)/shard_map/all_to_all | solution.py:335
  47.1 1.3 collective-permute-start.4
  48.4 0.0 copy-done.8
  48.4 3.2 %collective-permute-done.4.kv_low = bf16[8,2,128,256]{3,2,1,0:T(8,128)(2,1)S(1)} collective-permute-done((bf16[8,2,128,256]{3,2,1,0:T(8,128)(2,1)S(1)}, bf16[8,2,128,256]{3,2,1,0:T(8,128)(2,1)S(1)}, u32[]{:S(2)}, u32[]{:S(2)}) %collective-permute-start.4) | collective-permute-done | bytes 1048608 | tf_op jit(solution)/shard_map/ppermute | solution.py:365
  51.6 0.0 copy-done.4
  51.6 0.0 copy-start.1
  51.6 1.0 copy-done.1
  52.7 0.0 copy-start.3
  52.7 1.0 copy-done.3
  53.7 18.4 %shard_map.119 = (bf16[128,1792]{1,0:T(8,128)(2,1)S(1)}, bf16[128,1792]{1,0:T(8,128)(2,1)S(1)}, bf16[8,2,128,256]{3,2,1,0:T(8,128)(2,1)S(1)}, bf16[8,2,128,256]{3,2,1,0:T(8,128)(2,1)S(1)}, f32[8,128]{1,0:T(8,128)S(1)}) custom-call(s32[3]{0:T(128)S(1)} %pad_add_fusion.place, s32[1,16]{1,0:T(1,128)S(1)} %copy-done.4, ...), custom_call_target="tpu_custom_call" | custom-call | flops 9160359936 | bytes 8388608 | tf_op jit(solution)/shard_map/pallas_call | solution.py:219
  72.1 1.4 collective-permute-start.5
  73.4 1.9 %collective-permute-start.6 = (f32[8,128]{1,0:T(8,128)S(1)}, f32[8,128]{1,0:T(8,128)S(1)}, u32[]{:S(2)}, u32[]{:S(2)}) collective-permute-start(f32[8,128]{1,0:T(8,128)S(1)} %get-tuple-element.39.bias_own), channel_id=1, source_target_pairs={{0,1},{1,0},{2,3},{3,2},{4,5},{5,4},{6,7},{7,6},{8,9},{9,8},{10,11... | collective-permute-start | bytes 12296 | tf_op jit(solution)/shard_map/ppermute | solution.py:371
  75.4 1.1 collective-permute-done.6.bias_other
  76.5 0.0 collective-permute-done.5.upper
  76.5 1.3 shard_map.120
  77.8 9.0 %all-to-all-start.1 = ((bf16[8,272,256]{2,1,0:T(8,128)(2,1)}), bf16[8,272,256]{2,1,0:T(8,128)(2,1)S(1)}, u32[]{:S(2)}, u32[]{:S(2)}) async-start(bf16[8,272,256]{2,1,0:T(8,128)(2,1)} %shard_map.120), calls=%async_computation.1 | async-start | bytes 2228224 | tf_op jit(solution)/shard_map/all_to_all | solution.py:373
  86.7 1.9 %collective-permute-start.7 = (bf16[128,1792]{1,0:T(8,128)(2,1)S(1)}, bf16[128,1792]{1,0:T(8,128)(2,1)S(1)}, u32[]{:S(2)}, u32[]{:S(2)}) collective-permute-start(bf16[128,1792]{1,0:T(8,128)(2,1)S(1)} %get-tuple-element.40), channel_id=1, source_target_pairs={{0,0},{1,16},{16,1},{17,17},{2,2},{3,18},{18,3},{19,19},{4,4},{5,2... | collective-permute-start | bytes 1376264 | tf_op jit(solution)/shard_map/ppermute | solution.py:375
  88.6 1.9 %collective-permute-start.8 = (bf16[128,1792]{1,0:T(8,128)(2,1)S(1)}, bf16[128,1792]{1,0:T(8,128)(2,1)S(1)}, u32[]{:S(2)}, u32[]{:S(2)}) collective-permute-start(bf16[128,1792]{1,0:T(8,128)(2,1)S(1)} %get-tuple-element.41), channel_id=1, source_target_pairs={{16,0},{0,1},{17,16},{1,17},{18,2},{2,3},{19,18},{3,19},{20,4},{4,... | collective-permute-start | bytes 1376264 | tf_op jit(solution)/shard_map/ppermute | solution.py:376
  90.6 6.2 %collective-permute-done.7 = bf16[128,1792]{1,0:T(8,128)(2,1)S(1)} collective-permute-done((bf16[128,1792]{1,0:T(8,128)(2,1)S(1)}, bf16[128,1792]{1,0:T(8,128)(2,1)S(1)}, u32[]{:S(2)}, u32[]{:S(2)}) %collective-permute-start.7) | collective-permute-done | bytes 458784 | tf_op jit(solution)/shard_map/ppermute | solution.py:375
  96.9 2.1 %collective-permute-done.8 = bf16[128,1792]{1,0:T(8,128)(2,1)S(1)} collective-permute-done((bf16[128,1792]{1,0:T(8,128)(2,1)S(1)}, bf16[128,1792]{1,0:T(8,128)(2,1)S(1)}, u32[]{:S(2)}, u32[]{:S(2)}) %collective-permute-start.8) | collective-permute-done | bytes 458784 | tf_op jit(solution)/shard_map/ppermute | solution.py:376
  99.0 1.1 maximum_select_fusion
  100.1 17.3 %all-to-all-done.1.got = bf16[8,272,256]{2,1,0:T(8,128)(2,1)S(1)} async-done(((bf16[8,272,256]{2,1,0:T(8,128)(2,1)}), bf16[8,272,256]{2,1,0:T(8,128)(2,1)S(1)}, u32[]{:S(2)}, u32[]{:S(2)}) %all-to-all-start.1) | async-done | bytes 1114144 | tf_op jit(solution)/shard_map/all_to_all | solution.py:373
  117.4 0.1 shard_map.121
  117.6 0.7 broadcast_in_dim.21
  118.2 12.3 %all-to-all-start.2 = ((f32[32,8,128]{2,1,0:T(8,128)}), f32[32,8,128]{2,1,0:T(8,128)S(1)}, u32[]{:S(2)}, u32[]{:S(2)}) async-start(f32[32,8,128]{2,1,0:T(8,128)} %broadcast_in_dim.21), calls=%async_computation.2 | async-start | bytes 262144 | tf_op jit(solution)/shard_map/all_to_all | solution.py:335
  130.6 4.1 %collective-permute-start.9 = (bf16[128,256]{1,0:T(8,128)(2,1)S(1)}, bf16[128,256]{1,0:T(8,128)(2,1)S(1)}, u32[]{:S(2)}, u32[]{:S(2)}) collective-permute-start(bf16[128,256]{1,0:T(8,128)(2,1)S(1)} %get-tuple-element.45), channel_id=1, source_target_pairs={{0,0},{1,16},{16,1},{17,17},{2,2},{3,18},{18,3},{19,19},{4,4},{5,2... | collective-permute-start | bytes 196616 | tf_op jit(solution)/shard_map/ppermute | solution.py:382
  134.6 1.9 %collective-permute-start.10 = (bf16[128,256]{1,0:T(8,128)(2,1)S(1)}, bf16[128,256]{1,0:T(8,128)(2,1)S(1)}, u32[]{:S(2)}, u32[]{:S(2)}) collective-permute-start(bf16[128,256]{1,0:T(8,128)(2,1)S(1)} %get-tuple-element.46), channel_id=1, source_target_pairs={{16,0},{0,1},{17,16},{1,17},{18,2},{2,3},{19,18},{3,19},{20,4},{4,... | collective-permute-start | bytes 196616 | tf_op jit(solution)/shard_map/ppermute | solution.py:383
  136.6 0.6 collective-permute-done.9.mine
  137.1 0.7 collective-permute-done.10.other
  137.9 1.2 shard_map.122
  139.1 0.8 all-to-all-done.2
  139.9 0.6 slice.69
  140.5 0.6 reshape.21
  (10 shorter events, 0.2 us)
Async XLA Ops:
  2.2 10.7 %collective-permute-start.1 = (bf16[128,256]{1,0:T(8,128)(2,1)S(1)}, bf16[128,256]{1,0:T(8,128)(2,1)S(1)}, u32[]{:S(2)}, u32[]{:S(2)}) collective-permute-start(bf16[128,256]{1,0:T(8,128)(2,1)S(1)} %pad_maximum_fusion.4), channel_id=1, source_target_pairs={{0,16},{1,0},{16,17},{17,1},{2,18},{3,2},{18,19},{19,3},{4,20},{5,... | collective-permute-start | bytes 196616 | tf_op jit(solution)/shard_map/ppermute | solution.py:358
  11.0 5.6 %collective-permute-start = (bf16[128,256]{1,0:T(8,128)(2,1)S(1)}, bf16[128,256]{1,0:T(8,128)(2,1)S(1)}, u32[]{:S(2)}, u32[]{:S(2)}) collective-permute-start(bf16[128,256]{1,0:T(8,128)(2,1)S(1)} %pad_maximum_fusion.3), channel_id=1, source_target_pairs={{0,0},{1,16},{16,1},{17,17},{2,2},{3,18},{18,3},{19,19},{4,4},{5,2... | collective-permute-start | bytes 196616 | tf_op jit(solution)/shard_map/ppermute | solution.py:357
  17.7 3.7 %copy-start.5 = (bf16[128,1792]{1,0:T(8,128)(2,1)S(1)}, bf16[128,1792]{1,0:T(8,128)(2,1)}, u32[]{:S(2)}) copy-start(bf16[128,1792]{1,0:T(8,128)(2,1)} %param.7) | copy-start | bytes 1376260
  17.7 3.8 %copy-start.6 = (bf16[128,1792]{1,0:T(8,128)(2,1)S(1)}, bf16[128,1792]{1,0:T(8,128)(2,1)}, u32[]{:S(2)}) copy-start(bf16[128,1792]{1,0:T(8,128)(2,1)} %param.13) | copy-start | bytes 1376260
  17.7 29.4 %all-to-all-start = ((bf16[8,2,128,256]{3,2,1,0:T(8,128)(2,1)}), bf16[8,2,128,256]{3,2,1,0:T(8,128)(2,1)S(1)}, u32[]{:S(2)}, u32[]{:S(2)}) async-start(bf16[8,2,128,256]{3,2,1,0:T(8,128)(2,1)} %broadcast_in_dim.8), calls=%async_computation | async-start | bytes 2097152 | tf_op jit(solution)/shard_map/all_to_all | solution.py:335
  21.6 4.0 %copy-start.7 = (bf16[1792]{0:T(1024)(128)(2,1)S(1)}, bf16[1792]{0:T(1024)(128)(2,1)}, u32[]{:S(2)}) copy-start(bf16[1792]{0:T(1024)(128)(2,1)} %param.10) | copy-start | bytes 10756
  21.6 26.8 %copy-start.8 = (bf16[256]{0:T(256)(128)(2,1)S(1)}, bf16[256]{0:T(256)(128)(2,1)}, u32[]{:S(2)}) copy-start(bf16[256]{0:T(256)(128)(2,1)} %param.11) | copy-start | bytes 1540
  21.6 30.0 %copy-start.4 = (s32[1,16]{1,0:T(1,128)S(1)}, s32[1,16]{1,0:T(1,128)}, u32[]{:S(2)}) copy-start(s32[1,16]{1,0:T(1,128)} %lengths.1) | copy-start | bytes 196
  21.6 13.6 %collective-permute-start.2 = (bf16[128,1792]{1,0:T(8,128)(2,1)S(1)}, bf16[128,1792]{1,0:T(8,128)(2,1)S(1)}, u32[]{:S(2)}, u32[]{:S(2)}) collective-permute-start(bf16[128,1792]{1,0:T(8,128)(2,1)S(1)} %pad_maximum_fusion), channel_id=1, source_target_pairs={{0,0},{1,16},{16,1},{17,17},{2,2},{3,18},{18,3},{19,19},{4,4},{5,2... | collective-permute-start | bytes 1376264 | tf_op jit(solution)/shard_map/ppermute | solution.py:361
  23.6 13.0 %collective-permute-start.3 = (bf16[128,1792]{1,0:T(8,128)(2,1)S(1)}, bf16[128,1792]{1,0:T(8,128)(2,1)S(1)}, u32[]{:S(2)}, u32[]{:S(2)}) collective-permute-start(bf16[128,1792]{1,0:T(8,128)(2,1)S(1)} %pad_maximum_fusion.1), channel_id=1, source_target_pairs={{0,16},{1,0},{16,17},{17,1},{2,18},{3,2},{18,19},{19,3},{4,20},{5,... | collective-permute-start | bytes 1376264 | tf_op jit(solution)/shard_map/ppermute | solution.py:362
  37.5 0.8 copy-start
  38.3 0.8 copy-start.2
  47.1 4.5 %collective-permute-start.4 = (bf16[8,2,128,256]{3,2,1,0:T(8,128)(2,1)S(1)}, bf16[8,2,128,256]{3,2,1,0:T(8,128)(2,1)S(1)}, u32[]{:S(2)}, u32[]{:S(2)}) collective-permute-start(bf16[8,2,128,256]{3,2,1,0:T(8,128)(2,1)S(1)} %all-to-all-done.kv_half), channel_id=1, source_target_pairs={{0,1},{2,3},{4,5},{6,7},{8,9},{10,11},{12,13},{14,15},{16,17},{18,... | collective-permute-start | bytes 3145736 | tf_op jit(solution)/shard_map/ppermute | solution.py:365
  51.6 1.0 copy-start.1
  52.7 1.0 copy-start.3
  72.1 4.4 %collective-permute-start.5 = (bf16[8,2,128,256]{3,2,1,0:T(8,128)(2,1)S(1)}, bf16[8,2,128,256]{3,2,1,0:T(8,128)(2,1)S(1)}, u32[]{:S(2)}, u32[]{:S(2)}) collective-permute-start(bf16[8,2,128,256]{3,2,1,0:T(8,128)(2,1)S(1)} %get-tuple-element.38), channel_id=1, source_target_pairs={{1,0},{3,2},{5,4},{7,6},{9,8},{11,10},{13,12},{15,14},{17,16},{19,... | collective-permute-start | bytes 3145736 | tf_op jit(solution)/shard_map/ppermute | solution.py:370
  73.4 3.1 %collective-permute-start.6 = (f32[8,128]{1,0:T(8,128)S(1)}, f32[8,128]{1,0:T(8,128)S(1)}, u32[]{:S(2)}, u32[]{:S(2)}) collective-permute-start(f32[8,128]{1,0:T(8,128)S(1)} %get-tuple-element.39.bias_own), channel_id=1, source_target_pairs={{0,1},{1,0},{2,3},{3,2},{4,5},{5,4},{6,7},{7,6},{8,9},{9,8},{10,11... | collective-permute-start | bytes 12296 | tf_op jit(solution)/shard_map/ppermute | solution.py:371
  77.8 39.7 %all-to-all-start.1 = ((bf16[8,272,256]{2,1,0:T(8,128)(2,1)}), bf16[8,272,256]{2,1,0:T(8,128)(2,1)S(1)}, u32[]{:S(2)}, u32[]{:S(2)}) async-start(bf16[8,272,256]{2,1,0:T(8,128)(2,1)} %shard_map.120), calls=%async_computation.1 | async-start | bytes 2228224 | tf_op jit(solution)/shard_map/all_to_all | solution.py:373
  86.7 10.1 %collective-permute-start.7 = (bf16[128,1792]{1,0:T(8,128)(2,1)S(1)}, bf16[128,1792]{1,0:T(8,128)(2,1)S(1)}, u32[]{:S(2)}, u32[]{:S(2)}) collective-permute-start(bf16[128,1792]{1,0:T(8,128)(2,1)S(1)} %get-tuple-element.40), channel_id=1, source_target_pairs={{0,0},{1,16},{16,1},{17,17},{2,2},{3,18},{18,3},{19,19},{4,4},{5,2... | collective-permute-start | bytes 1376264 | tf_op jit(solution)/shard_map/ppermute | solution.py:375
  88.6 10.3 %collective-permute-start.8 = (bf16[128,1792]{1,0:T(8,128)(2,1)S(1)}, bf16[128,1792]{1,0:T(8,128)(2,1)S(1)}, u32[]{:S(2)}, u32[]{:S(2)}) collective-permute-start(bf16[128,1792]{1,0:T(8,128)(2,1)S(1)} %get-tuple-element.41), channel_id=1, source_target_pairs={{16,0},{0,1},{17,16},{1,17},{18,2},{2,3},{19,18},{3,19},{20,4},{4,... | collective-permute-start | bytes 1376264 | tf_op jit(solution)/shard_map/ppermute | solution.py:376
  118.2 21.7 %all-to-all-start.2 = ((f32[32,8,128]{2,1,0:T(8,128)}), f32[32,8,128]{2,1,0:T(8,128)S(1)}, u32[]{:S(2)}, u32[]{:S(2)}) async-start(f32[32,8,128]{2,1,0:T(8,128)} %broadcast_in_dim.21), calls=%async_computation.2 | async-start | bytes 262144 | tf_op jit(solution)/shard_map/all_to_all | solution.py:335
  130.6 6.6 %collective-permute-start.9 = (bf16[128,256]{1,0:T(8,128)(2,1)S(1)}, bf16[128,256]{1,0:T(8,128)(2,1)S(1)}, u32[]{:S(2)}, u32[]{:S(2)}) collective-permute-start(bf16[128,256]{1,0:T(8,128)(2,1)S(1)} %get-tuple-element.45), channel_id=1, source_target_pairs={{0,0},{1,16},{16,1},{17,17},{2,2},{3,18},{18,3},{19,19},{4,4},{5,2... | collective-permute-start | bytes 196616 | tf_op jit(solution)/shard_map/ppermute | solution.py:382
  134.6 3.2 %collective-permute-start.10 = (bf16[128,256]{1,0:T(8,128)(2,1)S(1)}, bf16[128,256]{1,0:T(8,128)(2,1)S(1)}, u32[]{:S(2)}, u32[]{:S(2)}) collective-permute-start(bf16[128,256]{1,0:T(8,128)(2,1)S(1)} %get-tuple-element.46), channel_id=1, source_target_pairs={{16,0},{0,1},{17,16},{1,17},{18,2},{2,3},{19,18},{3,19},{20,4},{4,... | collective-permute-start | bytes 196616 | tf_op jit(solution)/shard_map/ppermute | solution.py:383

commit v5 on v4

--- a/solution.py
+++ b/solution.py
@@ -248,41 +248,31 @@
     )(place, lengths, q_rows, q_cols, g_rows, g_cols, bias_v, kv_half, kv_low)
 
 
-def merge_kernel(half, upper, bias_own, bias_other, out):
-    sums = bias_own[...] + bias_other[...]
-    high = sums.astype(BF16)
-    rows = jnp.concatenate([high, (sums - high.astype(F32)).astype(BF16)], axis=1)
-    rows = jnp.concatenate([rows, jnp.zeros_like(rows)], axis=0)
+def merge_kernel(half, upper, out):
     for y in range(8):
         for part in range(2):
             total = half[y, part].astype(F32) + upper[y, part].astype(F32)
-            out[y, part * TOK : (part + 1) * TOK, :] = total.astype(BF16)
-        out[y, CHUNK:, :] = rows
-
-
-def merge(half, upper, bias_own, bias_other):
+            out[y, part] = total.astype(BF16)
+
+
+def merge(half, upper):
     vmem = pl.BlockSpec(memory_space=pltpu.VMEM)
     return pl.pallas_call(
         merge_kernel,
-        out_shape=jax.ShapeDtypeStruct((8, CHUNK + 16, 2 * HEAD_DIM), BF16),
-        in_specs=[vmem] * 4,
+        out_shape=jax.ShapeDtypeStruct(half.shape, BF16),
+        in_specs=[vmem] * 2,
         out_specs=vmem,
         compiler_params=pltpu.CompilerParams(vmem_limit_bytes=12 * 1024 * 1024),
         cost_estimate=pl.CostEstimate(flops=1 << 20, bytes_accessed=3 << 20, transcendentals=0),
-    )(half, upper, bias_own, bias_other)
-
-
-def reduce_kernel(got, first, second, bias_sum):
+    )(half, upper)
+
+
+def reduce_kernel(got, first, second):
     for part, out in enumerate((first, second)):
-        rows = pl.ds(part * TOK, TOK)
-        total = got[0, rows, :].astype(F32)
+        total = got[0, part].astype(F32)
         for y in range(1, 8):
-            total = total + got[y, rows, :].astype(F32)
+            total = total + got[y, part].astype(F32)
         out[...] = total.astype(BF16)
-    total = got[0, CHUNK:, :].astype(F32)
-    for y in range(1, 8):
-        total = total + got[y, CHUNK:, :].astype(F32)
-    bias_sum[...] = total[:8, :HEAD_DIM] + total[:8, HEAD_DIM:]
 
 
 def reduce(got):
@@ -290,15 +280,15 @@
     rows = jax.ShapeDtypeStruct((TOK, 2 * HEAD_DIM), BF16)
     return pl.pallas_call(
         reduce_kernel,
-        out_shape=[rows] * 2 + [jax.ShapeDtypeStruct((8, HEAD_DIM), F32)],
+        out_shape=[rows] * 2,
         in_specs=[vmem],
-        out_specs=[vmem] * 3,
+        out_specs=[vmem] * 2,
         compiler_params=pltpu.CompilerParams(vmem_limit_bytes=12 * 1024 * 1024),
         cost_estimate=pl.CostEstimate(flops=1 << 20, bytes_accessed=1 << 20, transcendentals=0),
     )(got)
 
 
-def combine_kernel(place, mine, other, gk, gv):
+def combine_kernel(place, mine, other, bias_sums, gk, gv, gbq, gbv):
     core = place[2]
     own_cols = pl.ds(pl.multiple_of(core * HEAD_DIM, HEAD_DIM), HEAD_DIM)
     other_cols = pl.ds(pl.multiple_of((1 - core) * HEAD_DIM, HEAD_DIM), HEAD_DIM)
@@ -306,20 +296,28 @@
     gk[:, other_cols] = other[:, :HEAD_DIM]
     gv[:, own_cols] = mine[:, HEAD_DIM:]
     gv[:, other_cols] = other[:, HEAD_DIM:]
-
-
-def combine(place, mine, other):
+    for head in range(KV_HEADS):
+        total = bias_sums[8 * head]
+        for y in range(1, 8):
+            total = total + bias_sums[8 * head + y]
+        for h in range(GROUP):
+            gbq[pl.ds((head * GROUP + h) * HEAD_DIM, HEAD_DIM)] = total[h]
+        gbv[pl.ds(head * HEAD_DIM, HEAD_DIM)] = total[GROUP]
+
+
+def combine(place, mine, other, bias_sums):
     rows = jax.ShapeDtypeStruct((TOK, KV_HEADS * HEAD_DIM), BF16)
     vmem = pl.BlockSpec(memory_space=pltpu.VMEM)
     smem = pl.BlockSpec(memory_space=pltpu.SMEM)
     return pl.pallas_call(
         combine_kernel,
-        out_shape=[rows] * 2,
-        in_specs=[smem] + [vmem] * 2,
-        out_specs=[vmem] * 2,
+        out_shape=[rows] * 2
+        + [jax.ShapeDtypeStruct((n * HEAD_DIM,), F32) for n in (HEADS, KV_HEADS)],
+        in_specs=[smem] + [vmem] * 3,
+        out_specs=[vmem] * 4,
         compiler_params=pltpu.CompilerParams(vmem_limit_bytes=8 * 1024 * 1024),
         cost_estimate=pl.CostEstimate(flops=1 << 17, bytes_accessed=1 << 19, transcendentals=0),
-    )(place, mine, other)
+    )(place, mine, other, bias_sums)
 
 
 SEQ = ("xlo", "y", "core")
@@ -360,32 +358,38 @@
     place = jnp.stack([x, core * 8 + y, core]).astype(jnp.int32)
     rows_first = lax.ppermute(head_of(queries, grad_out, core, width), QUAD, FIRST)
     rows_second = lax.ppermute(head_of(queries, grad_out, 1 - core, width), QUAD, SECOND)
+    kv_half, rows_first, rows_second = lax.optimization_barrier((kv_half, rows_first, rows_second))
+    kv_low = lax.ppermute(kv_half, "core", [(0, 1)])
     arranged = arrange(place, rows_first, rows_second, bias_query[None, :])
-    kv_half, *arranged = lax.optimization_barrier((kv_half, *arranged))
-    kv_low = lax.ppermute(kv_half, "core", [(0, 1)])
     back_first, back_second, dkv_half, dkv_low, bias_part = attention(
         place, doc_lengths, *arranged, bias_value[None, :], kv_half, kv_low
     )
 
     from_upper = lax.ppermute(dkv_low, "core", [(1, 0)])
-    bias_other = lax.ppermute(bias_part, "core", [(0, 1), (1, 0)])
-    terms = merge(dkv_half, from_upper, bias_part, bias_other)
+    bias_sum = bias_part + lax.ppermute(bias_part, "core", [(0, 1), (1, 0)])
+    dkv_half, from_upper, bias_sum = lax.optimization_barrier((dkv_half, from_upper, bias_sum))
+    terms = merge(dkv_half, from_upper)
     got = lax.all_to_all(terms, "y", split_axis=0, concat_axis=0, tiled=True)
 
     back_first = lax.ppermute(back_first, QUAD, FIRST)
     back_second = lax.ppermute(back_second, QUAD, SECOND_BACK)
     attended = joined(back_first[:, :width], back_second[:, :width])
     grad_queries = joined(back_first[:, width:], back_second[:, width:])
-    got, attended, grad_queries = lax.optimization_barrier((got, attended, grad_queries))
-
-    sum_first, sum_second, bias_sum = reduce(got)
+    for axis, size, step in (("z", 8, 1), ("z", 8, 2), ("z", 8, 4)):
+        bias_sum = bias_sum + lax.ppermute(bias_sum, axis, [(i, i ^ step) for i in range(size)])
+    got, attended, grad_queries, bias_sum = lax.optimization_barrier(
+        (got, attended, grad_queries, bias_sum)
+    )
+
+    sum_first, sum_second = reduce(got)
     sum_first = lax.ppermute(sum_first, QUAD, FIRST)
     sum_second = lax.ppermute(sum_second, QUAD, SECOND_BACK)
-    bias_all = everyone(bias_sum, ("z", "xhi", "xlo"), 32)
-    bias_both = jnp.sum(bias_all.reshape(16, 2, 8, HEAD_DIM), axis=0)
-    grad_bias_query = bias_both[:, :GROUP].reshape(HEADS * HEAD_DIM)
-    grad_bias_value = bias_both[:, GROUP].reshape(KV_HEADS * HEAD_DIM)
-    grad_keys, grad_values = combine(place, sum_first, sum_second)
+    bias_sum = bias_sum + lax.ppermute(bias_sum, "xhi", [(0, 1), (1, 0)])
+    bias_sum, sum_first, sum_second = lax.optimization_barrier((bias_sum, sum_first, sum_second))
+    bias_sums = everyone(bias_sum, ("xlo", "y"), 16)
+    grad_keys, grad_values, grad_bias_query, grad_bias_value = combine(
+        place, sum_first, sum_second, bias_sums
+    )
     return attended, grad_queries, grad_keys, grad_values, grad_bias_query, grad_bias_value
 
 

time: 142 us -> 141 us (level)
  waiting for transfers between devices: 54.8 us -> 35.8 us
  blocking collectives: 0 us -> 13.9 us
  starting transfers between devices: 53.9 us -> 64.3 us
  Pallas kernels: 21.9 us -> 18.1 us
  local copies, waits for them, and re-layouts: 6.59 us -> 3.47 us
    ppermute x1 -> x5, starting transfers between devices: 1.92 us -> 23.2 us  [the longest x3 16.6 us: body(): lax.ppermute(bias_sum, axis, [(i, i ^ step) for i in range(size)])]
    all_to_all x1, waiting for transfers between devices: 17.3 us -> 1.75 us  [body(): got = lax.all_to_all(terms, 'y', split_axis=0, concat_axis=0, tiled=True)]
    all_to_all x0 -> x1, blocking collectives: none -> 13.9 us  [everyone(): return lax.all_to_all(spread, axes, split_axis=0, concat_axis=0, tiled=True)]
    all_to_all x2 -> x1, starting transfers between devices: 16 us -> 3.69 us  [everyone(): return lax.all_to_all(spread, axes, split_axis=0, concat_axis=0, tiled=True)]
    pallas_call x1, Pallas kernels: 18.4 us -> 14.7 us  [attention(): pl.pallas_call(attention_kernel, out_shape=[jax.ShapeDtypeStruct((TOK, 2...]
    all_to_all x1, starting transfers between devices: 8.96 us -> 12.3 us  [body(): got = lax.all_to_all(terms, 'y', split_axis=0, concat_axis=0, tiled=True)]
    ppermute x1 -> x5, waiting for transfers between devices: 1.13 us -> 4.03 us  [the longest x3 1.67 us: body(): lax.ppermute(bias_sum, axis, [(i, i ^ step) for i in range(size)])]
    ppermute x1, waiting for transfers between devices: 6.24 us -> 4.08 us  [body(): back_first = lax.ppermute(back_first, QUAD, FIRST)]
  transfers between devices with their start and end apart: 14 -> 17, of which waited for: 12 -> 11; matrix products, arithmetic and copies ran while one was open for 1% -> 1% of each run, Pallas kernels for 1% -> 1%
where the time goes in v5:
time: 141 us; the launch traced here: 139 us
  starting transfers between devices  64.3 us (46%)
  waiting for transfers between devices  35.8 us (25%)
  Pallas kernels  18.1 us (13%)
  blocking collectives  13.9 us (10%)
  local copies, waits for them, and re-layouts  3.47 us (2%)
  other arithmetic  2.26 us (2%)
    ppermute x3, starting transfers between devices, body(): lax.ppermute(bias_sum, axis, [(i, i ^ step) for i in range(size)])  16.6 us
    pallas_call x1, Pallas kernels, attention(): pl.pallas_call(attention_kernel, out_shape=[jax.ShapeDtypeStruct((TOK, 2...  14.7 us
    all_to_all x1, blocking collectives, everyone(): return lax.all_to_all(spread, axes, split_axis=0, concat_axis=0, tiled=True)  13.9 us
    all_to_all x1, starting transfers between devices, body(): got = lax.all_to_all(terms, 'y', split_axis=0, concat_axis=0, tiled=True)  12.3 us
    ppermute x1, waiting for transfers between devices, body(): lax.ppermute(head_of(queries, grad_out, core, width), QUAD, FIRST)  9.65 us
    all_to_all x1, waiting for transfers between devices, everyone(): return lax.all_to_all(spread, axes, split_axis=0, concat_axis=0, tiled=True)  9.53 us
    ppermute x1, starting transfers between devices, body(): lax.ppermute(head_of(keys, values, 1 - core, HEAD_DIM), QUAD, SECOND)  8.79 us
    ppermute x1, starting transfers between devices, body(): bias_sum = bias_sum + lax.ppermute(bias_sum, 'xhi', [(0, 1), (1, 0)])  4.62 us
  transfers between devices with their start and end apart: 17, of which 11 were waited for; matrix products, arithmetic and copies ran while one was open for 1% of the time, Pallas kernels for 1%

profile of v5, /device:TPU:1, one launch (start us, length us, event | category | flops | bytes accessed | tf_op | source)
XLA Modules:
  0.0 138.8 jit_solution(11307477643472650557)
XLA Ops:
  0.6 0.0 copy-start.3
  0.7 0.8 broadcast_select_fusion.7
  1.5 0.0 copy-done.3
  1.5 8.8 %collective-permute-start.1 = (bf16[128,256]{1,0:T(8,128)(2,1)S(1)}, bf16[128,256]{1,0:T(8,128)(2,1)S(1)}, u32[]{:S(2)}, u32[]{:S(2)}) collective-permute-start(bf16[128,256]{1,0:T(8,128)(2,1)S(1)} %pad_maximum_fusion.4), channel_id=1, source_target_pairs={{0,16},{1,0},{16,17},{17,1},{2,18},{3,2},{18,19},{19,3},{4,20},{5,... | collective-permute-start | bytes 196616 | tf_op jit(solution)/shard_map/ppermute | solution.py:356
  10.3 1.9 %collective-permute-start = (bf16[128,256]{1,0:T(8,128)(2,1)S(1)}, bf16[128,256]{1,0:T(8,128)(2,1)S(1)}, u32[]{:S(2)}, u32[]{:S(2)}) collective-permute-start(bf16[128,256]{1,0:T(8,128)(2,1)S(1)} %pad_maximum_fusion.3), channel_id=1, source_target_pairs={{0,0},{1,16},{16,1},{17,17},{2,2},{3,18},{18,3},{19,19},{4,4},{5,2... | collective-permute-start | bytes 196616 | tf_op jit(solution)/shard_map/ppermute | solution.py:355
  12.3 0.0 collective-permute-done.1
  12.3 3.6 %collective-permute-done = bf16[128,256]{1,0:T(8,128)(2,1)S(1)} collective-permute-done((bf16[128,256]{1,0:T(8,128)(2,1)S(1)}, bf16[128,256]{1,0:T(8,128)(2,1)S(1)}, u32[]{:S(2)}, u32[]{:S(2)}) %collective-permute-start) | collective-permute-done | bytes 65568 | tf_op jit(solution)/shard_map/ppermute | solution.py:355
  15.9 1.1 broadcast_in_dim.8
  17.0 0.0 copy-start.1
  17.0 3.7 %all-to-all-start = ((bf16[8,2,128,256]{3,2,1,0:T(8,128)(2,1)}), bf16[8,2,128,256]{3,2,1,0:T(8,128)(2,1)S(1)}, u32[]{:S(2)}, u32[]{:S(2)}) async-start(bf16[8,2,128,256]{3,2,1,0:T(8,128)(2,1)} %broadcast_in_dim.8), calls=%async_computation | async-start | bytes 2097152 | tf_op jit(solution)/shard_map/all_to_all | solution.py:333
  20.7 0.0 copy-done.1
  20.7 0.0 copy-start.2
  20.7 0.1 broadcast_select_fusion.1
  20.8 0.9 copy-done.2
  21.7 0.1 broadcast_select_fusion
  21.8 1.9 %collective-permute-start.2 = (bf16[128,1792]{1,0:T(8,128)(2,1)S(1)}, bf16[128,1792]{1,0:T(8,128)(2,1)S(1)}, u32[]{:S(2)}, u32[]{:S(2)}) collective-permute-start(bf16[128,1792]{1,0:T(8,128)(2,1)S(1)} %pad_maximum_fusion), channel_id=1, source_target_pairs={{0,0},{1,16},{16,1},{17,17},{2,2},{3,18},{18,3},{19,19},{4,4},{5,2... | collective-permute-start | bytes 1376264 | tf_op jit(solution)/shard_map/ppermute | solution.py:359
  23.8 1.9 %collective-permute-start.3 = (bf16[128,1792]{1,0:T(8,128)(2,1)S(1)}, bf16[128,1792]{1,0:T(8,128)(2,1)S(1)}, u32[]{:S(2)}, u32[]{:S(2)}) collective-permute-start(bf16[128,1792]{1,0:T(8,128)(2,1)S(1)} %pad_maximum_fusion.1), channel_id=1, source_target_pairs={{0,16},{1,0},{16,17},{17,1},{2,18},{3,2},{18,19},{19,3},{4,20},{5,... | collective-permute-start | bytes 1376264 | tf_op jit(solution)/shard_map/ppermute | solution.py:360
  25.7 9.7 %collective-permute-done.2.first = bf16[128,1792]{1,0:T(8,128)(2,1)S(1)} collective-permute-done((bf16[128,1792]{1,0:T(8,128)(2,1)S(1)}, bf16[128,1792]{1,0:T(8,128)(2,1)S(1)}, u32[]{:S(2)}, u32[]{:S(2)}) %collective-permute-start.2) | collective-permute-done | bytes 458784 | tf_op jit(solution)/shard_map/ppermute | solution.py:359
  35.4 1.5 %collective-permute-done.3.second = bf16[128,1792]{1,0:T(8,128)(2,1)S(1)} collective-permute-done((bf16[128,1792]{1,0:T(8,128)(2,1)S(1)}, bf16[128,1792]{1,0:T(8,128)(2,1)S(1)}, u32[]{:S(2)}, u32[]{:S(2)}) %collective-permute-start.3) | collective-permute-done | bytes 458784 | tf_op jit(solution)/shard_map/ppermute | solution.py:360
  36.8 9.5 %all-to-all-done.kv_half = bf16[8,2,128,256]{3,2,1,0:T(8,128)(2,1)S(1)} async-done(((bf16[8,2,128,256]{3,2,1,0:T(8,128)(2,1)}), bf16[8,2,128,256]{3,2,1,0:T(8,128)(2,1)S(1)}, u32[]{:S(2)}, u32[]{:S(2)}) %all-to-all-start) | async-done | bytes 1048608 | tf_op jit(solution)/shard_map/all_to_all | solution.py:333
  46.4 1.3 collective-permute-start.4
  47.7 0.0 copy-start.4
  47.7 0.0 copy-start.5
  47.7 0.6 copy-done.5
  48.4 0.0 copy-done.4
  48.4 0.1 pad_add_fusion.place
  48.4 0.9 shard_map.118
  49.3 1.6 %collective-permute-done.4.kv_low = bf16[8,2,128,256]{3,2,1,0:T(8,128)(2,1)S(1)} collective-permute-done((bf16[8,2,128,256]{3,2,1,0:T(8,128)(2,1)S(1)}, bf16[8,2,128,256]{3,2,1,0:T(8,128)(2,1)S(1)}, u32[]{:S(2)}, u32[]{:S(2)}) %collective-permute-start.4) | collective-permute-done | bytes 1048608 | tf_op jit(solution)/shard_map/ppermute | solution.py:362
  50.9 0.0 copy-start
  50.9 0.7 copy-done
  51.6 14.7 %shard_map.119 = (bf16[128,1792]{1,0:T(8,128)(2,1)S(1)}, bf16[128,1792]{1,0:T(8,128)(2,1)S(1)}, bf16[8,2,128,256]{3,2,1,0:T(8,128)(2,1)S(1)}, bf16[8,2,128,256]{3,2,1,0:T(8,128)(2,1)S(1)}, f32[8,128]{1,0:T(8,128)S(1)}) custom-call(s32[3]{0:T(128)S(1)} %pad_add_fusion.place, s32[1,16]{1,0:T(1,128)S(1)} %copy-done, ...), custom_call_target="tpu_custom_call" | custom-call | flops 9160359936 | bytes 8388608 | tf_op jit(solution)/shard_map/pallas_call | solution.py:219
  66.2 1.4 collective-permute-start.5
  67.6 1.9 %collective-permute-start.6 = (f32[8,128]{1,0:T(8,128)S(1)}, f32[8,128]{1,0:T(8,128)S(1)}, u32[]{:S(2)}, u32[]{:S(2)}) collective-permute-start(f32[8,128]{1,0:T(8,128)S(1)} %get-tuple-element.43), channel_id=1, source_target_pairs={{0,1},{1,0},{2,3},{3,2},{4,5},{5,4},{6,7},{7,6},{8,9},{9,8},{10,11... | collective-permute-start | bytes 12296 | tf_op jit(solution)/shard_map/ppermute | solution.py:369
  69.5 1.1 collective-permute-done.6
  70.7 0.0 collective-permute-done.5.upper
  70.7 1.3 shard_map.120
  71.9 12.3 %all-to-all-start.1 = ((bf16[8,2,128,256]{3,2,1,0:T(8,128)(2,1)}), bf16[8,2,128,256]{3,2,1,0:T(8,128)(2,1)S(1)}, u32[]{:S(2)}, u32[]{:S(2)}) async-start(bf16[8,2,128,256]{3,2,1,0:T(8,128)(2,1)} %shard_map.120), calls=%async_computation.1 | async-start | bytes 2097152 | tf_op jit(solution)/shard_map/all_to_all | solution.py:372
  84.2 1.9 %collective-permute-start.7 = (bf16[128,1792]{1,0:T(8,128)(2,1)S(1)}, bf16[128,1792]{1,0:T(8,128)(2,1)S(1)}, u32[]{:S(2)}, u32[]{:S(2)}) collective-permute-start(bf16[128,1792]{1,0:T(8,128)(2,1)S(1)} %get-tuple-element.46), channel_id=1, source_target_pairs={{0,0},{1,16},{16,1},{17,17},{2,2},{3,18},{18,3},{19,19},{4,4},{5,2... | collective-permute-start | bytes 1376264 | tf_op jit(solution)/shard_map/ppermute | solution.py:374
  86.1 1.9 %collective-permute-start.8 = (bf16[128,1792]{1,0:T(8,128)(2,1)S(1)}, bf16[128,1792]{1,0:T(8,128)(2,1)S(1)}, u32[]{:S(2)}, u32[]{:S(2)}) collective-permute-start(bf16[128,1792]{1,0:T(8,128)(2,1)S(1)} %get-tuple-element.47), channel_id=1, source_target_pairs={{16,0},{0,1},{17,16},{1,17},{18,2},{2,3},{19,18},{3,19},{20,4},{4,... | collective-permute-start | bytes 1376264 | tf_op jit(solution)/shard_map/ppermute | solution.py:375
  88.0 2.1 %collective-permute-start.9 = (f32[8,128]{1,0:T(8,128)S(1)}, f32[8,128]{1,0:T(8,128)S(1)}, u32[]{:S(2)}, u32[]{:S(2)}) collective-permute-start(f32[8,128]{1,0:T(8,128)S(1)} %add.19), channel_id=1, source_target_pairs={{0,64},{64,0},{128,192},{192,128},{256,320},{320,256},{384,448},{4... | collective-permute-start | bytes 12296 | tf_op jit(solution)/shard_map/ppermute | solution.py:379
  90.2 4.1 %collective-permute-done.7 = bf16[128,1792]{1,0:T(8,128)(2,1)S(1)} collective-permute-done((bf16[128,1792]{1,0:T(8,128)(2,1)S(1)}, bf16[128,1792]{1,0:T(8,128)(2,1)S(1)}, u32[]{:S(2)}, u32[]{:S(2)}) %collective-permute-start.7) | collective-permute-done | bytes 458784 | tf_op jit(solution)/shard_map/ppermute | solution.py:374
  94.3 0.0 collective-permute-done.9
  94.3 4.0 %collective-permute-start.10 = (f32[8,128]{1,0:T(8,128)S(1)}, f32[8,128]{1,0:T(8,128)S(1)}, u32[]{:S(2)}, u32[]{:S(2)}) collective-permute-start(f32[8,128]{1,0:T(8,128)S(1)} %add.20), channel_id=1, source_target_pairs={{0,128},{64,192},{128,0},{192,64},{256,384},{320,448},{384,256},{4... | collective-permute-start | bytes 12296 | tf_op jit(solution)/shard_map/ppermute | solution.py:379
  98.3 0.0 collective-permute-done.8
  98.3 1.5 %collective-permute-done.10 = f32[8,128]{1,0:T(8,128)S(1)} collective-permute-done((f32[8,128]{1,0:T(8,128)S(1)}, f32[8,128]{1,0:T(8,128)S(1)}, u32[]{:S(2)}, u32[]{:S(2)}) %collective-permute-start.10) | collective-permute-done | bytes 4128 | tf_op jit(solution)/shard_map/ppermute | solution.py:379
  99.9 10.5 %collective-permute-start.11 = (f32[8,128]{1,0:T(8,128)S(1)}, f32[8,128]{1,0:T(8,128)S(1)}, u32[]{:S(2)}, u32[]{:S(2)}) collective-permute-start(f32[8,128]{1,0:T(8,128)S(1)} %add.21), channel_id=1, source_target_pairs={{0,256},{64,320},{128,384},{192,448},{256,0},{320,64},{384,128},{4... | collective-permute-start | bytes 12296 | tf_op jit(solution)/shard_map/ppermute | solution.py:379
  110.4 1.1 maximum_select_fusion
  111.5 0.1 collective-permute-done.11
  111.7 1.7 %all-to-all-done.1.got = bf16[8,2,128,256]{3,2,1,0:T(8,128)(2,1)S(1)} async-done(((bf16[8,2,128,256]{3,2,1,0:T(8,128)(2,1)}), bf16[8,2,128,256]{3,2,1,0:T(8,128)(2,1)S(1)}, u32[]{:S(2)}, u32[]{:S(2)}) %all-to-all-start.1) | async-done | bytes 1048608 | tf_op jit(solution)/shard_map/all_to_all | solution.py:372
  113.4 0.1 shard_map.121
  113.6 2.2 %collective-permute-start.13 = (bf16[128,256]{1,0:T(8,128)(2,1)S(1)}, bf16[128,256]{1,0:T(8,128)(2,1)S(1)}, u32[]{:S(2)}, u32[]{:S(2)}) collective-permute-start(bf16[128,256]{1,0:T(8,128)(2,1)S(1)} %get-tuple-element.53), channel_id=1, source_target_pairs={{0,0},{1,16},{16,1},{17,17},{2,2},{3,18},{18,3},{19,19},{4,4},{5,2... | collective-permute-start | bytes 196616 | tf_op jit(solution)/shard_map/ppermute | solution.py:385
  115.8 1.9 %collective-permute-start.14 = (bf16[128,256]{1,0:T(8,128)(2,1)S(1)}, bf16[128,256]{1,0:T(8,128)(2,1)S(1)}, u32[]{:S(2)}, u32[]{:S(2)}) collective-permute-start(bf16[128,256]{1,0:T(8,128)(2,1)S(1)} %get-tuple-element.54), channel_id=1, source_target_pairs={{16,0},{0,1},{17,16},{1,17},{18,2},{2,3},{19,18},{3,19},{20,4},{4,... | collective-permute-start | bytes 196616 | tf_op jit(solution)/shard_map/ppermute | solution.py:386
  117.7 4.6 %collective-permute-start.12 = (f32[8,128]{1,0:T(8,128)S(1)}, f32[8,128]{1,0:T(8,128)S(1)}, u32[]{:S(2)}, u32[]{:S(2)}) collective-permute-start(f32[8,128]{1,0:T(8,128)S(1)} %add.22), channel_id=1, source_target_pairs={{0,32},{32,0},{1,33},{33,1},{2,34},{34,2},{3,35},{35,3},{4,36},{36... | collective-permute-start | bytes 12296 | tf_op jit(solution)/shard_map/ppermute | solution.py:387
  122.4 1.2 collective-permute-done.12
  123.6 0.0 collective-permute-done.13.mine
  123.6 0.0 collective-permute-done.14.other
  123.6 13.9 %all_to_all.15.bias_sums = f32[16,8,128]{2,1,0:T(8,128)S(1)} all-to-all(f32[16,8,128]{2,1,0:T(8,128)S(1)} %broadcast_in_dim.21), channel_id=1, replica_groups=mesh['z'=8,'xhi'=2,'xlo'=2,'y'=8,'core'=2] {'xlo','y'}, dimensions={0} | all-to-all | bytes 131072 | tf_op jit(solution)/shard_map/all_to_all | solution.py:333
  137.6 1.2 shard_map.122
  (16 shorter events, 0.2 us)
Async XLA Ops:
  0.6 0.8 copy-start.3
  1.5 10.7 %collective-permute-start.1 = (bf16[128,256]{1,0:T(8,128)(2,1)S(1)}, bf16[128,256]{1,0:T(8,128)(2,1)S(1)}, u32[]{:S(2)}, u32[]{:S(2)}) collective-permute-start(bf16[128,256]{1,0:T(8,128)(2,1)S(1)} %pad_maximum_fusion.4), channel_id=1, source_target_pairs={{0,16},{1,0},{16,17},{17,1},{2,18},{3,2},{18,19},{19,3},{4,20},{5,... | collective-permute-start | bytes 196616 | tf_op jit(solution)/shard_map/ppermute | solution.py:356
  10.3 5.6 %collective-permute-start = (bf16[128,256]{1,0:T(8,128)(2,1)S(1)}, bf16[128,256]{1,0:T(8,128)(2,1)S(1)}, u32[]{:S(2)}, u32[]{:S(2)}) collective-permute-start(bf16[128,256]{1,0:T(8,128)(2,1)S(1)} %pad_maximum_fusion.3), channel_id=1, source_target_pairs={{0,0},{1,16},{16,1},{17,17},{2,2},{3,18},{18,3},{19,19},{4,4},{5,2... | collective-permute-start | bytes 196616 | tf_op jit(solution)/shard_map/ppermute | solution.py:355
  17.0 3.7 %copy-start.1 = (bf16[128,1792]{1,0:T(8,128)(2,1)S(1)}, bf16[128,1792]{1,0:T(8,128)(2,1)}, u32[]{:S(2)}) copy-start(bf16[128,1792]{1,0:T(8,128)(2,1)} %param.7) | copy-start | bytes 1376260
  17.0 29.4 %all-to-all-start = ((bf16[8,2,128,256]{3,2,1,0:T(8,128)(2,1)}), bf16[8,2,128,256]{3,2,1,0:T(8,128)(2,1)S(1)}, u32[]{:S(2)}, u32[]{:S(2)}) async-start(bf16[8,2,128,256]{3,2,1,0:T(8,128)(2,1)} %broadcast_in_dim.8), calls=%async_computation | async-start | bytes 2097152 | tf_op jit(solution)/shard_map/all_to_all | solution.py:333
  20.7 1.0 copy-start.2
  21.8 13.6 %collective-permute-start.2 = (bf16[128,1792]{1,0:T(8,128)(2,1)S(1)}, bf16[128,1792]{1,0:T(8,128)(2,1)S(1)}, u32[]{:S(2)}, u32[]{:S(2)}) collective-permute-start(bf16[128,1792]{1,0:T(8,128)(2,1)S(1)} %pad_maximum_fusion), channel_id=1, source_target_pairs={{0,0},{1,16},{16,1},{17,17},{2,2},{3,18},{18,3},{19,19},{4,4},{5,2... | collective-permute-start | bytes 1376264 | tf_op jit(solution)/shard_map/ppermute | solution.py:359
  23.8 13.0 %collective-permute-start.3 = (bf16[128,1792]{1,0:T(8,128)(2,1)S(1)}, bf16[128,1792]{1,0:T(8,128)(2,1)S(1)}, u32[]{:S(2)}, u32[]{:S(2)}) collective-permute-start(bf16[128,1792]{1,0:T(8,128)(2,1)S(1)} %pad_maximum_fusion.1), channel_id=1, source_target_pairs={{0,16},{1,0},{16,17},{17,1},{2,18},{3,2},{18,19},{19,3},{4,20},{5,... | collective-permute-start | bytes 1376264 | tf_op jit(solution)/shard_map/ppermute | solution.py:360
  46.4 4.5 %collective-permute-start.4 = (bf16[8,2,128,256]{3,2,1,0:T(8,128)(2,1)S(1)}, bf16[8,2,128,256]{3,2,1,0:T(8,128)(2,1)S(1)}, u32[]{:S(2)}, u32[]{:S(2)}) collective-permute-start(bf16[8,2,128,256]{3,2,1,0:T(8,128)(2,1)S(1)} %all-to-all-done.kv_half), channel_id=1, source_target_pairs={{0,1},{2,3},{4,5},{6,7},{8,9},{10,11},{12,13},{14,15},{16,17},{18,... | collective-permute-start | bytes 3145736 | tf_op jit(solution)/shard_map/ppermute | solution.py:362
  47.7 0.7 copy-start.4
  47.7 0.7 copy-start.5
  50.9 0.7 copy-start
  66.2 4.4 %collective-permute-start.5 = (bf16[8,2,128,256]{3,2,1,0:T(8,128)(2,1)S(1)}, bf16[8,2,128,256]{3,2,1,0:T(8,128)(2,1)S(1)}, u32[]{:S(2)}, u32[]{:S(2)}) collective-permute-start(bf16[8,2,128,256]{3,2,1,0:T(8,128)(2,1)S(1)} %get-tuple-element.42), channel_id=1, source_target_pairs={{1,0},{3,2},{5,4},{7,6},{9,8},{11,10},{13,12},{15,14},{17,16},{19,... | collective-permute-start | bytes 3145736 | tf_op jit(solution)/shard_map/ppermute | solution.py:368
  67.6 3.1 %collective-permute-start.6 = (f32[8,128]{1,0:T(8,128)S(1)}, f32[8,128]{1,0:T(8,128)S(1)}, u32[]{:S(2)}, u32[]{:S(2)}) collective-permute-start(f32[8,128]{1,0:T(8,128)S(1)} %get-tuple-element.43), channel_id=1, source_target_pairs={{0,1},{1,0},{2,3},{3,2},{4,5},{5,4},{6,7},{7,6},{8,9},{9,8},{10,11... | collective-permute-start | bytes 12296 | tf_op jit(solution)/shard_map/ppermute | solution.py:369
  71.9 41.5 %all-to-all-start.1 = ((bf16[8,2,128,256]{3,2,1,0:T(8,128)(2,1)}), bf16[8,2,128,256]{3,2,1,0:T(8,128)(2,1)S(1)}, u32[]{:S(2)}, u32[]{:S(2)}) async-start(bf16[8,2,128,256]{3,2,1,0:T(8,128)(2,1)} %shard_map.120), calls=%async_computation.1 | async-start | bytes 2097152 | tf_op jit(solution)/shard_map/all_to_all | solution.py:372
  84.2 10.1 %collective-permute-start.7 = (bf16[128,1792]{1,0:T(8,128)(2,1)S(1)}, bf16[128,1792]{1,0:T(8,128)(2,1)S(1)}, u32[]{:S(2)}, u32[]{:S(2)}) collective-permute-start(bf16[128,1792]{1,0:T(8,128)(2,1)S(1)} %get-tuple-element.46), channel_id=1, source_target_pairs={{0,0},{1,16},{16,1},{17,17},{2,2},{3,18},{18,3},{19,19},{4,4},{5,2... | collective-permute-start | bytes 1376264 | tf_op jit(solution)/shard_map/ppermute | solution.py:374
  86.1 12.2 %collective-permute-start.8 = (bf16[128,1792]{1,0:T(8,128)(2,1)S(1)}, bf16[128,1792]{1,0:T(8,128)(2,1)S(1)}, u32[]{:S(2)}, u32[]{:S(2)}) collective-permute-start(bf16[128,1792]{1,0:T(8,128)(2,1)S(1)} %get-tuple-element.47), channel_id=1, source_target_pairs={{16,0},{0,1},{17,16},{1,17},{18,2},{2,3},{19,18},{3,19},{20,4},{4,... | collective-permute-start | bytes 1376264 | tf_op jit(solution)/shard_map/ppermute | solution.py:375
  88.0 6.3 %collective-permute-start.9 = (f32[8,128]{1,0:T(8,128)S(1)}, f32[8,128]{1,0:T(8,128)S(1)}, u32[]{:S(2)}, u32[]{:S(2)}) collective-permute-start(f32[8,128]{1,0:T(8,128)S(1)} %add.19), channel_id=1, source_target_pairs={{0,64},{64,0},{128,192},{192,128},{256,320},{320,256},{384,448},{4... | collective-permute-start | bytes 12296 | tf_op jit(solution)/shard_map/ppermute | solution.py:379
  94.3 5.5 %collective-permute-start.10 = (f32[8,128]{1,0:T(8,128)S(1)}, f32[8,128]{1,0:T(8,128)S(1)}, u32[]{:S(2)}, u32[]{:S(2)}) collective-permute-start(f32[8,128]{1,0:T(8,128)S(1)} %add.20), channel_id=1, source_target_pairs={{0,128},{64,192},{128,0},{192,64},{256,384},{320,448},{384,256},{4... | collective-permute-start | bytes 12296 | tf_op jit(solution)/shard_map/ppermute | solution.py:379
  99.9 11.8 %collective-permute-start.11 = (f32[8,128]{1,0:T(8,128)S(1)}, f32[8,128]{1,0:T(8,128)S(1)}, u32[]{:S(2)}, u32[]{:S(2)}) collective-permute-start(f32[8,128]{1,0:T(8,128)S(1)} %add.21), channel_id=1, source_target_pairs={{0,256},{64,320},{128,384},{192,448},{256,0},{320,64},{384,128},{4... | collective-permute-start | bytes 12296 | tf_op jit(solution)/shard_map/ppermute | solution.py:379
  113.6 10.0 %collective-permute-start.13 = (bf16[128,256]{1,0:T(8,128)(2,1)S(1)}, bf16[128,256]{1,0:T(8,128)(2,1)S(1)}, u32[]{:S(2)}, u32[]{:S(2)}) collective-permute-start(bf16[128,256]{1,0:T(8,128)(2,1)S(1)} %get-tuple-element.53), channel_id=1, source_target_pairs={{0,0},{1,16},{16,1},{17,17},{2,2},{3,18},{18,3},{19,19},{4,4},{5,2... | collective-permute-start | bytes 196616 | tf_op jit(solution)/shard_map/ppermute | solution.py:385
  115.8 7.8 %collective-permute-start.14 = (bf16[128,256]{1,0:T(8,128)(2,1)S(1)}, bf16[128,256]{1,0:T(8,128)(2,1)S(1)}, u32[]{:S(2)}, u32[]{:S(2)}) collective-permute-start(bf16[128,256]{1,0:T(8,128)(2,1)S(1)} %get-tuple-element.54), channel_id=1, source_target_pairs={{16,0},{0,1},{17,16},{1,17},{18,2},{2,3},{19,18},{3,19},{20,4},{4,... | collective-permute-start | bytes 196616 | tf_op jit(solution)/shard_map/ppermute | solution.py:386
  117.7 5.9 %collective-permute-start.12 = (f32[8,128]{1,0:T(8,128)S(1)}, f32[8,128]{1,0:T(8,128)S(1)}, u32[]{:S(2)}, u32[]{:S(2)}) collective-permute-start(f32[8,128]{1,0:T(8,128)S(1)} %add.22), channel_id=1, source_target_pairs={{0,32},{32,0},{1,33},{33,1},{2,34},{34,2},{3,35},{35,3},{4,36},{36... | collective-permute-start | bytes 12296 | tf_op jit(solution)/shard_map/ppermute | solution.py:387
